TPU v7x, 32 devices: a whole 2x2x4 slice. The times are simulated.
32 devices in a mesh: section: 2 (over x), seq: 4 (over y, core), shard: 4 (over z).
Axes of the slice: x: 2, y: 2, z: 4, core: 2. Of those that a mesh axis runs over, the one named last changes fastest.
Arguments:
- inputs: bfloat16 [2, 4, 512, 1024], P(None, 'shard', 'seq'), may hold values from -6 to 6
- segment_ids: int32 [2, 4, 512], P(None, 'shard'), may hold values from 0 to 3, never falling along the last dimension, each value on 1 to 256 neighbouring positions
- cotangent: bfloat16 [2, 4, 512, 1024], P(None, 'shard', 'seq'), may hold values from -6 to 6
- w_mix: bfloat16 [2, 1024, 4096], P('section', 'shard'), may hold values from -0.1875 to 0.1875
- w_out: bfloat16 [2, 1024, 1024], P('section', 'shard'), may hold values from -0.375 to 0.375
- w_gu: bfloat16 [2, 1024, 5632], P('section', 'shard'), may hold values from -0.1875 to 0.1875
- w_down: bfloat16 [2, 2816, 1024], P('section', 'shard'), may hold values from -0.109375 to 0.109375
- norm_gains: bfloat16 [2, 1024, 2], P('section', 'shard'), may hold values from 0.25 to 1.75
- persist_kv: bfloat16 [2, 2, 16, 1024], P('section', None, None, 'seq'), may hold values from -6 to 6
- memory_decay: float32 [2, 8], P('section', 'seq'), may hold values from 0.00048828125 to 0.05
Outputs:
- section_outputs: bfloat16 [2, 2, 4, 512, 1024], P('section', None, 'shard', 'seq')
- section_grads: float32 [2, 2, 4, 512, 1024], P('section', None, 'shard', 'seq')
- grad_w_mix: float32 [2, 1024, 4096], P('section', 'shard')
- grad_w_out: float32 [2, 1024, 1024], P('section', 'shard')
- grad_w_gu: float32 [2, 1024, 5632], P('section', 'shard')
- grad_w_down: float32 [2, 2816, 1024], P('section', 'shard')
- grad_gains: float32 [2, 1024, 2], P('section', 'shard')
- grad_persist: float32 [2, 2, 16, 1024], P('section', None, None, 'seq')
- grad_decay: float32 [2, 8], P('section', 'seq')
Inputs may be any that keep to these rules, and one draw needn't show every extreme that they name: `segment_ids`: within one sequence the ids never fall; equal ids mark one document.
All inputs are finite; a program needn't handle non-finite values.
Results may differ from a plain program's by a relative error of at most 0.033.
Values may be sent and summed in bfloat16 or wider, within the bound.
A program may use at most 256 MiB of HBM per device.

v0:
```python
import math

import jax
import jax.numpy as jnp
from jax import lax
from jax.sharding import PartitionSpec as P

D = 1024
H = 8
HD = 128
FF = 2816


def shifted(value, axis, by):
    size = lax.axis_size(axis)
    pairs = [(i, i + by) for i in range(size) if 0 <= i + by < size]
    return lax.ppermute(value, axis, pairs)


def as_sent(value):
    return jax.tree.map(lambda a: a.astype(jnp.bfloat16) if a.dtype == jnp.float32 else a, value)


def rms_scale(values):
    return lax.rsqrt(jnp.mean(values * values, axis=-1, keepdims=True) + 1e-06)


def norm_back(grad_normed, scaled, inverse, gain):
    grad_scaled = grad_normed * gain
    grad_rows = inverse * (
        grad_scaled - scaled * jnp.mean(grad_scaled * scaled, axis=-1, keepdims=True)
    )
    return (grad_rows, jnp.sum(grad_normed * scaled, axis=0))


def block_terms(query_rows, key_rows, seg_ids, begin, reach, rate):
    inner = jnp.dot(query_rows, key_rows.T, preferred_element_type=jnp.float32)
    row_places = begin + jnp.arange(reach - begin, dtype=jnp.int32)
    col_places = jnp.arange(reach, dtype=jnp.int32)
    allowed = (seg_ids[begin:reach][:, None] == seg_ids[:reach][None, :]) & (
        col_places[None, :] <= row_places[:, None]
    )
    distance = jnp.maximum(row_places[:, None] - col_places[None, :], 0).astype(jnp.float32)
    decay_w = jnp.where(allowed, jnp.exp(-rate * distance), jnp.float32(0.0))
    return (inner, allowed, decay_w, distance)


def head_forward(query, keys, values, pkeys, pvalues, rate, seg_ids):
    length, width = query.shape
    block = min(512, length)
    scale = 1.0 / math.sqrt(width)
    attn_parts, memory_parts, lse_parts = ([], [], [])
    for begin in range(0, length, block):
        reach = begin + block
        query_rows = query[begin:reach]
        inner, allowed, decay_w, distance = block_terms(
            query_rows, keys[:reach], seg_ids, begin, reach, rate
        )
        per_scores = jnp.dot(query_rows, pkeys.T, preferred_element_type=jnp.float32) * scale
        seq_scores = jnp.where(allowed, inner * scale, -jnp.inf)
        top = jnp.maximum(
            jnp.max(per_scores, axis=1, keepdims=True), jnp.max(seq_scores, axis=1, keepdims=True)
        )
        per_exp = jnp.exp(per_scores - top)
        seq_exp = jnp.exp(seq_scores - top)
        denom = jnp.sum(per_exp, axis=1, keepdims=True) + jnp.sum(seq_exp, axis=1, keepdims=True)
        attended = jnp.dot(
            (per_exp / denom).astype(jnp.bfloat16), pvalues, preferred_element_type=jnp.float32
        )
        attended = attended + jnp.dot(
            (seq_exp / denom).astype(jnp.bfloat16),
            values[:reach],
            preferred_element_type=jnp.float32,
        )
        memory_w = (inner * decay_w * (1.0 / width)).astype(jnp.bfloat16)
        recalled = jnp.dot(memory_w, values[:reach], preferred_element_type=jnp.float32)
        attn_parts.append(attended)
        memory_parts.append(recalled)
        lse_parts.append(top[:, 0] + jnp.log(denom[:, 0]))
    return (
        jnp.concatenate(attn_parts, 0),
        jnp.concatenate(memory_parts, 0),
        jnp.concatenate(lse_parts, 0),
    )


def head_backward(query, keys, values, pkeys, pvalues, rate, seg_ids, lse, grad_attn, grad_memory):
    length, width = query.shape
    block = min(512, length)
    scale = 1.0 / math.sqrt(width)
    query_grads = []
    grad_keys = jnp.zeros((length, width), jnp.float32)
    grad_values = jnp.zeros((length, width), jnp.float32)
    grad_pkeys = jnp.zeros(pkeys.shape, jnp.float32)
    grad_pvalues = jnp.zeros(pvalues.shape, jnp.float32)
    grad_rate = jnp.float32(0.0)
    for begin in range(0, length, block):
        reach = begin + block
        query_rows = query[begin:reach]
        key_rows = keys[:reach]
        value_rows = values[:reach]
        inner, allowed, decay_w, distance = block_terms(
            query_rows, key_rows, seg_ids, begin, reach, rate
        )
        per_scores = jnp.dot(query_rows, pkeys.T, preferred_element_type=jnp.float32) * scale
        seq_scores = jnp.where(allowed, inner * scale, -jnp.inf)
        row_lse = lse[begin:reach][:, None]
        per_prob = jnp.exp(per_scores - row_lse)
        seq_prob = jnp.exp(seq_scores - row_lse)
        attn_rows = grad_attn[begin:reach]
        memory_rows = grad_memory[begin:reach]
        per_dp = jnp.dot(attn_rows, pvalues.T, preferred_element_type=jnp.float32)
        seq_dp = jnp.dot(attn_rows, value_rows.T, preferred_element_type=jnp.float32)
        delta = jnp.sum(per_prob * per_dp, axis=1, keepdims=True) + jnp.sum(
            seq_prob * seq_dp, axis=1, keepdims=True
        )
        per_ds = (per_prob * (per_dp - delta)).astype(jnp.bfloat16)
        seq_ds = (seq_prob * (seq_dp - delta)).astype(jnp.bfloat16)
        rows_grad = (
            jnp.dot(per_ds, pkeys, preferred_element_type=jnp.float32)
            + jnp.dot(seq_ds, key_rows, preferred_element_type=jnp.float32)
        ) * scale
        grad_pkeys = (
            grad_pkeys
            + jnp.einsum("qk,qd->kd", per_ds, query_rows, preferred_element_type=jnp.float32)
            * scale
        )
        grad_pvalues = grad_pvalues + jnp.einsum(
            "qk,qd->kd",
            per_prob.astype(jnp.bfloat16),
            attn_rows,
            preferred_element_type=jnp.float32,
        )
        key_part = (
            jnp.einsum("qk,qd->kd", seq_ds, query_rows, preferred_element_type=jnp.float32) * scale
        )
        value_part = jnp.einsum(
            "qk,qd->kd",
            seq_prob.astype(jnp.bfloat16),
            attn_rows,
            preferred_element_type=jnp.float32,
        )
        memory_w = (inner * decay_w * (1.0 / width)).astype(jnp.bfloat16)
        grad_mw = jnp.dot(memory_rows, value_rows.T, preferred_element_type=jnp.float32)
        value_part = value_part + jnp.einsum(
            "qk,qd->kd", memory_w, memory_rows, preferred_element_type=jnp.float32
        )
        grad_inner = (grad_mw * decay_w * (1.0 / width)).astype(jnp.bfloat16)
        rows_grad = rows_grad + jnp.dot(grad_inner, key_rows, preferred_element_type=jnp.float32)
        key_part = key_part + jnp.einsum(
            "qk,qd->kd", grad_inner, query_rows, preferred_element_type=jnp.float32
        )
        grad_rate = grad_rate - jnp.sum(grad_mw * inner * decay_w * (1.0 / width) * distance)
        grad_keys = grad_keys.at[:reach].add(key_part)
        grad_values = grad_values.at[:reach].add(value_part)
        query_grads.append(rows_grad)
    return (
        jnp.concatenate(query_grads, 0),
        grad_keys,
        grad_values,
        grad_pkeys,
        grad_pvalues,
        grad_rate,
    )


def layer_forward(rows_in, seg_ids, full, pkv, rates):
    mix_w, out_w, gu_w, down_w, gains = full
    tokens = rows_in.shape[0]
    gain_one = gains[:, 0].astype(jnp.float32)
    gain_two = gains[:, 1].astype(jnp.float32)
    inverse_one = rms_scale(rows_in)
    scaled_one = rows_in * inverse_one
    normed = (scaled_one * gain_one).astype(jnp.bfloat16)
    proj = jnp.dot(normed, mix_w, preferred_element_type=jnp.float32)
    qkv = proj[:, : 3 * D].astype(jnp.bfloat16).reshape(tokens, 3, H, HD)
    gate = jax.nn.sigmoid(proj[:, 3 * D :])
    grouped = lax.all_to_all(qkv, "seq", split_axis=2, concat_axis=0, tiled=True)
    attn_heads, memory_heads, lse_heads = ([], [], [])
    for head in range(grouped.shape[2]):
        cols = slice(head * HD, (head + 1) * HD)
        attended, recalled, lse = head_forward(
            grouped[:, 0, head],
            grouped[:, 1, head],
            grouped[:, 2, head],
            pkv[0][:, cols],
            pkv[1][:, cols],
            rates[head],
            seg_ids,
        )
        attn_heads.append(attended)
        memory_heads.append(recalled)
        lse_heads.append(lse)
    mixed = jnp.stack([jnp.stack(attn_heads, 1), jnp.stack(memory_heads, 1)], 1).astype(
        jnp.bfloat16
    )
    returned = lax.all_to_all(mixed, "seq", split_axis=0, concat_axis=2, tiled=True)
    attended = returned[:, 0].reshape(tokens, D).astype(jnp.float32)
    recalled = returned[:, 1].reshape(tokens, D).astype(jnp.float32)
    combined = (attended + gate * recalled).astype(jnp.bfloat16)
    mid = rows_in + jnp.dot(combined, out_w, preferred_element_type=jnp.float32)
    inverse_two = rms_scale(mid)
    scaled_two = mid * inverse_two
    normed_two = (scaled_two * gain_two).astype(jnp.bfloat16)
    gate_up = jnp.dot(normed_two, gu_w, preferred_element_type=jnp.float32)
    hidden = (jax.nn.silu(gate_up[:, :FF]) * gate_up[:, FF:]).astype(jnp.bfloat16)
    result = mid + jnp.dot(hidden, down_w, preferred_element_type=jnp.float32)
    kept = (
        seg_ids,
        inverse_one,
        scaled_one,
        normed,
        grouped,
        jnp.stack(lse_heads, 1),
        gate,
        recalled,
        combined,
        inverse_two,
        scaled_two,
        normed_two,
        gate_up,
        hidden,
    )
    return (result, kept)


def layer_backward(grad_out, kept, full, pkv, rates):
    (
        seg_ids,
        inverse_one,
        scaled_one,
        normed,
        grouped,
        lse_all,
        gate,
        recalled,
        combined,
        inverse_two,
        scaled_two,
        normed_two,
        gate_up,
        hidden,
    ) = kept
    mix_w, out_w, gu_w, down_w, gains = full
    tokens = grad_out.shape[0]
    gain_one = gains[:, 0].astype(jnp.float32)
    gain_two = gains[:, 1].astype(jnp.float32)
    grad_f = grad_out.astype(jnp.bfloat16)
    grad_down = jnp.einsum("tf,td->fd", hidden, grad_f, preferred_element_type=jnp.float32)
    grad_hidden = jnp.dot(grad_f, down_w.T, preferred_element_type=jnp.float32)
    gate_part = gate_up[:, :FF]
    up_part = gate_up[:, FF:]
    sig_part = jax.nn.sigmoid(gate_part)
    grad_gate_part = grad_hidden * up_part * sig_part * (1.0 + gate_part * (1.0 - sig_part))
    grad_up_part = grad_hidden * gate_part * sig_part
    grad_gate_up = jnp.concatenate([grad_gate_part, grad_up_part], 1).astype(jnp.bfloat16)
    grad_gu = jnp.einsum("td,tf->df", normed_two, grad_gate_up, preferred_element_type=jnp.float32)
    grad_normed_two = jnp.dot(grad_gate_up, gu_w.T, preferred_element_type=jnp.float32)
    grad_mid_norm, grad_gain_two = norm_back(grad_normed_two, scaled_two, inverse_two, gain_two)
    grad_mid = grad_out + grad_mid_norm
    grad_branch = grad_mid.astype(jnp.bfloat16)
    grad_out_w = jnp.einsum("td,te->de", combined, grad_branch, preferred_element_type=jnp.float32)
    grad_combined = jnp.dot(grad_branch, out_w.T, preferred_element_type=jnp.float32)
    grad_attended = grad_combined.astype(jnp.bfloat16).reshape(tokens, H, HD)
    grad_recalled = (grad_combined * gate).astype(jnp.bfloat16).reshape(tokens, H, HD)
    grad_gate_pre = grad_combined * recalled * gate * (1.0 - gate)
    outgoing = jnp.stack([grad_attended, grad_recalled], 1)
    headward = lax.all_to_all(outgoing, "seq", split_axis=2, concat_axis=0, tiled=True)
    head_grads, pkey_grads, pvalue_grads, rate_grads = ([], [], [], [])
    for head in range(grouped.shape[2]):
        cols = slice(head * HD, (head + 1) * HD)
        dq, dk, dv, dpk, dpv, drate = head_backward(
            grouped[:, 0, head],
            grouped[:, 1, head],
            grouped[:, 2, head],
            pkv[0][:, cols],
            pkv[1][:, cols],
            rates[head],
            seg_ids,
            lse_all[:, head],
            headward[:, 0, head],
            headward[:, 1, head],
        )
        head_grads.append(jnp.stack([dq, dk, dv], 1))
        pkey_grads.append(dpk)
        pvalue_grads.append(dpv)
        rate_grads.append(drate)
    grads_heads = jnp.stack(head_grads, 2).astype(jnp.bfloat16)
    tokenward = lax.all_to_all(grads_heads, "seq", split_axis=0, concat_axis=2, tiled=True)
    grad_proj = jnp.concatenate(
        [tokenward.reshape(tokens, 3 * D), grad_gate_pre.astype(jnp.bfloat16)], 1
    )
    grad_mix = jnp.einsum("td,tf->df", normed, grad_proj, preferred_element_type=jnp.float32)
    grad_normed = jnp.dot(grad_proj, mix_w.T, preferred_element_type=jnp.float32)
    grad_in_norm, grad_gain_one = norm_back(grad_normed, scaled_one, inverse_one, gain_one)
    grad_rows = grad_mid + grad_in_norm
    weight_terms = (
        grad_mix,
        grad_out_w,
        grad_gu,
        grad_down,
        jnp.stack([grad_gain_one, grad_gain_two], 1),
    )
    memory_terms = (
        jnp.stack([jnp.concatenate(pkey_grads, 1), jnp.concatenate(pvalue_grads, 1)], 0),
        jnp.stack(rate_grads, 0),
    )
    return (weight_terms, memory_terms, grad_rows)


def on_device(
    inputs, segment_ids, cotangent, w_mix, w_out, w_gu, w_down, norm_gains, persist_kv, memory_decay
):
    first = lax.axis_index("section") == 0
    own_weights = (w_mix[0], w_out[0], w_gu[0], w_down[0], norm_gains[0])
    pkv = persist_kv[0]
    rates = memory_decay[0]
    count = inputs.shape[0]
    tokens = inputs.shape[2]
    zero_rows = jnp.zeros((tokens, D), jnp.float32)
    received = jnp.zeros((tokens, D), jnp.bfloat16)
    kept_ticks, out_ticks = ([], [])
    for tick in range(count + 1):
        own_rows = inputs[tick, 0].astype(jnp.float32) if tick < count else zero_rows
        layer_in = jnp.where(first, own_rows, received.astype(jnp.float32))
        seg_ids = jnp.where(
            first, segment_ids[min(tick, count - 1), 0], segment_ids[max(tick - 1, 0), 0]
        )
        full = (
            lax.all_gather(own_weights[0], "shard", axis=0, tiled=True),
            lax.all_gather(own_weights[1], "shard", axis=0, tiled=True),
            lax.all_gather(own_weights[2], "shard", axis=0, tiled=True),
            lax.all_gather(own_weights[3], "shard", axis=0, tiled=True),
            lax.all_gather(own_weights[4], "shard", axis=0, tiled=True),
        )
        result, kept = layer_forward(layer_in, seg_ids, full, pkv, rates)
        result_low = result.astype(jnp.bfloat16)
        out_ticks.append(result_low)
        kept_ticks.append(kept)
        if tick < count:
            received = shifted(result_low, "section", 1)
    grad_weights = (
        jnp.zeros((D, 4 * D), jnp.float32),
        jnp.zeros((D, D), jnp.float32),
        jnp.zeros((D, 2 * FF), jnp.float32),
        jnp.zeros((FF, D), jnp.float32),
        jnp.zeros((D, 2), jnp.float32),
    )
    grad_memory = (
        jnp.zeros((2,) + pkv.shape[1:], jnp.float32),
        jnp.zeros(rates.shape, jnp.float32),
    )
    back_received = jnp.zeros((tokens, D), jnp.bfloat16)
    grad_ticks = []
    for tick in range(count + 1):
        lower = max(tick - 1, 0)
        upper = min(tick + 1, count)
        kept = jax.tree.map(
            lambda early, late: jnp.where(first, early, late), kept_ticks[lower], kept_ticks[upper]
        )
        given = cotangent[tick, 0].astype(jnp.float32) if tick < count else zero_rows
        grad_out = jnp.where(first, back_received.astype(jnp.float32), given)
        full = (
            lax.all_gather(own_weights[0], "shard", axis=0, tiled=True),
            lax.all_gather(own_weights[1], "shard", axis=0, tiled=True),
            lax.all_gather(own_weights[2], "shard", axis=0, tiled=True),
            lax.all_gather(own_weights[3], "shard", axis=0, tiled=True),
            lax.all_gather(own_weights[4], "shard", axis=0, tiled=True),
        )
        weight_terms, memory_terms, grad_rows = layer_backward(grad_out, kept, full, pkv, rates)
        grad_weights = jax.tree.map(jnp.add, grad_weights, weight_terms)
        grad_memory = jax.tree.map(jnp.add, grad_memory, memory_terms)
        grad_ticks.append(grad_rows)
        if tick < count:
            back_received = shifted(grad_rows.astype(jnp.bfloat16), "section", -1)
    section_out = jnp.stack(
        [jnp.where(first, out_ticks[batch], out_ticks[batch + 1]) for batch in range(count)], 0
    )
    section_grad = jnp.stack(
        [
            jnp.where(
                first,
                grad_ticks[batch + 1],
                grad_ticks[batch].astype(jnp.bfloat16).astype(jnp.float32),
            )
            for batch in range(count)
        ],
        0,
    )
    shares = jax.tree.map(
        lambda part: part.astype(jnp.float32),
        lax.psum_scatter(as_sent(grad_weights), "shard", scatter_dimension=0, tiled=True),
    )
    shares = jax.tree.map(lambda part: part.astype(jnp.float32), lax.psum(as_sent(shares), "seq"))
    memory_sums = lax.psum(grad_memory, "shard")
    return (
        section_out.reshape(1, count, 1, tokens, D),
        section_grad.reshape(1, count, 1, tokens, D),
        shares[0][None],
        shares[1][None],
        shares[2][None],
        shares[3][None],
        shares[4][None],
        memory_sums[0][None],
        memory_sums[1][None],
    )


def solution(mesh):
    placed = (
        P(None, "shard", "seq", None),
        P(None, "shard", None),
        P(None, "shard", "seq", None),
        P("section", "shard", None),
        P("section", "shard", None),
        P("section", "shard", None),
        P("section", "shard", None),
        P("section", "shard", None),
        P("section", None, None, "seq"),
        P("section", "seq"),
    )
    return jax.shard_map(
        on_device,
        mesh=mesh,
        in_specs=placed,
        out_specs=(
            P("section", None, "shard", "seq", None),
            P("section", None, "shard", "seq", None),
            P("section", "shard", None),
            P("section", "shard", None),
            P("section", "shard", None),
            P("section", "shard", None),
            P("section", "shard", None),
            P("section", None, None, "seq"),
            P("section", "seq"),
        ),
        check_vma=False,
    )
```

profile of v0, /device:TPU:3, one launch (start us, length us, event | category | flops | bytes accessed | tf_op | source)
XLA Modules:
  0.0 1490.6 jit_solution(2207354995321027607)
XLA Ops:
  10.2 9.1 all-gather
  19.3 141.4 %all-gather.10.cloned.1.call-done = bf16[1,1024,4096]{2,1,0:T(8,128)(2,1)} async-done(((bf16[1,256,4096]{2,1,0:T(8,128)(2,1)}), bf16[1,1024,4096]{2,1,0:T(8,128)(2,1)}) %all-gather.10.cloned.1.call-update) | async-done | bytes 8388624 | tf_op jit(solution)/shard_map/all_gather | solution.py:330
  172.8 9.0 all-to-all-done
  188.9 11.4 all_to_all.207
  210.0 197.8 %all-gather.14.cloned.1.call-done = bf16[1,1024,5632]{2,1,0:T(8,128)(2,1)} async-done(((bf16[1,256,5632]{2,1,0:T(8,128)(2,1)}), bf16[1,1024,5632]{2,1,0:T(8,128)(2,1)}) %all-gather.14.cloned.1.call-update) | async-done | bytes 11534352 | tf_op jit(solution)/shard_map/all_gather | solution.py:332
  415.2 99.0 %all-gather.16.cloned.1.call-done = bf16[1,2816,1024]{2,1,0:T(8,128)(2,1)} async-done(((bf16[1,704,1024]{2,1,0:T(8,128)(2,1)}), bf16[1,2816,1024]{2,1,0:T(8,128)(2,1)}) %all-gather.16.cloned.1.call-update) | async-done | bytes 5767184 | tf_op jit(solution)/shard_map/all_gather | solution.py:333
  519.6 7.8 collective-permute-done
  541.7 10.3 all-to-all-done.2
  558.3 11.2 all_to_all.208
  589.3 15.0 %all_to_all.209 = bf16[128,3,8,128]{3,0,1,2:T(8,128)(2,1)S(1)} all-to-all(bf16[128,3,8,128]{3,0,1,2:T(8,128)(2,1)S(1)} %copy.207), channel_id=1, replica_groups=mesh['section'=2,'seq'=4,'shard'=4] {'seq'}, dimensions={2} | all-to-all | bytes 1572864 | tf_op jit(solution)/shard_map/all_to_all | solution.py:178
  628.9 12.5 broadcast_select_fusion
  694.1 9.1 all-to-all-done.7
  832.2 8.9 add_convert_fusion.2
  854.4 9.5 fusion.197
  881.5 8.3 fusion.196
  894.5 15.8 %add_convert_fusion.1 = bf16[1024,4096]{1,0:T(8,128)(2,1)} fusion(f32[1024,4096]{1,0:T(8,128)} %fusion.197, f32[1024,4096]{1,0:T(8,128)} %fusion.196, bf16[128,1024]{0,1:T(8,128)(2,1)S(1)} %copy.241, bf16[128,3072]{0,1:T(8,128)(2,1)} %bitcast.895, bf16[128,1024]{1,0:T(8,128)(2,1)S(1)} %copy-done.41, pred[]{:T(512)S(6)} %eq.40, ...), kind=kOutput, calls=%fused_computation.1 | convolution fusion | flops 1089208320 | bytes 43520512 | tf_op jit(solution)/shard_map/td,tf->df/dot_general | solution.py:293
  911.5 10.6 fusion.178
  922.2 9.5 fusion.177
  931.7 20.5 %add_convert_fusion = bf16[1024,5632]{1,0:T(8,128)(2,1)} fusion(f32[1024,5632]{1,0:T(8,128)} %fusion.178, f32[1024,5632]{1,0:T(8,128)} %fusion.177, bf16[128,2816]{1,0:T(8,128)(2,1)S(1)} %copy-done.77, bf16[128,2816]{1,0:T(8,128)(2,1)S(1)} %copy-done.75, bf16[128,1024]{1,0:T(8,128)(2,1)S(1)} %copy-done.36, bf16[128,1024]{1,0:T(8,128)(2,1)S(1)} %copy-done.34, ...), kind=kOutput, calls=%fused_computation | convolution fusion | flops 1496711168 | bytes 59637760 | tf_op jit(solution)/shard_map/td,tf->df/dot_general | solution.py:257
  969.9 147.3 %reduce-scatter.8.cloned.1.call-done = bf16[256,4096]{1,0:T(8,128)(2,1)} async-done(((bf16[1024,4096]{1,0:T(8,128)(2,1)}), bf16[256,4096]{1,0:T(8,128)(2,1)}) %reduce-scatter.8.cloned.1.call-update) | async-done | bytes 2097168 | tf_op jit(solution)/shard_map/reduce_scatter | solution.py:392
  1117.2 198.4 %reduce-scatter.12.cloned.1.call-done = bf16[256,5632]{1,0:T(8,128)(2,1)} async-done(((bf16[1024,5632]{1,0:T(8,128)(2,1)}), bf16[256,5632]{1,0:T(8,128)(2,1)}) %reduce-scatter.12.cloned.1.call-update) | async-done | bytes 2883600 | tf_op jit(solution)/shard_map/reduce_scatter | solution.py:392
  1324.8 16.3 %all-reduce = (f32[1,2,16,256]{3,2,1,0:T(8,128)}, f32[1,2]{1,0:T(1,128)}) all-reduce(f32[1,2,16,256]{3,2,1,0:T(8,128)S(1)} %fusion.359, f32[1,2]{1,0:T(1,128)S(1)} %fusion.405), channel_id=1, replica_groups=mesh['section'=2,'seq'=4,'shard'=4] {'shard'}, use_global_device_ids=true, to_apply=%region_64.65 | all-reduce | flops 8194 | bytes 65552 | tf_op jit(solution)/shard_map/psum | solution.py:395
  1345.5 9.6 psum.53
  1355.7 115.2 %all-reduce.4.cloned.1.call-done = (bf16[1,256,4096]{2,1,0:T(8,128)(2,1)}, bf16[1,256,1024]{2,1,0:T(8,128)(2,1)}, bf16[1,256,5632]{2,1,0:T(8,128)(2,1)}, bf16[1,704,1024]{2,1,0:T(8,128)(2,1)}) async-done(((bf16[1,256,4096]{2,1,0:T(8,128)(2,1)}, bf16[1,256,1024]{2,1,0:T(8,128)(2,1)}, bf16[1,256,5632]{2,1,0:T(8,128)(2,1)}, bf16[1,704,1024]{2,1,0:T(8,128)(2,1)}), (bf16[1,256,4096]{2,1,0:T(8,128)(2,1)}, ...) | async-done | bytes 6946832 | tf_op jit(solution)/shard_map/psum | solution.py:394
  (691 shorter events, 364.6 us)
Async XLA Ops:
  7.2 153.5 %all-gather.10.cloned.1.call-start = ((), (), s32[]{:S(2)}) async-start(), calls=%async_computation.21 | async-start | bytes 10485760 | tf_op jit(solution)/shard_map/all_gather | solution.py:330
  7.9 198.3 %all-gather.12.cloned.1.call-start = ((), (), s32[]{:S(2)}) async-start(), calls=%async_computation.22 | async-start | bytes 2621440 | tf_op jit(solution)/shard_map/all_gather | solution.py:331
  8.7 399.2 %all-gather.14.cloned.1.call-start = ((), (), s32[]{:S(2)}) async-start(), calls=%async_computation.23 | async-start | bytes 14417920 | tf_op jit(solution)/shard_map/all_gather | solution.py:332
  9.4 504.8 %all-gather.16.cloned.1.call-start = ((), (), s32[]{:S(2)}) async-start(), calls=%async_computation.24 | async-start | bytes 7208960 | tf_op jit(solution)/shard_map/all_gather | solution.py:333
  167.0 14.8 all-to-all-start
  518.1 9.3 collective-permute-start
  528.1 187.0 %copy-start.137 = (f32[128]{0:T(128)}, f32[128]{0:T(128)S(1)}, u32[]{:S(2)}) copy-start(f32[128]{0:T(128)S(1)} %add_rsqrt_fusion.3) | copy-start | bytes 1540
  535.7 16.3 %all-to-all-start.2 = ((bf16[128,3,8,128]{3,0,1,2:T(8,128)(2,1)}), bf16[128,3,8,128]{3,0,1,2:T(8,128)(2,1)}, u32[]{:S(2)}, u32[]{:S(2)}) async-start(bf16[128,3,8,128]{3,0,1,2:T(8,128)(2,1)} %copy.202), calls=%async_computation.2 | async-start | bytes 1572864 | tf_op jit(solution)/shard_map/all_to_all | solution.py:178
  577.1 8.8 collective-permute-start.1
  610.1 13.7 all-to-all-start.5
  659.5 13.2 all-to-all-start.6
  687.3 15.9 %all-to-all-start.7 = ((bf16[512,3,2,128]{3,2,1,0:T(2,128)(2,1)}), bf16[512,3,2,128]{3,2,1,0:T(2,128)(2,1)}, u32[]{:S(2)}, u32[]{:S(2)}) async-start(bf16[512,3,2,128]{3,2,1,0:T(2,128)(2,1)} %copy.218), calls=%async_computation.7 | async-start | bytes 1572864 | tf_op jit(solution)/shard_map/all_to_all | solution.py:289
  715.4 6.3 collective-permute-start.2
  740.4 13.8 all-to-all-start.8
  768.6 15.1 %all-to-all-start.9 = ((bf16[512,3,2,128]{3,2,1,0:T(2,128)(2,1)}), bf16[512,3,2,128]{3,2,1,0:T(2,128)(2,1)S(1)}, u32[]{:S(2)}, u32[]{:S(2)}) async-start(bf16[512,3,2,128]{3,2,1,0:T(2,128)(2,1)} %copy.228), calls=%async_computation.9 | async-start | bytes 1572864 | tf_op jit(solution)/shard_map/all_to_all | solution.py:289
  772.9 196.3 %reduce-scatter.10.cloned.1.call-start = ((), (), s32[]{:S(2)}) async-start(), calls=%async_computation.18 | async-start | bytes 2621440 | tf_op jit(solution)/shard_map/reduce_scatter | solution.py:392
  794.7 9.1 collective-permute-start.3
  821.9 148.0 %reduce-scatter.14.cloned.1.call-start = ((), (), s32[]{:S(2)}) async-start(), calls=%async_computation.20 | async-start | bytes 7208960 | tf_op jit(solution)/shard_map/reduce_scatter | solution.py:392
  848.1 15.7 %all-to-all-start.10 = ((bf16[128,2,8,128]{3,0,1,2:T(8,128)(2,1)}), bf16[128,2,8,128]{3,0,1,2:T(8,128)(2,1)}, u32[]{:S(2)}, u32[]{:S(2)}) async-start(bf16[128,2,8,128]{3,0,1,2:T(8,128)(2,1)} %pad_maximum_fusion.26), calls=%async_computation.10 | async-start | bytes 1048576 | tf_op jit(solution)/shard_map/all_to_all | solution.py:268
  876.9 15.1 %all-to-all-start.11 = ((bf16[512,3,2,128]{3,2,1,0:T(2,128)(2,1)}), bf16[512,3,2,128]{3,2,1,0:T(2,128)(2,1)}, u32[]{:S(2)}, u32[]{:S(2)}) async-start(bf16[512,3,2,128]{3,2,1,0:T(2,128)(2,1)} %copy.238), calls=%async_computation.11 | async-start | bytes 1572864 | tf_op jit(solution)/shard_map/all_to_all | solution.py:289
  881.2 236.0 %reduce-scatter.8.cloned.1.call-start = ((), (), s32[]{:S(2)}) async-start(), calls=%async_computation.17 | async-start | bytes 10485760 | tf_op jit(solution)/shard_map/reduce_scatter | solution.py:392
  910.3 405.2 %reduce-scatter.12.cloned.1.call-start = ((), (), s32[]{:S(2)}) async-start(), calls=%async_computation.19 | async-start | bytes 14417920 | tf_op jit(solution)/shard_map/reduce_scatter | solution.py:392
  952.3 392.3 %reduce-scatter.16.cloned.1.call-start = ((), (), s32[]{:S(2)}) async-start(), calls=%async_computation.25 | async-start | bytes 327680
  967.9 503.0 %all-reduce.4.cloned.1.call-start = ((), (), s32[]{:S(2)}) async-start(), calls=%async_computation.26 | async-start | bytes 13893632 | tf_op jit(solution)/shard_map/psum | solution.py:394
  (165 other events, 1290.3 us)
Sparse Core Ops, SparseCore 0:
  9.6 151.0 all-gather.9
  162.3 43.9 all-gather.11
  207.8 199.9 all-gather.13
  409.3 104.8 all-gather.15
  822.0 43.1 reduce-scatter.9
  868.0 101.8 reduce-scatter.13
  972.4 144.7 reduce-scatter.7
  1119.7 195.8 reduce-scatter.11
  1318.5 18.6 reduce-scatter.15
  1339.6 131.2 all-reduce.3
where the time goes:
time: 1500 us; the launch traced here: 1490 us
  waiting for transfers between devices  981 us (65%)
  matrix products  266 us (18%)
  blocking collectives  72.5 us (5%)
  starting transfers between devices  56.4 us (4%)
  local copies, waits for them, and re-layouts  49.9 us (3%)
  other arithmetic  41.7 us (3%)
  between operations  22.7 us (2%)
    reduce_scatter x4, waiting for transfers between devices, on_device(): lax.psum_scatter(as_sent(grad_weights), 'shard', scatter_dimension=0, til...  346 us
    all_gather x1, waiting for transfers between devices, on_device(): lax.all_gather(own_weights[2], 'shard', axis=0, tiled=True)  198 us
    all_gather x1, waiting for transfers between devices, on_device(): lax.all_gather(own_weights[0], 'shard', axis=0, tiled=True)  141 us
    psum x1, waiting for transfers between devices, on_device(): lax.psum(as_sent(shares), 'seq')  115 us
    all_gather x1, waiting for transfers between devices, on_device(): lax.all_gather(own_weights[3], 'shard', axis=0, tiled=True)  99 us
    dot_general x3, matrix products, layer_backward(): jnp.einsum('td,tf->df', normed_two, grad_gate_up, preferred_element_type=...  40.7 us
    dot_general x3, matrix products, layer_backward(): jnp.einsum('td,tf->df', normed, grad_proj, preferred_element_type=jnp.flo...  33.5 us
  transfers between devices with their start and end apart: 23, of which 20 were waited for; matrix products, arithmetic and copies ran while one was open for 12% of the time, Pallas kernels for 0%

commit v1 on v0

--- a/solution.py
+++ b/solution.py
@@ -1,8 +1,11 @@
+import functools
 import math
 
 import jax
 import jax.numpy as jnp
 from jax import lax
+from jax.experimental import pallas as pl
+from jax.experimental.pallas import tpu as pltpu
 from jax.sharding import PartitionSpec as P
 
 D = 1024
@@ -406,7 +409,511 @@
     )
 
 
+MESH = pl.DeviceIdType.MESH
+BF = jnp.bfloat16
+F32 = jnp.float32
+
+
+def here():
+    return (lax.axis_index("section"), lax.axis_index("seq"), lax.axis_index("shard"))
+
+
+def peer(place, chip, flip):
+    x, s, z = place
+    if chip % 2:
+        x = 1 - x
+    if chip // 2:
+        s = (s + 2) % 4
+    if flip:
+        s = s + 1 - 2 * (s % 2)
+    return (x, s, z)
+
+
+def rows_of(device, size):
+    x, s, _ = device
+    return pl.ds(pl.multiple_of((s * 2 + x) * size, size), size)
+
+
+class Gather:
+    def __init__(self, full, batch, send, recv):
+        self.place = here()
+        self.full, self.batch, self.send, self.recv = full, batch, send, recv
+        self.size = full.shape[1] // 8
+
+    def copy(self, owner, target, sem):
+        block = self.full.at[self.batch, rows_of(owner, self.size)]
+        return pltpu.make_async_remote_copy(
+            src_ref=block,
+            dst_ref=block,
+            send_sem=self.send.at[self.batch, sem],
+            recv_sem=self.recv.at[self.batch, sem],
+            device_id=target,
+            device_id_type=MESH,
+        )
+
+    def start(self, value):
+        self.full[self.batch, rows_of(self.place, self.size), :] = value
+        for chip in (3, 1, 2, 0):
+            self.copy(self.place, peer(self.place, chip, chip == 0), chip).start()
+
+    def forward(self):
+        other = peer(self.place, 0, True)
+        for chip in (1, 2, 3):
+            owner = peer(self.place, chip, False)
+            self.copy(owner, owner, chip).wait_recv()
+            self.copy(owner, other, 3 + chip).start()
+
+    def finish(self):
+        other = peer(self.place, 0, True)
+        self.copy(other, other, 0).wait_recv()
+        for chip in (1, 2, 3):
+            owner = peer(self.place, chip, True)
+            self.copy(owner, other, 3 + chip).wait_recv()
+        for chip in (0, 1, 2, 3):
+            self.copy(self.place, peer(self.place, chip, chip == 0), chip).wait_send()
+        for chip in (1, 2, 3):
+            self.copy(peer(self.place, chip, False), other, 3 + chip).wait_send()
+
+
+class Scatter:
+    def __init__(self, part, batch, pair, away, near, send, recv):
+        self.place = here()
+        self.part, self.batch, self.pair, self.away, self.near = part, batch, pair, away, near
+        self.send, self.recv = send, recv
+        self.size = part.shape[1] // 8
+
+    def to_pair(self, chip):
+        return pltpu.make_async_remote_copy(
+            src_ref=self.part.at[self.batch, rows_of(peer(self.place, chip, True), self.size)],
+            dst_ref=self.pair.at[self.batch, chip],
+            send_sem=self.send.at[self.batch, chip],
+            recv_sem=self.recv.at[self.batch, chip],
+            device_id=peer(self.place, 0, True),
+            device_id_type=MESH,
+        )
+
+    def to_chip(self, chip):
+        return pltpu.make_async_remote_copy(
+            src_ref=self.away.at[self.batch, chip - 1],
+            dst_ref=self.near.at[self.batch, chip - 1],
+            send_sem=self.send.at[self.batch, 3 + chip],
+            recv_sem=self.recv.at[self.batch, 3 + chip],
+            device_id=peer(self.place, chip, False),
+            device_id_type=MESH,
+        )
+
+    def start(self):
+        for chip in (3, 1, 2, 0):
+            self.to_pair(chip).start()
+
+    def chip_sum(self, chip):
+        self.to_pair(chip).wait_recv()
+        own = self.part[self.batch, rows_of(peer(self.place, chip, False), self.size), :]
+        return own.astype(F32) + self.pair[self.batch, chip].astype(F32)
+
+    def forward(self):
+        for chip in (3, 1, 2):
+            self.away[self.batch, chip - 1] = self.chip_sum(chip).astype(BF)
+            self.to_chip(chip).start()
+
+    def finish(self):
+        total = self.chip_sum(0)
+        for chip in (1, 2, 3):
+            self.to_chip(chip).wait_recv()
+            total = total + self.near[self.batch, chip - 1].astype(F32)
+        for chip in (0, 1, 2, 3):
+            self.to_pair(chip).wait_send()
+        for chip in (1, 2, 3):
+            self.to_chip(chip).wait_send()
+        return total
+
+
+def meet():
+    place = here()
+    barrier = pltpu.get_barrier_semaphore()
+    for chip in (0, 1, 2, 3):
+        pl.semaphore_signal(
+            barrier, inc=1, device_id=peer(place, chip, chip == 0), device_id_type=MESH
+        )
+    pl.semaphore_wait(barrier, 4)
+
+
+def start_kernel(rows_ref, gain_ref, full_ref, gsend, grecv):
+    meet()
+    gathers = [Gather(full_ref, batch, gsend, grecv) for batch in range(2)]
+    for batch, gather in enumerate(gathers):
+        rows = rows_ref[batch]
+        gather.start((rows * rms_scale(rows) * gain_ref[...]).astype(BF))
+    for gather in gathers:
+        gather.forward()
+    for gather in gathers:
+        gather.finish()
+
+
+def forward_kernel(low, last, part_ref, rows_ref, gain_ref, own_ref, *rest):
+    if last:
+        pair, away, near, ssend, srecv = rest
+    else:
+        full_ref, pair, away, near, ssend, srecv, gsend, grecv = rest
+    meet()
+    scatters = [Scatter(part_ref, b, pair, away, near, ssend, srecv) for b in range(2)]
+    for scatter in scatters:
+        scatter.start()
+    for scatter in scatters:
+        scatter.forward()
+    gathers = []
+    for batch, scatter in enumerate(scatters):
+        own = (rows_ref[batch] + scatter.finish()).astype(own_ref.dtype)
+        own_ref[batch] = own
+        if not last:
+            own = own.astype(F32)
+            gather = Gather(full_ref, batch, gsend, grecv)
+            gather.start((own * rms_scale(own) * gain_ref[...]).astype(BF))
+            gathers.append(gather)
+    for gather in gathers:
+        gather.forward()
+    for gather in gathers:
+        gather.finish()
+
+
+def backward_kernel(last, part_ref, rows_ref, gain_ref, grad_ref, own_ref, gains_ref, *rest):
+    if last:
+        pair, away, near, ssend, srecv = rest
+    else:
+        full_ref, pair, away, near, ssend, srecv, gsend, grecv = rest
+    meet()
+    scatters = [Scatter(part_ref, b, pair, away, near, ssend, srecv) for b in range(2)]
+    for scatter in scatters:
+        scatter.start()
+    for scatter in scatters:
+        scatter.forward()
+    gathers = []
+    sums = jnp.zeros((1, D), F32)
+    for batch, scatter in enumerate(scatters):
+        grad_normed = scatter.finish()
+        rows = rows_ref[batch]
+        inverse = rms_scale(rows)
+        grad_rows, gain_sum = norm_back(grad_normed, rows * inverse, inverse, gain_ref[...])
+        sums = sums + gain_sum[None]
+        own = (grad_ref[batch] + grad_rows).astype(own_ref.dtype)
+        own_ref[batch] = own
+        if not last:
+            gather = Gather(full_ref, batch, gsend, grecv)
+            gather.start(own.astype(BF))
+            gathers.append(gather)
+    gains_ref[...] = sums
+    for gather in gathers:
+        gather.forward()
+    for gather in gathers:
+        gather.finish()
+
+
+def plane_call(kernel, number, operands, outs, scatter, gather):
+    _, length, width = outs["full"].shape
+    size = length // 8
+    scratch = []
+    if scatter:
+        scratch += [
+            pltpu.VMEM((2, 4, size, width), BF),
+            pltpu.VMEM((2, 3, size, width), BF),
+            pltpu.VMEM((2, 3, size, width), BF),
+            pltpu.SemaphoreType.DMA((2, 7)),
+            pltpu.SemaphoreType.DMA((2, 7)),
+        ]
+    if gather:
+        scratch += [pltpu.SemaphoreType.DMA((2, 7)), pltpu.SemaphoreType.DMA((2, 7))]
+    else:
+        outs = {name: out for name, out in outs.items() if name != "full"}
+    vmem = pl.BlockSpec(memory_space=pltpu.VMEM)
+    return pl.pallas_call(
+        kernel,
+        out_shape=list(outs.values()),
+        in_specs=[vmem] * len(operands),
+        out_specs=[vmem] * len(outs),
+        scratch_shapes=scratch,
+        compiler_params=pltpu.CompilerParams(
+            collective_id=number, has_side_effects=True, vmem_limit_bytes=24 * 2**20
+        ),
+    )(*operands)
+
+
+def tensor_parallel(
+    inputs, segment_ids, cotangent, w_mix, w_out, w_gu, w_down, norm_gains, persist_kv, memory_decay
+):
+    x, s, z = here()
+    nx, ns, nz = (lax.axis_size(a) for a in ("section", "seq", "shard"))
+    width = nx * ns
+    mine = x * ns + s
+    other = (1 - x) * ns + s
+    first = x == 0
+    count, _, tokens, _ = inputs.shape
+    length = tokens * ns
+    size = length // width
+    depth = w_mix.shape[1]
+    unit = w_down.shape[1] // width
+
+    heads = w_mix[0].reshape(depth, 4, H, HD)
+    halves = w_gu[0].reshape(depth, 2, nz, width, unit)
+    downs = w_down[0].reshape(width, unit, D)
+
+    def pick(which):
+        return (
+            lax.dynamic_index_in_dim(heads, which, 2, keepdims=False).reshape(depth, 4 * HD),
+            lax.dynamic_index_in_dim(halves, which, 3, keepdims=False).reshape(
+                depth, 2 * nz * unit
+            ),
+            lax.dynamic_index_in_dim(downs, which, 0, keepdims=False),
+        )
+
+    def layers(own, got):
+        return (jnp.where(first, own, got), jnp.where(first, got, own))
+
+    swap = [(0, 1), (1, 0)]
+    parts = [layers(o, lax.ppermute(g, "section", swap)) for o, g in zip(pick(mine), pick(other))]
+    out_rows = lax.dynamic_index_in_dim(
+        w_out[0].reshape(2, HD, D), lax.rem(s, 2), 0, keepdims=False
+    )
+    out_all = lax.all_gather(out_rows, "shard", axis=0)
+    out_own = lax.dynamic_index_in_dim(out_all, mine // 2, 0, keepdims=False)
+    out_got = lax.ppermute(
+        lax.dynamic_index_in_dim(out_all, other // 2, 0, keepdims=False), "section", swap
+    )
+    out_w = layers(out_own, out_got)
+    mix_w, gu_w, down_w = (
+        [lax.all_gather(part[layer], "shard", axis=0, tiled=True) for layer in range(2)]
+        for part in parts
+    )
+
+    small = jnp.concatenate([persist_kv[0].reshape(-1).astype(F32), memory_decay[0]])
+    small = lax.all_gather(small, ("section", "seq"), axis=0)
+    rates = small[:, -2:].reshape(2, H)[:, mine]
+    persist = small[:, :-2].astype(BF).reshape(2, ns, 2, persist_kv.shape[2], 2, HD)
+    persist = lax.dynamic_index_in_dim(persist, mine // 2, 1, keepdims=False)
+    persist = lax.dynamic_index_in_dim(persist, lax.rem(mine, 2), 3, keepdims=False)
+    gains = lax.all_gather(norm_gains[0], ("section", "shard"), axis=0, tiled=True)
+    gains = gains.astype(F32).reshape(2, 1, D, 2)
+
+    def own_rows(whole):
+        return lax.dynamic_slice_in_dim(whole[:, 0], x * size, size, 1).astype(F32)
+
+    full = jax.ShapeDtypeStruct((count, length, D), BF)
+    own32 = jax.ShapeDtypeStruct((count, size, D), F32)
+    own16 = jax.ShapeDtypeStruct((count, size, D), BF)
+    sums = jax.ShapeDtypeStruct((1, D), F32)
+
+    cot_full = lax.all_gather(cotangent[:, 0], "seq", axis=1, tiled=True)
+    rows = own_rows(inputs)
+    (normed,) = plane_call(
+        start_kernel, 0, (rows, gains[0, :, :, 0]), {"full": full}, False, True
+    )
+    kept = []
+    outputs = []
+    flat = count * length
+    for layer in range(2):
+        proj = jnp.dot(normed.reshape(flat, D), mix_w[layer], preferred_element_type=F32)
+        qkv = proj[:, : 3 * HD].astype(BF).reshape(count, length, 3, HD)
+        gate = jax.nn.sigmoid(proj[:, 3 * HD :])
+        results = [
+            head_forward(
+                qkv[b, :, 0],
+                qkv[b, :, 1],
+                qkv[b, :, 2],
+                persist[layer, 0],
+                persist[layer, 1],
+                rates[layer],
+                segment_ids[b, 0],
+            )
+            for b in range(count)
+        ]
+        attended = jnp.concatenate([r[0] for r in results], 0).astype(BF).astype(F32)
+        recalled = jnp.concatenate([r[1] for r in results], 0).astype(BF).astype(F32)
+        combined = (attended + gate * recalled).astype(BF)
+        partial = jnp.dot(combined, out_w[layer], preferred_element_type=F32).astype(BF)
+        mid, normed_two = plane_call(
+            functools.partial(forward_kernel, False, False),
+            1 + 2 * layer,
+            (partial.reshape(count, length, D), rows, gains[layer, :, :, 1]),
+            {"own": own32, "full": full},
+            True,
+            True,
+        )
+        gate_up = jnp.dot(normed_two.reshape(flat, D), gu_w[layer], preferred_element_type=F32)
+        half = gate_up.shape[1] // 2
+        hidden = (jax.nn.silu(gate_up[:, :half]) * gate_up[:, half:]).astype(BF)
+        partial = jnp.dot(hidden, down_w[layer], preferred_element_type=F32).astype(BF)
+        kept.append(
+            (rows, normed, qkv, gate, [r[2] for r in results], recalled, combined, mid)
+            + (normed_two, gate_up, hidden)
+        )
+        last = layer == 1
+        found = plane_call(
+            functools.partial(forward_kernel, True, last),
+            2 + 2 * layer,
+            (partial.reshape(count, length, D), mid, gains[1, :, :, 0]),
+            {"own": own16, "full": full},
+            True,
+            not last,
+        )
+        outputs.append(found[0])
+        if not last:
+            rows = found[0].astype(F32)
+            normed = found[1]
+
+    grad_full = cot_full
+    grad_own = own_rows(cotangent)
+    pieces, gain_sums, memory_terms, grads = ([None] * 2, [None] * 2, [None] * 2, [None] * 2)
+    for layer in (1, 0):
+        (
+            rows,
+            normed,
+            qkv,
+            gate,
+            lse,
+            recalled,
+            combined,
+            mid,
+            normed_two,
+            gate_up,
+            hidden,
+        ) = kept[layer]
+        grad_f = grad_full.reshape(flat, D)
+        grad_hidden = jnp.dot(grad_f, down_w[layer].T, preferred_element_type=F32)
+        half = gate_up.shape[1] // 2
+        gate_part = gate_up[:, :half]
+        up_part = gate_up[:, half:]
+        sig_part = jax.nn.sigmoid(gate_part)
+        grad_gate_up = jnp.concatenate(
+            [
+                grad_hidden * up_part * sig_part * (1.0 + gate_part * (1.0 - sig_part)),
+                grad_hidden * gate_part * sig_part,
+            ],
+            1,
+        ).astype(BF)
+        partial = jnp.dot(grad_gate_up, gu_w[layer].T, preferred_element_type=F32).astype(BF)
+        grad_down = jnp.einsum("tf,td->fd", hidden, grad_f, preferred_element_type=F32)
+        grad_gu = jnp.einsum(
+            "td,tf->df", normed_two.reshape(flat, D), grad_gate_up, preferred_element_type=F32
+        )
+        grad_mid, gain_two, branch = plane_call(
+            functools.partial(backward_kernel, False),
+            5 + 2 * (1 - layer),
+            (partial.reshape(count, length, D), mid, gains[layer, :, :, 1], grad_own),
+            {"own": own32, "sums": sums, "full": full},
+            True,
+            True,
+        )
+        branch = branch.reshape(flat, D)
+        grad_combined = jnp.dot(branch, out_w[layer].T, preferred_element_type=F32)
+        grad_out = jnp.einsum("td,te->de", combined, branch, preferred_element_type=F32)
+        grad_attended = grad_combined.astype(BF).reshape(count, length, HD)
+        grad_recalled = (grad_combined * gate).astype(BF).reshape(count, length, HD)
+        grad_gate_pre = grad_combined * recalled * gate * (1.0 - gate)
+        found = [
+            head_backward(
+                qkv[b, :, 0],
+                qkv[b, :, 1],
+                qkv[b, :, 2],
+                persist[layer, 0],
+                persist[layer, 1],
+                rates[layer],
+                segment_ids[b, 0],
+                lse[b],
+                grad_attended[b],
+                grad_recalled[b],
+            )
+            for b in range(count)
+        ]
+        grad_heads = jnp.concatenate([jnp.concatenate(f[:3], 1) for f in found], 0)
+        grad_proj = jnp.concatenate([grad_heads, grad_gate_pre], 1).astype(BF)
+        memory_terms[layer] = (
+            jnp.stack([sum(f[3] for f in found), sum(f[4] for f in found)], 0),
+            sum(f[5] for f in found),
+        )
+        partial = jnp.dot(grad_proj, mix_w[layer].T, preferred_element_type=F32).astype(BF)
+        grad_mix = jnp.einsum(
+            "td,tf->df", normed.reshape(flat, D), grad_proj, preferred_element_type=F32
+        )
+        last = layer == 0
+        found = plane_call(
+            functools.partial(backward_kernel, last),
+            6 + 2 * (1 - layer),
+            (partial.reshape(count, length, D), rows, gains[layer, :, :, 0], grad_mid),
+            {"own": own32 if last else own16, "sums": sums, "full": full},
+            True,
+            not last,
+        )
+        grads[layer] = found[0].astype(BF)
+        gain_sums[layer] = jnp.stack([found[1][0], gain_two[0]], 1)
+        if not last:
+            grad_own = found[0].astype(F32)
+            grad_full = found[2]
+        owner = mine // 2 == jnp.arange(nz)
+        grad_out = jnp.where(owner[:, None, None], grad_out[None], 0.0)
+        pieces[layer] = [
+            lax.psum_scatter(part.astype(BF), "shard", scatter_dimension=0, tiled=True)
+            for part in (grad_mix, grad_gu, grad_down, grad_out.reshape(nz * HD, D))
+        ]
+
+    def to_section(of_layer):
+        own = jnp.where(first, of_layer[0], of_layer[1])
+        got = lax.ppermute(jnp.where(first, of_layer[1], of_layer[0]), "section", swap)
+        return layers(own, got)
+
+    def whole_rows(of_layer):
+        return jnp.concatenate(to_section(of_layer), 1)[None, :, None]
+
+    section_out = whole_rows(outputs)
+    section_grad = whole_rows(grads).astype(F32)
+
+    def collect(index):
+        both = jnp.stack(to_section([pieces[layer][index] for layer in range(2)]), 0)
+        return lax.all_gather(both, "seq", axis=0).astype(F32)
+
+    mix_all = collect(0).reshape(ns, nx, depth, 4, HD)
+    gu_all = collect(1).reshape(ns, nx, depth, 2, nz, unit)
+    down_all = collect(2)
+    out_all = collect(3)
+    grad_mix = mix_all.transpose(2, 3, 1, 0, 4).reshape(1, depth, 4 * D)
+    grad_gu = gu_all.transpose(2, 3, 4, 1, 0, 5).reshape(1, depth, 2 * FF)
+    grad_down = down_all.transpose(1, 0, 2, 3).reshape(1, unit * width, D)
+    out_all = lax.dynamic_index_in_dim(out_all, z // 2, 1, keepdims=False)
+    grad_out = lax.dynamic_slice_in_dim(out_all, 2 * lax.rem(z, 2), 2, 0).reshape(1, 2 * HD, D)
+
+    memory_all = jnp.stack([m[0] for m in memory_terms], 0)
+    places = jnp.arange(width) == mine
+    memory_all = jnp.where(places[None, None, None, :, None], memory_all[:, :, :, None, :], 0.0)
+    rate_all = jnp.where(places[None], jnp.stack([m[1] for m in memory_terms])[:, None], 0.0)
+    gain_all = jnp.stack(gain_sums, 0)
+    packed = jnp.concatenate(
+        [memory_all.reshape(-1), rate_all.reshape(-1), gain_all.reshape(-1)]
+    )
+    packed = lax.psum(packed, ("section", "seq", "shard"))
+    cut = memory_all.size
+    memory_all = packed[:cut].reshape(2, 2, -1, D)
+    rate_all = packed[cut : cut + 2 * width].reshape(2, width)
+    gain_all = packed[cut + 2 * width :].reshape(2, D, 2)
+    own = lax.dynamic_index_in_dim
+    grad_persist = lax.dynamic_slice_in_dim(
+        own(memory_all, x, 0), s * 2 * HD, 2 * HD, 3
+    )
+    grad_rate = lax.dynamic_slice_in_dim(own(rate_all, x, 0), 2 * s, 2, 1)
+    grad_gain = lax.dynamic_slice_in_dim(own(gain_all, x, 0), z * depth, depth, 1)
+    return (
+        section_out,
+        section_grad,
+        grad_mix,
+        grad_out,
+        grad_gu,
+        grad_down,
+        grad_gain,
+        grad_persist,
+        grad_rate,
+    )
+
+
 def solution(mesh):
+    sizes = mesh.shape
+    planar = (sizes["section"], sizes["seq"]) == (2, 4)
     placed = (
         P(None, "shard", "seq", None),
         P(None, "shard", None),
@@ -420,7 +927,7 @@
         P("section", "seq"),
     )
     return jax.shard_map(
-        on_device,
+        tensor_parallel if planar else on_device,
         mesh=mesh,
         in_specs=placed,
         out_specs=(

time: 1500 us -> 790 us (0.53)
  waiting for transfers between devices: 981 us -> 217 us
  Pallas kernels: 0 us -> 244 us
  matrix products: 266 us -> 106 us
  starting transfers between devices: 56.4 us -> 9.27 us
  local copies, waits for them, and re-layouts: 49.9 us -> 82 us
    all_gather x4 -> x10, waiting for transfers between devices: 443 us -> 31.2 us  [the longest x4 31.2 us: collect(): return lax.all_gather(both, 'seq', axis=0).astype(F32)]
    pallas_call x0 -> x9, Pallas kernels: none -> 244 us  [plane_call(): pl.pallas_call(kernel, out_shape=list(outs.values()), in_specs=[vmem] * l...]
    reduce_scatter x4 -> x8, waiting for transfers between devices: 346 us -> 138 us  [tensor_parallel(): lax.psum_scatter(part.astype(BF), 'shard', scatter_dimension=0, tiled=True)]
    dot_general x42 -> x24, matrix products: 213 us -> 61.6 us  [the longest x2 9.13 us: tensor_parallel(): jnp.dot(normed_two.reshape(flat, D), gu_w[layer], preferred_element_type=...]
    psum x1, waiting for transfers between devices: 115 us -> 0.01 us  [tensor_parallel(): packed = lax.psum(packed, ('section', 'seq', 'shard'))]
    all_to_all x9 -> x0, waiting for transfers between devices: 54.4 us -> none  [the longest x2 19.3 us: layer_forward(): lax.all_to_all(qkv, 'seq', split_axis=2, concat_axis=0, tiled=True)]
    all_gather x1 -> x3, blocking collectives: 9.15 us -> 58.9 us  [the longest x2 43.6 us: tensor_parallel(): lax.all_gather(part[layer], 'shard', axis=0, tiled=True)]
    all_to_all x9 -> x0, starting transfers between devices: 45.7 us -> none  [the longest x3 17.1 us: layer_backward(): lax.all_to_all(outgoing, 'seq', split_axis=2, concat_axis=0, tiled=True)]
  transfers between devices with their start and end apart: 23 -> 30, of which waited for: 20 -> 16; matrix products, arithmetic and copies ran while one was open for 12% -> 21% of each run, Pallas kernels for 0% -> 20%
where the time goes in v1:
time: 790 us; the launch traced here: 782 us
  Pallas kernels  244 us (31%)
  waiting for transfers between devices  217 us (27%)
  matrix products  106 us (13%)
  local copies, waits for them, and re-layouts  82 us (10%)
  blocking collectives  58.9 us (7%)
  other arithmetic  42.7 us (5%)
  between operations  23.4 us (3%)
  starting transfers between devices  9.27 us (1%)
    pallas_call x9, Pallas kernels, plane_call(): pl.pallas_call(kernel, out_shape=list(outs.values()), in_specs=[vmem] * l...  244 us
    reduce_scatter x8, waiting for transfers between devices, tensor_parallel(): lax.psum_scatter(part.astype(BF), 'shard', scatter_dimension=0, tiled=True)  138 us
    all_gather x2, blocking collectives, tensor_parallel(): lax.all_gather(part[layer], 'shard', axis=0, tiled=True)  43.6 us
    unnamed x329, local copies, waits for them, and re-layouts  38.3 us
    all_gather x4, waiting for transfers between devices, collect(): return lax.all_gather(both, 'seq', axis=0).astype(F32)  31.2 us
    ppermute x6, waiting for transfers between devices, to_section(): lax.ppermute(jnp.where(first, of_layer[1], of_layer[0]), 'section', swap)  30.1 us
    reshape x3, local copies, waits for them, and re-layouts, tensor_parallel(): grad_mix = mix_all.transpose(2, 3, 1, 0, 4).reshape(1, depth, 4 * D)  17.3 us
  transfers between devices with their start and end apart: 30, of which 16 were waited for; matrix products, arithmetic and copies ran while one was open for 21% of the time, Pallas kernels for 20%

profile of v1, /device:TPU:3, one launch (start us, length us, event | category | flops | bytes accessed | tf_op | source)
XLA Modules:
  0.0 782.4 jit_solution(3989664536394374931)
XLA Ops:
  18.9 7.8 collective-permute-done
  32.2 7.5 collective-permute-done.2
  46.2 15.3 %all-gather = bf16[1,2048,2]{1,2,0:T(2,128)(2,1)S(1)} all-gather(bf16[1,256,2]{1,2,0:T(2,128)(2,1)S(1)} %copy-done.116), channel_id=2, replica_groups=mesh['section'=2,'seq'=4,'shard'=4] {'section','shard'}, dimensions={1}, use_global_device_ids=true | all-gather | bytes 9216 | tf_op jit(solution)/shard_map/all_gather | solution.py:693
  62.5 21.9 %shard_map.209 = bf16[2,512,1024]{2,1,0:T(8,128)(2,1)S(1)} custom-call(f32[2,64,1024]{2,1,0:T(8,128)S(1)} %bitcast_convert_fusion.1.rows_ref, f32[1,1024]{1,0:T(1,128)S(1)} %get-tuple-element.312.gain_ref), custom_call_target="tpu_custom_call" | custom-call | tf_op jit(solution)/shard_map/pallas_call | solution.py:628
  89.0 26.7 %all_gather.64 = bf16[352,1024]{1,0:T(8,128)(2,1)} all-gather(bf16[88,1024]{1,0:T(8,128)(2,1)S(1)} %get-tuple-element.278), channel_id=1, replica_groups=mesh['section'=2,'seq'=4,'shard'=4] {'shard'}, dimensions={0}, use_global_device_ids=true | all-gather | bytes 901120 | tf_op jit(solution)/shard_map/all_gather | solution.py:683
  115.7 16.9 %all_gather.67 = bf16[352,1024]{1,0:T(8,128)(2,1)} all-gather(bf16[88,1024]{1,0:T(8,128)(2,1)S(1)} %get-tuple-element.277), channel_id=1, replica_groups=mesh['section'=2,'seq'=4,'shard'=4] {'shard'}, dimensions={0}, use_global_device_ids=true | all-gather | bytes 901120 | tf_op jit(solution)/shard_map/all_gather | solution.py:683
  156.0 31.8 %shard_map.210 = (f32[2,64,1024]{2,1,0:T(8,128)S(1)}, bf16[2,512,1024]{2,1,0:T(8,128)(2,1)S(1)}) custom-call(bf16[2,512,1024]{2,1,0:T(8,128)(2,1)S(1)} %bitcast.398, f32[2,64,1024]{2,1,0:T(8,128)S(1)} %bitcast_convert_fusion.1.rows_ref, f32[1,1024]{1,0:T(1,128)S(1)} %get-tuple-element.311.gain_ref), custom_call_target="tpu_custom_call" | custom-call | tf_op jit(solution)/shard_map/pallas_call | solution.py:628
  195.8 39.2 %shard_map.211 = (bf16[2,64,1024]{2,1,0:T(8,128)(2,1)S(1)}, bf16[2,512,1024]{2,1,0:T(8,128)(2,1)S(1)}) custom-call(bf16[2,512,1024]{2,1,0:T(8,128)(2,1)S(1)} %bitcast.405, f32[2,64,1024]{2,1,0:T(8,128)S(1)} %get-tuple-element.187.rows_ref, f32[1,1024]{1,0:T(1,128)S(1)} %get-tuple-element.310.gain_ref), custom_call_target="tpu_custom_call" | custom-call | tf_op jit(solution)/shard_map/pallas_call | solution.py:628
  264.8 28.8 %shard_map.212 = (f32[2,64,1024]{2,1,0:T(8,128)S(1)}, bf16[2,512,1024]{2,1,0:T(8,128)(2,1)S(1)}) custom-call(bf16[2,512,1024]{2,1,0:T(8,128)(2,1)S(1)} %bitcast.397, f32[2,64,1024]{2,1,0:T(8,128)S(1)} %convert_element_type.285.rows_ref, f32[1,1024]{1,0:T(1,128)S(1)} %get-tuple-element.309.gain_ref), custom_call_target="tpu_custom_call" | custom-call | tf_op jit(solution)/shard_map/pallas_call | solution.py:628
  307.0 29.7 %shard_map.214 = (f32[2,64,1024]{2,1,0:T(8,128)S(1)}, f32[1,1024]{1,0:T(1,128)S(1)}, bf16[2,512,1024]{2,1,0:T(8,128)(2,1)S(1)}) custom-call(bf16[2,512,1024]{2,1,0:T(8,128)(2,1)S(1)} %bitcast.407, f32[2,64,1024]{2,1,0:T(8,128)S(1)} %get-tuple-element.191.rows_ref, f32[1,1024]{1,0:T(1,128)S(1)} %get-tuple-element.309.gain_ref, f32[2,64,1024]{2,1,0:T(8,128)S(1)} %copy-done.7), custom_call_target="tpu_custom_call" | custom-call | tf_op jit(solution)/shard_map/pallas_call | solution.py:628
  354.4 28.9 %shard_map.215 = (bf16[2,64,1024]{2,1,0:T(8,128)(2,1)S(1)}, f32[1,1024]{1,0:T(1,128)S(1)}, bf16[2,512,1024]{2,1,0:T(8,128)(2,1)S(1)}) custom-call(bf16[2,512,1024]{2,1,0:T(8,128)(2,1)S(1)} %bitcast.409, f32[2,64,1024]{2,1,0:T(8,128)S(1)} %convert_element_type.285.rows_ref, f32[1,1024]{1,0:T(1,128)S(1)} %get-tuple-element.310.gain_ref, ...), custom_call_target="tpu_custom_call" | custom-call | tf_op jit(solution)/shard_map/pallas_call | solution.py:628
  387.3 29.7 %shard_map.216 = (f32[2,64,1024]{2,1,0:T(8,128)S(1)}, f32[1,1024]{1,0:T(1,128)S(1)}, bf16[2,512,1024]{2,1,0:T(8,128)(2,1)S(1)}) custom-call(bf16[2,512,1024]{2,1,0:T(8,128)(2,1)S(1)} %bitcast.408, f32[2,64,1024]{2,1,0:T(8,128)S(1)} %get-tuple-element.187.rows_ref, f32[1,1024]{1,0:T(1,128)S(1)} %get-tuple-element.311.gain_ref, ...), custom_call_target="tpu_custom_call" | custom-call | tf_op jit(solution)/shard_map/pallas_call | solution.py:628
  476.7 16.1 %shard_map.217 = (f32[2,64,1024]{2,1,0:T(8,128)S(1)}, f32[1,1024]{1,0:T(1,128)S(1)}) custom-call(bf16[2,512,1024]{2,1,0:T(8,128)(2,1)S(1)} %bitcast.406, f32[2,64,1024]{2,1,0:T(8,128)S(1)} %bitcast_convert_fusion.1.rows_ref, f32[1,1024]{1,0:T(1,128)S(1)} %get-tuple-element.312.gain_ref, f32[2,64,1024]{2,1,0:T(8,128)S(1)} %copy-done.11), custom_call_target="tpu_custom_call" | custom-call | tf_op jit(solution)/shard_map/pallas_call | solution.py:628
  504.0 29.4 %reduce-scatter.9.cloned.1.call-done = bf16[256,512]{1,0:T(8,128)(2,1)} async-done(((bf16[1024,512]{1,0:T(8,128)(2,1)}), bf16[256,512]{1,0:T(8,128)(2,1)}) %reduce-scatter.9.cloned.1.call-update) | async-done | bytes 262160 | tf_op jit(solution)/shard_map/reduce_scatter | solution.py:853
  534.6 6.6 collective-permute-done.6
  543.2 18.5 %reduce-scatter.15.cloned.1.call-done = bf16[128,1024]{1,0:T(8,128)(2,1)} async-done(((bf16[512,1024]{1,0:T(8,128)(2,1)}), bf16[128,1024]{1,0:T(8,128)(2,1)}) %reduce-scatter.15.cloned.1.call-update) | async-done | bytes 262160 | tf_op jit(solution)/shard_map/reduce_scatter | solution.py:853
  561.6 29.2 %reduce-scatter.13.cloned.1.call-done = bf16[128,1024]{1,0:T(8,128)(2,1)} async-done(((bf16[512,1024]{1,0:T(8,128)(2,1)}), bf16[128,1024]{1,0:T(8,128)(2,1)}) %reduce-scatter.13.cloned.1.call-update) | async-done | bytes 262160 | tf_op jit(solution)/shard_map/reduce_scatter | solution.py:853
  592.1 6.7 collective-permute-done.7
  600.8 24.7 %reduce-scatter.19.cloned.1.call-done = bf16[256,704]{0,1:T(8,128)(2,1)} async-done(((bf16[1024,704]{0,1:T(8,128)(2,1)}), bf16[256,704]{0,1:T(8,128)(2,1)}) %reduce-scatter.19.cloned.1.call-update) | async-done | bytes 360464 | tf_op jit(solution)/shard_map/reduce_scatter | solution.py:853
  625.4 35.5 %reduce-scatter.17.cloned.1.call-done = bf16[256,704]{0,1:T(8,128)(2,1)} async-done(((bf16[1024,704]{0,1:T(8,128)(2,1)}), bf16[256,704]{0,1:T(8,128)(2,1)}) %reduce-scatter.17.cloned.1.call-update) | async-done | bytes 360464 | tf_op jit(solution)/shard_map/reduce_scatter | solution.py:853
  662.4 8.6 %collective-permute-done.8 = bf16[256,704]{0,1:T(8,128)(2,1)S(1)} collective-permute-done((bf16[256,704]{0,1:T(8,128)(2,1)S(1)}, bf16[256,704]{0,1:T(8,128)(2,1)S(1)}, u32[]{:S(2)}, u32[]{:S(2)}) %collective-permute-start.8) | collective-permute-done | bytes 360480 | tf_op jit(solution)/shard_map/ppermute | solution.py:859
  674.4 17.7 %shard_map.213 = bf16[2,64,1024]{2,1,0:T(8,128)(2,1)S(1)} custom-call(bf16[2,512,1024]{2,1,0:T(8,128)(2,1)S(1)} %bitcast.410, f32[2,64,1024]{2,1,0:T(8,128)S(1)} %copy-done.9, f32[1,1024]{1,0:T(1,128)S(1)} %get-tuple-element.310.gain_ref), custom_call_target="tpu_custom_call" | custom-call | tf_op jit(solution)/shard_map/pallas_call | solution.py:628
  716.6 7.1 copy.217
  736.2 26.4 %all-gather.34.cloned.1.call-done = bf16[8,256,704]{1,2,0:T(8,128)(2,1)} async-done(((bf16[2,256,704]{1,2,0:T(8,128)(2,1)}), bf16[8,256,704]{1,2,0:T(8,128)(2,1)}) %all-gather.34.cloned.1.call-update) | async-done | bytes 2883600 | tf_op jit(solution)/shard_map/all_gather | solution.py:870
  (604 shorter events, 248.4 us)
Async XLA Ops:
  8.0 76.4 %all-reduce.6.cloned.1.call-start = ((), (), s32[]{:S(2)}) async-start(), calls=%async_computation.27 | async-start | bytes 532480
  12.4 120.1 %all-gather.20.cloned.1.call-start = ((), (), s32[]{:S(2)}) async-start(), calls=%async_computation.9 | async-start | bytes 1310720 | tf_op jit(solution)/shard_map/all_gather | solution.py:676
  13.3 121.6 %all-gather.18.cloned.1.call-start = ((), (), s32[]{:S(2)}) async-start(), calls=%async_computation.8 | async-start | bytes 1310720 | tf_op jit(solution)/shard_map/all_gather | solution.py:683
  27.5 161.7 %all-gather.22.cloned.1.call-start = ((), (), s32[]{:S(2)}) async-start(), calls=%async_computation.10 | async-start | bytes 1802240 | tf_op jit(solution)/shard_map/all_gather | solution.py:683
  40.7 195.7 %all-gather.24.cloned.1.call-start = ((), (), s32[]{:S(2)}) async-start(), calls=%async_computation.11 | async-start | bytes 1310720 | tf_op jit(solution)/shard_map/all_gather | solution.py:683
  41.4 253.6 %all-gather.26.cloned.1.call-start = ((), (), s32[]{:S(2)}) async-start(), calls=%async_computation.12 | async-start | bytes 1802240 | tf_op jit(solution)/shard_map/all_gather | solution.py:683
  42.2 258.3 %all-gather.28.cloned.1.call-start = ((), (), s32[]{:S(2)}) async-start(), calls=%async_computation.22 | async-start | bytes 2621440 | tf_op jit(solution)/shard_map/all_gather | solution.py:704
  43.8 44.2 %collective-permute-start.3 = (bf16[88,1024]{1,0:T(8,128)(2,1)}, bf16[88,1024]{1,0:T(8,128)(2,1)}, u32[]{:S(2)}, u32[]{:S(2)}) collective-permute-start(bf16[88,1024]{1,0:T(8,128)(2,1)} %dynamic-slice_bitcast_fusion.1), channel_id=1, source_target_pairs={{0,16},{16,0},{1,17},{17,1},{2,18},{18,2},{3,19},{19,3},{4,20},{20... | collective-permute-start | bytes 540680 | tf_op jit(solution)/shard_map/ppermute | solution.py:672
  46.1 448.9 %reduce-scatter.23.cloned.1.call-start = ((), (), s32[]{:S(2)}) async-start(), calls=%async_computation.20 | async-start | bytes 901120 | tf_op jit(solution)/shard_map/reduce_scatter | solution.py:853
  134.2 19.8 %collective-permute-start.1 = (bf16[128,1024]{1,0:T(8,128)(2,1)}, bf16[128,1024]{1,0:T(8,128)(2,1)S(1)}, u32[]{:S(2)}, u32[]{:S(2)}) collective-permute-start(bf16[128,1024]{1,0:T(8,128)(2,1)} %dynamic-slice_bitcast_fusion), channel_id=1, source_target_pairs={{0,16},{16,0},{1,17},{17,1},{2,18},{18,2},{3,19},{19,3},{4,20},{20... | collective-permute-start | bytes 786440 | tf_op jit(solution)/shard_map/ppermute | solution.py:678
  429.0 66.1 %reduce-scatter.21.cloned.1.call-start = ((), (), s32[]{:S(2)}) async-start(), calls=%async_computation.19 | async-start | bytes 901120 | tf_op jit(solution)/shard_map/reduce_scatter | solution.py:853
  436.3 67.6 %reduce-scatter.11.cloned.1.call-start = ((), (), s32[]{:S(2)}) async-start(), calls=%async_computation.14 | async-start | bytes 1310720 | tf_op jit(solution)/shard_map/reduce_scatter | solution.py:853
  444.3 89.0 %reduce-scatter.9.cloned.1.call-start = ((), (), s32[]{:S(2)}) async-start(), calls=%async_computation.13 | async-start | bytes 1310720 | tf_op jit(solution)/shard_map/reduce_scatter | solution.py:853
  454.6 107.0 %reduce-scatter.15.cloned.1.call-start = ((), (), s32[]{:S(2)}) async-start(), calls=%async_computation.16 | async-start | bytes 1310720 | tf_op jit(solution)/shard_map/reduce_scatter | solution.py:853
  460.1 130.7 %reduce-scatter.13.cloned.1.call-start = ((), (), s32[]{:S(2)}) async-start(), calls=%async_computation.15 | async-start | bytes 1310720 | tf_op jit(solution)/shard_map/reduce_scatter | solution.py:853
  460.9 164.5 %reduce-scatter.19.cloned.1.call-start = ((), (), s32[]{:S(2)}) async-start(), calls=%async_computation.18 | async-start | bytes 1802240 | tf_op jit(solution)/shard_map/reduce_scatter | solution.py:853
  465.9 195.1 %reduce-scatter.17.cloned.1.call-start = ((), (), s32[]{:S(2)}) async-start(), calls=%async_computation.17 | async-start | bytes 1802240 | tf_op jit(solution)/shard_map/reduce_scatter | solution.py:853
  472.6 222.4 %all-reduce.4.cloned.1.call-start = ((), (), s32[]{:S(2)}) async-start(), calls=%async_computation.21 | async-start | bytes 565248 | tf_op jit(solution)/shard_map/psum | solution.py:890
  500.0 208.4 %all-gather.36.cloned.1.call-start = ((), (), s32[]{:S(2)}) async-start(), calls=%async_computation.26 | async-start | bytes 1802240 | tf_op jit(solution)/shard_map/all_gather | solution.py:870
  503.5 208.3 %all-gather.30.cloned.1.call-start = ((), (), s32[]{:S(2)}) async-start(), calls=%async_computation.23 | async-start | bytes 2621440 | tf_op jit(solution)/shard_map/all_gather | solution.py:870
  543.1 191.0 %all-gather.32.cloned.1.call-start = ((), (), s32[]{:S(2)}) async-start(), calls=%async_computation.24 | async-start | bytes 2621440 | tf_op jit(solution)/shard_map/all_gather | solution.py:870
  600.7 161.9 %all-gather.34.cloned.1.call-start = ((), (), s32[]{:S(2)}) async-start(), calls=%async_computation.25 | async-start | bytes 3604480 | tf_op jit(solution)/shard_map/all_gather | solution.py:870
  662.0 9.0 %collective-permute-start.8 = (bf16[256,704]{0,1:T(8,128)(2,1)S(1)}, bf16[256,704]{0,1:T(8,128)(2,1)S(1)}, u32[]{:S(2)}, u32[]{:S(2)}) collective-permute-start(bf16[256,704]{0,1:T(8,128)(2,1)S(1)} %broadcast_select_fusion), channel_id=1, source_target_pairs={{0,16},{16,0},{1,17},{17,1},{2,18},{18,2},{3,19},{19,3},{4,20},{20... | collective-permute-start | bytes 1081352 | tf_op jit(solution)/shard_map/ppermute | solution.py:859
  693.8 12.5 %collective-permute-start.5 = (bf16[2,64,1024]{2,1,0:T(8,128)(2,1)}, bf16[2,64,1024]{2,1,0:T(8,128)(2,1)}, u32[]{:S(2)}, u32[]{:S(2)}) collective-permute-start(bf16[2,64,1024]{2,1,0:T(8,128)(2,1)} %broadcast_select_fusion.6), channel_id=1, source_target_pairs={{0,16},{16,0},{1,17},{17,1},{2,18},{18,2},{3,19},{19,3},{4,20},{20... | collective-permute-start | bytes 786440 | tf_op jit(solution)/shard_map/ppermute | solution.py:859
  (162 other events, 1263.3 us)
Sparse Core Ops, SparseCore 0:
  12.5 54.3 all-reduce.5
  500.1 170.3 all-reduce.3
Sparse Core Ops, SparseCore 1:
  15.0 28.7 all-gather.19
  45.8 27.3 all-gather.17
  75.2 47.7 all-gather.21
  125.1 27.0 all-gather.23
  154.3 35.4 all-gather.25
  191.4 41.8 all-gather.27
  429.1 20.4 reduce-scatter.22
  451.7 21.9 reduce-scatter.20
  476.4 27.5 reduce-scatter.10
  507.0 26.3 reduce-scatter.8
  535.5 26.1 reduce-scatter.14
  564.6 26.1 reduce-scatter.12
  593.6 31.8 reduce-scatter.18
  628.3 32.6 reduce-scatter.16
  662.5 18.4 all-gather.35
  683.2 26.8 all-gather.29
  711.6 22.4 all-gather.31
  735.6 26.9 all-gather.33

commit v2 on v1

--- a/solution.py
+++ b/solution.py
@@ -528,14 +528,142 @@
         return total
 
 
-def meet():
+class ColumnSum:
+    def __init__(self, own, slots, out, send, recv, index):
+        self.place = here()
+        self.own, self.slots, self.out = own, slots, out
+        self.send, self.recv, self.index = send, recv, index
+
+    def copy(self, down, owner, source=None):
+        x, s, z = self.place
+        slot = owner if down else owner - 1
+        target = (x, s, (z + 3) % 4 if down else (z + 1) % 4)
+        landing = self.slots.at[down, slot]
+        return pltpu.make_async_remote_copy(
+            src_ref=landing if source is None else source,
+            dst_ref=landing,
+            send_sem=self.send.at[self.index, down, slot],
+            recv_sem=self.recv.at[self.index, down, slot],
+            device_id=target,
+            device_id_type=MESH,
+        )
+
+    def start(self):
+        z = self.place[2]
+        for down in (0, 1):
+
+            @pl.when(z == 3 * down)
+            def _():
+                for owner in (0, 1, 2) if down else (3, 2, 1):
+                    self.copy(down, owner, self.own.at[owner]).start()
+
+    def relay(self, down, owner, at):
+        @pl.when(self.place[2] == at)
+        def _():
+            self.copy(down, owner).wait_recv()
+            slot = owner if down else owner - 1
+            self.slots[down, slot] = (
+                self.slots[down, slot].astype(F32) + self.own[owner].astype(F32)
+            ).astype(BF)
+            self.copy(down, owner).start()
+
+    def hop(self, number):
+        if number == 1:
+            self.relay(0, 3, 1)
+            self.relay(1, 0, 2)
+        else:
+            self.relay(0, 2, 1)
+            self.relay(1, 1, 2)
+            self.relay(0, 3, 2)
+            self.relay(1, 0, 1)
+
+    def finish(self):
+        z = self.place[2]
+        for at in range(4):
+
+            @pl.when(z == at)
+            def _():
+                total = self.own[at].astype(F32)
+                if at > 0:
+                    self.copy(0, at).wait_recv()
+                    total = total + self.slots[0, at - 1].astype(F32)
+                if at < 3:
+                    self.copy(1, at).wait_recv()
+                    total = total + self.slots[1, at].astype(F32)
+                self.out[...] = total.astype(BF)
+                for owner in range(at + 1, 4):
+                    self.copy(0, owner).wait_send()
+                for owner in range(at):
+                    self.copy(1, owner).wait_send()
+
+
+class RootSum:
+    def __init__(self, own, slots, out, send, recv):
+        self.place = here()
+        x, s, _ = self.place
+        self.root = 2 * x + s // 2
+        self.own, self.slots, self.out = own, slots, out
+        self.send, self.recv = send, recv
+
+    def copy(self, down, source=None):
+        x, s, z = self.place
+        landing = self.slots.at[down]
+        return pltpu.make_async_remote_copy(
+            src_ref=landing if source is None else source,
+            dst_ref=landing,
+            send_sem=self.send.at[down],
+            recv_sem=self.recv.at[down],
+            device_id=(x, s, (z + 3) % 4 if down else (z + 1) % 4),
+            device_id_type=MESH,
+        )
+
+    def sends(self, down):
+        z = self.place[2]
+        return z > self.root if down else z < self.root
+
+    def start(self):
+        for down in (0, 1):
+
+            @pl.when((self.place[2] == 3 * down) & self.sends(down))
+            def _():
+                self.copy(down, self.own).start()
+
+    def relay(self, down, at):
+        @pl.when((self.place[2] == at) & self.sends(down))
+        def _():
+            self.copy(down).wait_recv()
+            self.slots[down] = (self.slots[down].astype(F32) + self.own[...].astype(F32)).astype(BF)
+            self.copy(down).start()
+
+    def hop(self, number):
+        self.relay(0, number)
+        self.relay(1, 3 - number)
+
+    def finish(self):
+        z = self.place[2]
+        self.out[...] = self.own[...]
+        for down in (0, 1):
+
+            @pl.when((z == self.root) & (z < 3 if down else z > 0))
+            def _():
+                self.copy(down).wait_recv()
+                self.out[...] = (self.out[...].astype(F32) + self.slots[down].astype(F32)).astype(BF)
+
+            @pl.when(self.sends(down))
+            def _():
+                self.copy(down).wait_send()
+
+
+def meet(column=False):
     place = here()
+    x, s, z = place
+    others = [peer(place, chip, chip == 0) for chip in range(4)]
+    if column:
+        others += [(x, s, (z + 1) % 4), (x, s, (z + 3) % 4)]
     barrier = pltpu.get_barrier_semaphore()
-    for chip in (0, 1, 2, 3):
-        pl.semaphore_signal(
-            barrier, inc=1, device_id=peer(place, chip, chip == 0), device_id_type=MESH
-        )
-    pl.semaphore_wait(barrier, 4)
+    for other in others:
+        pl.semaphore_signal(barrier, inc=1, device_id=other, device_id_type=MESH)
+    pl.semaphore_wait(barrier, len(others))
 
 
 def start_kernel(rows_ref, gain_ref, full_ref, gsend, grecv):
@@ -576,15 +704,30 @@
         gather.finish()
 
 
-def backward_kernel(last, part_ref, rows_ref, gain_ref, grad_ref, own_ref, gains_ref, *rest):
-    if last:
-        pair, away, near, ssend, srecv = rest
+def backward_kernel(last, rooted, *refs):
+    part_ref, rows_ref, gain_ref, grad_ref, *refs = refs
+    columns = 2
+    owns, refs = refs[:columns], refs[columns:]
+    own_ref, gains_ref, *refs = refs
+    if not last:
+        full_ref, *refs = refs
+    outs, refs = refs[:columns], refs[columns:]
+    pair, away, near, ssend, srecv, *refs = refs
+    if not last:
+        gsend, grecv, *refs = refs
+    slots, refs = refs[:columns], refs[columns:]
+    csend, crecv, *refs = refs
+    sums_of = [ColumnSum(owns[0], slots[0], outs[0], csend, crecv, 0)]
+    if rooted:
+        sums_of.append(RootSum(owns[1], slots[1], outs[1], *refs))
     else:
-        full_ref, pair, away, near, ssend, srecv, gsend, grecv = rest
-    meet()
+        sums_of.append(ColumnSum(owns[1], slots[1], outs[1], csend, crecv, 1))
+    meet(True)
     scatters = [Scatter(part_ref, b, pair, away, near, ssend, srecv) for b in range(2)]
     for scatter in scatters:
         scatter.start()
+    for column in sums_of:
+        column.start()
     for scatter in scatters:
         scatter.forward()
     gathers = []
@@ -602,16 +745,163 @@
             gather.start(own.astype(BF))
             gathers.append(gather)
     gains_ref[...] = sums
+    for column in sums_of:
+        column.hop(1)
     for gather in gathers:
         gather.forward()
+    for column in sums_of:
+        column.hop(2)
     for gather in gathers:
         gather.finish()
-
-
-def plane_call(kernel, number, operands, outs, scatter, gather):
+    for column in sums_of:
+        column.finish()
+
+
+def final_kernel(*refs):
+    place = here()
+    x, s, z = place
+    sibling, beside, partner = (peer(place, 0, True), peer(place, 2, False), peer(place, 1, False))
+    across = peer(place, 3, False)
+    by_layer = [refs[0:6], refs[6:12]]
+    small_ref = refs[12]
+    bufs = refs[13:16]
+    out_buf, rows_buf, grads_buf, plane_buf = refs[16:20]
+    column_buf, psend, precv, osend, orecv, rsend, rrecv, zsend, zrecv, ssend, srecv = refs[20:]
+
+    def copy(source, landing, sems, index, target):
+        return pltpu.make_async_remote_copy(
+            src_ref=source,
+            dst_ref=landing,
+            send_sem=sems[0].at[index],
+            recv_sem=sems[1].at[index],
+            device_id=target,
+            device_id_type=MESH,
+        )
+
+    flips = [(dx, ds) for dx in (0, 1) for ds in range(4) if dx or ds]
+    plane = [((x + dx) % 2, (s + ds) % 4, z) for dx, ds in flips]
+    column = [(x, s, (z + dz) % 4) for dz in (1, 2, 3)]
+    barrier = pltpu.get_barrier_semaphore()
+    for other in plane + column:
+        pl.semaphore_signal(barrier, inc=1, device_id=other, device_id_type=MESH)
+    pl.semaphore_wait(barrier, len(plane) + len(column))
+
+    def to_plane_of(dz):
+        target = (z + dz) % 4
+        return copy(
+            small_ref.at[target], column_buf.at[dz - 1], (zsend, zrecv), dz - 1, (x, s, target)
+        )
+
+    def to_plane(index):
+        slot = plane_buf.at[x * 4 + s]
+        return copy(slot, slot, (ssend, srecv), index, plane[index])
+
+    for dz in (1, 2, 3):
+        to_plane_of(dz).start()
+
+    psems = [(psend.at[i], precv.at[i]) for i in range(3)]
+
+    def piece(index, kind, slot, target, source=None):
+        landing = bufs[index].at[slot]
+        return copy(landing if source is None else source, landing, psems[index], kind, target)
+
+    mine = (x, s)
+    turned = (1 - x, s)
+    for layer in (0, 1):
+        own, theirs = by_layer[layer], by_layer[1 - layer]
+
+        @pl.when(x == layer)
+        def _():
+            for index in range(3):
+                piece(index, 2, mine, partner, theirs[index]).start()
+                piece(index, 0, mine, beside, own[index]).start()
+                piece(index, 1, mine, sibling, own[index]).start()
+            copy(theirs[4], rows_buf, (rsend, rrecv), 0, partner).start()
+            copy(theirs[5], grads_buf, (rsend, rrecv), 1, partner).start()
+            for index in range(3):
+                bufs[index][mine] = own[index][...]
+
+    total = small_ref[z]
+    for dz in (1, 2, 3):
+        to_plane_of(dz).wait_recv()
+        total = total + column_buf[dz - 1]
+    plane_buf[x * 4 + s] = total
+    for index in range(7):
+        to_plane(index).start()
+
+    core = s % 2
+    root = z == 2 * x + s // 2
+    of_root = (z // 2, 2 * (z % 2) + core)
+    apart = 2 * ((x + of_root[0]) % 2) + (s // 2 + of_root[1] // 2) % 2
+
+    def out_copy(index, target, source=None):
+        landing = out_buf.at[core]
+        return copy(landing if source is None else source, landing, (osend, orecv), index, target)
+
+    for layer in (0, 1):
+
+        @pl.when(root & (x == layer))
+        def _():
+            out_copy(1, beside, by_layer[layer][3]).start()
+            out_copy(2, partner, by_layer[1 - layer][3]).start()
+            out_copy(3, across, by_layer[1 - layer][3]).start()
+            out_buf[core] = by_layer[layer][3][...]
+
+    for apart_by in (1, 2, 3):
+
+        @pl.when(apart == apart_by)
+        def _():
+            out_copy(apart_by, beside).wait_recv()
+
+    out_copy(0, sibling).start()
+
+    for index in range(3):
+        piece(index, 2, turned, partner).wait_recv()
+        piece(index, 3, turned, beside).start()
+        piece(index, 4, turned, sibling).start()
+    far = (x, (s + 2) % 4)
+    far_turned = (1 - x, (s + 2) % 4)
+    for index in range(3):
+        piece(index, 0, far, beside).wait_recv()
+        piece(index, 5, far, sibling).start()
+    for index in range(3):
+        piece(index, 3, far_turned, beside).wait_recv()
+        piece(index, 6, far_turned, sibling).start()
+    twin = sibling[1]
+    far_twin = (twin + 2) % 4
+    for index in range(3):
+        piece(index, 1, (x, twin), sibling).wait_recv()
+        piece(index, 4, (1 - x, twin), sibling).wait_recv()
+        piece(index, 5, (x, far_twin), sibling).wait_recv()
+        piece(index, 6, (1 - x, far_twin), sibling).wait_recv()
+    other_out = out_buf.at[1 - core]
+    copy(other_out, other_out, (osend, orecv), 0, sibling).wait_recv()
+    for index in range(7):
+        dx, ds = flips[index]
+        slot = plane_buf.at[((x + dx) % 2) * 4 + (s + 4 - ds) % 4]
+        copy(slot, slot, (ssend, srecv), index, plane[index]).wait_recv()
+    for index in (0, 1):
+        copy(rows_buf, rows_buf, (rsend, rrecv), index, partner).wait()
+    for index in range(7):
+        to_plane(index).wait_send()
+    for dz in (1, 2, 3):
+        to_plane_of(dz).wait_send()
+    for index in range(3):
+        for kind in range(7):
+            piece(index, kind, mine, sibling).wait_send()
+    out_copy(0, sibling).wait_send()
+
+    @pl.when(root)
+    def _():
+        for index in (1, 2, 3):
+            out_copy(index, sibling).wait_send()
+
+
+def plane_call(kernel, number, operands, outs, scatter, gather, sums=(), root=None):
     _, length, width = outs["full"].shape
     size = length // 8
     scratch = []
+    outs = dict(outs)
     if scatter:
         scratch += [
             pltpu.VMEM((2, 4, size, width), BF),
@@ -623,18 +913,101 @@
     if gather:
         scratch += [pltpu.SemaphoreType.DMA((2, 7)), pltpu.SemaphoreType.DMA((2, 7))]
     else:
-        outs = {name: out for name, out in outs.items() if name != "full"}
+        del outs["full"]
+    outs = list(outs.values())
+    for part in sums:
+        outs.append(jax.ShapeDtypeStruct(part.shape[1:], BF))
+        scratch.append(pltpu.VMEM((2, 3) + part.shape[1:], BF))
+    if root is not None:
+        outs.append(jax.ShapeDtypeStruct(root.shape, BF))
+        scratch.append(pltpu.VMEM((2,) + root.shape, BF))
+        sums = (*sums, root)
+    if sums:
+        scratch += [pltpu.SemaphoreType.DMA((2, 2, 3)), pltpu.SemaphoreType.DMA((2, 2, 3))]
+    if root is not None:
+        scratch += [pltpu.SemaphoreType.DMA((2,)), pltpu.SemaphoreType.DMA((2,))]
+    operands = (*operands, *sums)
     vmem = pl.BlockSpec(memory_space=pltpu.VMEM)
     return pl.pallas_call(
         kernel,
-        out_shape=list(outs.values()),
+        out_shape=outs,
         in_specs=[vmem] * len(operands),
         out_specs=[vmem] * len(outs),
         scratch_shapes=scratch,
         compiler_params=pltpu.CompilerParams(
-            collective_id=number, has_side_effects=True, vmem_limit_bytes=24 * 2**20
+            collective_id=number, has_side_effects=True, vmem_limit_bytes=40 * 2**20
         ),
     )(*operands)
+
+
+def final_call(number, by_layer, small):
+    operands = (*by_layer[0], *by_layer[1], small)
+    outs = [jax.ShapeDtypeStruct((2, 4) + part.shape, BF) for part in by_layer[0][:3]]
+    outs.append(jax.ShapeDtypeStruct((2,) + by_layer[0][3].shape, BF))
+    outs += [jax.ShapeDtypeStruct(part.shape, BF) for part in by_layer[0][4:]]
+    outs.append(jax.ShapeDtypeStruct((8,) + small.shape[1:], F32))
+    sizes = [(3, 7), (4,), (2,), (3,), (7,)]
+    scratch = [pltpu.VMEM((3,) + small.shape[1:], F32)]
+    scratch += [pltpu.SemaphoreType.DMA(size) for size in sizes for _ in range(2)]
+    vmem = pl.BlockSpec(memory_space=pltpu.VMEM)
+    return pl.pallas_call(
+        final_kernel,
+        out_shape=outs,
+        in_specs=[vmem] * len(operands),
+        out_specs=[vmem] * len(outs),
+        scratch_shapes=scratch,
+        compiler_params=pltpu.CompilerParams(
+            collective_id=number, has_side_effects=True, vmem_limit_bytes=40 * 2**20
+        ),
+    )(*operands)
+
+
+def assemble_kernel(mix_buf, gu_buf, down_buf, mix_ref, gu_ref, down_ref):
+    unit = down_buf.shape[2] // 2
+    half = gu_buf.shape[3] // 2
+    width = 4 * HD
+    for which in range(8):
+        slot = (which // 4, which % 4)
+        mix = mix_buf[slot].astype(F32)
+        for kind in range(4):
+            begin = kind * D + which * HD
+            mix_ref[0, :, begin : begin + HD] = mix[:, kind * HD : (kind + 1) * HD]
+        part = gu_buf[slot].astype(F32)
+        for side in range(2):
+            for owner in range(half // unit):
+                begin = side * FF + (owner * 8 + which) * unit
+                source = side * half + owner * unit
+                gu_ref[0, :, begin : begin + unit] = part[:, source : source + unit]
+    for pair in range(2):
+        down = down_buf[0, pair].astype(F32)
+        down_ref[0, pair * unit : (pair + 1) * unit, :width] = down[:unit]
+        down_ref[0, pair * unit : (pair + 1) * unit, width:] = down[unit:]
+
+
+def assemble_call(mix_buf, gu_buf, down_buf):
+    depth, unit = mix_buf.shape[2], down_buf.shape[2] // 2
+    rows = depth // 4
+    wide = gu_buf.shape[3] * 8
+    return pl.pallas_call(
+        assemble_kernel,
+        grid=(4,),
+        out_shape=[
+            jax.ShapeDtypeStruct((1, depth, 4 * D), F32),
+            jax.ShapeDtypeStruct((1, depth, wide), F32),
+            jax.ShapeDtypeStruct((1, 8 * unit, D), F32),
+        ],
+        in_specs=[
+            pl.BlockSpec((2, 4, rows, 4 * HD), lambda i: (0, 0, i, 0)),
+            pl.BlockSpec((2, 4, rows, wide // 8), lambda i: (0, 0, i, 0)),
+            pl.BlockSpec((1, 2, 2 * unit, D // 2), lambda i: (i // 2, i % 2, 0, 0)),
+        ],
+        out_specs=[
+            pl.BlockSpec((1, rows, 4 * D), lambda i: (0, i, 0)),
+            pl.BlockSpec((1, rows, wide), lambda i: (0, i, 0)),
+            pl.BlockSpec((1, 2 * unit, D), lambda i: (0, i, 0)),
+        ],
+        compiler_params=pltpu.CompilerParams(vmem_limit_bytes=40 * 2**20),
+    )(mix_buf, gu_buf, down_buf)
 
 
 def tensor_parallel(
@@ -794,13 +1167,19 @@
         grad_gu = jnp.einsum(
             "td,tf->df", normed_two.reshape(flat, D), grad_gate_up, preferred_element_type=F32
         )
-        grad_mid, gain_two, branch = plane_call(
-            functools.partial(backward_kernel, False),
+        halves_of_down = grad_down.astype(BF).reshape(nz, unit, 2, D // 2)
+        sent = (
+            grad_gu.astype(BF).reshape(nz, depth, 2 * nz * unit),
+            halves_of_down.transpose(0, 2, 1, 3).reshape(nz, 2 * unit, D // 2),
+        )
+        grad_mid, gain_two, branch, gu_sum, down_sum = plane_call(
+            functools.partial(backward_kernel, False, False),
             5 + 2 * (1 - layer),
             (partial.reshape(count, length, D), mid, gains[layer, :, :, 1], grad_own),
             {"own": own32, "sums": sums, "full": full},
             True,
             True,
+            sent,
         )
         branch = branch.reshape(flat, D)
         grad_combined = jnp.dot(branch, out_w[layer].T, preferred_element_type=F32)
@@ -835,69 +1214,52 @@
         )
         last = layer == 0
         found = plane_call(
-            functools.partial(backward_kernel, last),
+            functools.partial(backward_kernel, last, True),
             6 + 2 * (1 - layer),
             (partial.reshape(count, length, D), rows, gains[layer, :, :, 0], grad_mid),
-            {"own": own32 if last else own16, "sums": sums, "full": full},
+            {"own": own16, "sums": sums, "full": full},
             True,
             not last,
-        )
-        grads[layer] = found[0].astype(BF)
-        gain_sums[layer] = jnp.stack([found[1][0], gain_two[0]], 1)
+            (grad_mix.astype(BF).reshape(nz, depth, 4 * HD),),
+            grad_out.astype(BF),
+        )
+        grads[layer] = found[0]
+        gain_sums[layer] = jnp.concatenate([found[1], gain_two], 0)
         if not last:
             grad_own = found[0].astype(F32)
             grad_full = found[2]
-        owner = mine // 2 == jnp.arange(nz)
-        grad_out = jnp.where(owner[:, None, None], grad_out[None], 0.0)
-        pieces[layer] = [
-            lax.psum_scatter(part.astype(BF), "shard", scatter_dimension=0, tiled=True)
-            for part in (grad_mix, grad_gu, grad_down, grad_out.reshape(nz * HD, D))
-        ]
-
-    def to_section(of_layer):
-        own = jnp.where(first, of_layer[0], of_layer[1])
-        got = lax.ppermute(jnp.where(first, of_layer[1], of_layer[0]), "section", swap)
-        return layers(own, got)
-
-    def whole_rows(of_layer):
-        return jnp.concatenate(to_section(of_layer), 1)[None, :, None]
-
-    section_out = whole_rows(outputs)
-    section_grad = whole_rows(grads).astype(F32)
-
-    def collect(index):
-        both = jnp.stack(to_section([pieces[layer][index] for layer in range(2)]), 0)
-        return lax.all_gather(both, "seq", axis=0).astype(F32)
-
-    mix_all = collect(0).reshape(ns, nx, depth, 4, HD)
-    gu_all = collect(1).reshape(ns, nx, depth, 2, nz, unit)
-    down_all = collect(2)
-    out_all = collect(3)
-    grad_mix = mix_all.transpose(2, 3, 1, 0, 4).reshape(1, depth, 4 * D)
-    grad_gu = gu_all.transpose(2, 3, 4, 1, 0, 5).reshape(1, depth, 2 * FF)
-    grad_down = down_all.transpose(1, 0, 2, 3).reshape(1, unit * width, D)
-    out_all = lax.dynamic_index_in_dim(out_all, z // 2, 1, keepdims=False)
-    grad_out = lax.dynamic_slice_in_dim(out_all, 2 * lax.rem(z, 2), 2, 0).reshape(1, 2 * HD, D)
-
-    memory_all = jnp.stack([m[0] for m in memory_terms], 0)
-    places = jnp.arange(width) == mine
-    memory_all = jnp.where(places[None, None, None, :, None], memory_all[:, :, :, None, :], 0.0)
-    rate_all = jnp.where(places[None], jnp.stack([m[1] for m in memory_terms])[:, None], 0.0)
-    gain_all = jnp.stack(gain_sums, 0)
-    packed = jnp.concatenate(
-        [memory_all.reshape(-1), rate_all.reshape(-1), gain_all.reshape(-1)]
-    )
-    packed = lax.psum(packed, ("section", "seq", "shard"))
-    cut = memory_all.size
-    memory_all = packed[:cut].reshape(2, 2, -1, D)
-    rate_all = packed[cut : cut + 2 * width].reshape(2, width)
-    gain_all = packed[cut + 2 * width :].reshape(2, D, 2)
-    own = lax.dynamic_index_in_dim
-    grad_persist = lax.dynamic_slice_in_dim(
-        own(memory_all, x, 0), s * 2 * HD, 2 * HD, 3
-    )
-    grad_rate = lax.dynamic_slice_in_dim(own(rate_all, x, 0), 2 * s, 2, 1)
-    grad_gain = lax.dynamic_slice_in_dim(own(gain_all, x, 0), z * depth, depth, 1)
+        pieces[layer] = (found[-2], gu_sum, down_sum, found[-1])
+
+    memory_all = jnp.stack([m[0] for m in memory_terms], 0).reshape(-1, HD)
+    rate_all = jnp.pad(jnp.stack([m[1] for m in memory_terms])[None], ((0, 7), (0, HD - 2)))
+    gain_all = jnp.stack(gain_sums, 0).reshape(4, nz, 2, HD).transpose(1, 0, 2, 3)
+    memory_all = jnp.concatenate([memory_all, rate_all], 0)
+    small = jnp.concatenate(
+        [jnp.broadcast_to(memory_all[None], (nz,) + memory_all.shape), gain_all.reshape(nz, 8, HD)],
+        1,
+    )
+    by_layer = [(*pieces[layer], outputs[layer], grads[layer]) for layer in range(2)]
+    mix_all, gu_all, down_all, out_all, rows_got, grads_got, plane_all = final_call(
+        9, by_layer, small
+    )
+
+    def whole_rows(of_layer, got):
+        both = layers(jnp.where(first, of_layer[0], of_layer[1]), got)
+        return jnp.concatenate(both, 1)[None, :, None]
+
+    section_out = whole_rows(outputs, rows_got)
+    section_grad = whole_rows(grads, grads_got).astype(F32)
+    grad_mix, grad_gu, grad_down = assemble_call(mix_all, gu_all, down_all)
+    grad_out = out_all.astype(F32).reshape(1, 2 * HD, D)
+
+    heads_of = lax.dynamic_slice_in_dim(plane_all, 2 * s, 2, 0)
+    of_layer = lax.dynamic_index_in_dim(
+        heads_of[:, :64].reshape(2, 2, 2, -1, HD), x, 1, keepdims=False
+    )
+    grad_persist = of_layer.transpose(1, 2, 0, 3).reshape(1, 2, -1, 2 * HD)
+    grad_rate = lax.dynamic_index_in_dim(heads_of[:, 64], x, 1, keepdims=False)[None]
+    gain_all = jnp.sum(plane_all[:, 72:], 0).reshape(2, 2, depth)
+    grad_gain = lax.dynamic_index_in_dim(gain_all, x, 0).transpose(0, 2, 1)
     return (
         section_out,
         section_grad,

time: 790 us -> 686 us (0.87)
  waiting for transfers between devices: 217 us -> 18.7 us
  Pallas kernels: 244 us -> 390 us
  other arithmetic: 42.7 us -> 17.9 us
  local copies, waits for them, and re-layouts: 82 us -> 65.3 us
  starting transfers between devices: 9.27 us -> 0.66 us
    pallas_call x9 -> x11, Pallas kernels: 244 us -> 390 us  [the longest x9 316 us: plane_call(): pl.pallas_call(kernel, out_shape=outs, in_specs=[vmem] * len(operands), o...]
    reduce_scatter x8 -> x0, waiting for transfers between devices: 138 us -> none  [tensor_parallel(): lax.psum_scatter(part.astype(BF), 'shard', scatter_dimension=0, tiled=True)]
    all_gather x4 -> x0, waiting for transfers between devices: 31.2 us -> none  [collect(): return lax.all_gather(both, 'seq', axis=0).astype(F32)]
    ppermute x6 -> x0, waiting for transfers between devices: 30.1 us -> none  [to_section(): lax.ppermute(jnp.where(first, of_layer[1], of_layer[0]), 'section', swap)]
    reshape x9 -> x8, local copies, waits for them, and re-layouts: 23.8 us -> 5.75 us  [the longest x4 5.06 us: tensor_parallel(): halves_of_down = grad_down.astype(BF).reshape(nz, unit, 2, D // 2)]
    unnamed x329 -> x326, local copies, waits for them, and re-layouts: 38.3 us -> 41.5 us
  transfers between devices with their start and end apart: 30 -> 11, of which waited for: 16 -> 2; matrix products, arithmetic and copies ran while one was open for 21% -> 9% of each run, Pallas kernels for 20% -> 17%
where the time goes in v2:
time: 686 us; the launch traced here: 681 us
  Pallas kernels  390 us (57%)
  matrix products  101 us (15%)
  local copies, waits for them, and re-layouts  65.3 us (10%)
  blocking collectives  64.4 us (9%)
  between operations  22.9 us (3%)
  waiting for transfers between devices  18.7 us (3%)
  other arithmetic  17.9 us (3%)
    pallas_call x9, Pallas kernels, plane_call(): pl.pallas_call(kernel, out_shape=outs, in_specs=[vmem] * len(operands), o...  316 us
    pallas_call x1, Pallas kernels, final_call(): pl.pallas_call(final_kernel, out_shape=outs, in_specs=[vmem] * len(operan...  68.7 us
    all_gather x2, blocking collectives, tensor_parallel(): lax.all_gather(part[layer], 'shard', axis=0, tiled=True)  47 us
    unnamed x326, local copies, waits for them, and re-layouts  41.5 us
    all_gather x1, blocking collectives, tensor_parallel(): lax.all_gather(norm_gains[0], ('section', 'shard'), axis=0, tiled=True)  17.4 us
    ppermute x3, waiting for transfers between devices, tensor_parallel(): lax.ppermute(g, 'section', swap)  17.2 us
  transfers between devices with their start and end apart: 11, of which 2 were waited for; matrix products, arithmetic and copies ran while one was open for 9% of the time, Pallas kernels for 17%

profile of v2, /device:TPU:3, one launch (start us, length us, event | category | flops | bytes accessed | tf_op | source)
XLA Modules:
  0.0 680.9 jit_solution(2139262430498669538)
XLA Ops:
  16.7 8.1 %collective-permute-done = bf16[256,512]{0,1:T(8,128)(2,1)S(1)} collective-permute-done((bf16[256,512]{0,1:T(8,128)(2,1)S(1)}, bf16[256,512]{0,1:T(8,128)(2,1)S(1)}, u32[]{:S(2)}, u32[]{:S(2)}) %collective-permute-start) | collective-permute-done | bytes 262176 | tf_op jit(solution)/shard_map/ppermute | solution.py:1045
  29.1 9.1 %collective-permute-done.2 = bf16[256,704]{0,1:T(8,128)(2,1)S(1)} collective-permute-done((bf16[256,704]{0,1:T(8,128)(2,1)S(1)}, bf16[256,704]{0,1:T(8,128)(2,1)S(1)}, u32[]{:S(2)}, u32[]{:S(2)}) %collective-permute-start.2) | collective-permute-done | bytes 360480 | tf_op jit(solution)/shard_map/ppermute | solution.py:1045
  41.9 17.4 %all-gather = bf16[1,2048,2]{1,2,0:T(2,128)(2,1)S(1)} all-gather(bf16[1,256,2]{1,2,0:T(2,128)(2,1)S(1)} %copy-done.140), channel_id=2, replica_groups=mesh['section'=2,'seq'=4,'shard'=4] {'section','shard'}, dimensions={1}, use_global_device_ids=true | all-gather | bytes 9216 | tf_op jit(solution)/shard_map/all_gather | solution.py:1066
  60.9 21.6 %shard_map.209 = bf16[2,512,1024]{2,1,0:T(8,128)(2,1)S(1)} custom-call(f32[2,64,1024]{2,1,0:T(8,128)S(1)} %bitcast_convert_fusion.2.rows_ref.refs_1_, f32[1,1024]{1,0:T(1,128)S(1)} %get-tuple-element.331.gain_ref.refs_2_), custom_call_target="tpu_custom_call" | custom-call | tf_op jit(solution)/shard_map/pallas_call | solution.py:931
  87.0 26.3 %all_gather.40 = bf16[352,1024]{1,0:T(8,128)(2,1)} all-gather(bf16[88,1024]{1,0:T(8,128)(2,1)S(1)} %get-tuple-element.304), channel_id=1, replica_groups=mesh['section'=2,'seq'=4,'shard'=4] {'shard'}, dimensions={0}, use_global_device_ids=true | all-gather | bytes 901120 | tf_op jit(solution)/shard_map/all_gather | solution.py:1056
  113.3 20.7 %all_gather.43 = bf16[352,1024]{1,0:T(8,128)(2,1)} all-gather(bf16[88,1024]{1,0:T(8,128)(2,1)S(1)} %get-tuple-element.305), channel_id=1, replica_groups=mesh['section'=2,'seq'=4,'shard'=4] {'shard'}, dimensions={0}, use_global_device_ids=true | all-gather | bytes 901120 | tf_op jit(solution)/shard_map/all_gather | solution.py:1056
  155.4 30.5 %shard_map.210 = (f32[2,64,1024]{2,1,0:T(8,128)S(1)}, bf16[2,512,1024]{2,1,0:T(8,128)(2,1)S(1)}) custom-call(bf16[2,512,1024]{2,1,0:T(8,128)(2,1)S(1)} %bitcast.376, f32[2,64,1024]{2,1,0:T(8,128)S(1)} %bitcast_convert_fusion.2.rows_ref.refs_1_, f32[1,1024]{1,0:T(1,128)S(1)} %get-tuple-element.330.gain_ref.refs_2_), custom_call_target="tpu_custom_call" | custom-call | tf_op jit(solution)/shard_map/pallas_call | solution.py:931
  186.0 4.0 fusion.217
  193.0 36.7 %shard_map.211 = (bf16[2,64,1024]{2,1,0:T(8,128)(2,1)S(1)}, bf16[2,512,1024]{2,1,0:T(8,128)(2,1)S(1)}) custom-call(bf16[2,512,1024]{2,1,0:T(8,128)(2,1)S(1)} %bitcast.389, f32[2,64,1024]{2,1,0:T(8,128)S(1)} %get-tuple-element.205.rows_ref.refs_1_, f32[1,1024]{1,0:T(1,128)S(1)} %get-tuple-element.329.gain_ref.refs_2_), custom_call_target="tpu_custom_call" | custom-call | tf_op jit(solution)/shard_map/pallas_call | solution.py:931
  252.0 30.1 %shard_map.212 = (f32[2,64,1024]{2,1,0:T(8,128)S(1)}, bf16[2,512,1024]{2,1,0:T(8,128)(2,1)S(1)}) custom-call(bf16[2,512,1024]{2,1,0:T(8,128)(2,1)S(1)} %bitcast.375, f32[2,64,1024]{2,1,0:T(8,128)S(1)} %convert_element_type.279.rows_ref.refs_1_, f32[1,1024]{1,0:T(1,128)S(1)} %get-tuple-element.328.gain_ref.refs_2_), custom_call_target="tpu_custom_call" | custom-call | tf_op jit(solution)/shard_map/pallas_call | solution.py:931
  284.3 5.3 fusion.219
  289.6 4.8 multiply_convert_fusion.3
  300.1 3.6 convolution_convert_fusion.13
  303.7 3.3 reshape.559
  308.2 3.7 convolution_convert_fusion.7
  312.0 45.9 %shard_map.214 = (f32[2,64,1024]{2,1,0:T(8,128)S(1)}, f32[1,1024]{1,0:T(1,128)S(1)}, bf16[2,512,1024]{2,1,0:T(8,128)(2,1)S(1)}, bf16[256,704]{1,0:T(8,128)(2,1)S(1)}, bf16[176,512]{1,0:T(8,128)(2,1)S(1)}) custom-call(bf16[2,512,1024]{2,1,0:T(8,128)(2,1)S(1)} %bitcast.391, f32[2,64,1024]{2,1,0:T(8,128)S(1)} %copy-done.11, ...), custom_call_target="tpu_custom_call" | custom-call | tf_op jit(solution)/shard_map/pallas_call | solution.py:931
  377.0 40.5 %shard_map.215 = (bf16[2,64,1024]{2,1,0:T(8,128)(2,1)S(1)}, f32[1,1024]{1,0:T(1,128)S(1)}, bf16[2,512,1024]{2,1,0:T(8,128)(2,1)S(1)}, bf16[256,512]{1,0:T(8,128)(2,1)S(1)}, bf16[128,1024]{1,0:T(8,128)(2,1)S(1)}) custom-call(bf16[2,512,1024]{2,1,0:T(8,128)(2,1)S(1)} %bitcast.387, f32[2,64,1024]{2,1,0:T(8,128)S(1)} %convert_element_type.279.rows_ref.refs_1_, ...), custom_call_target="tpu_custom_call" | custom-call | tf_op jit(solution)/shard_map/pallas_call | solution.py:931
  422.7 4.6 convolution_convert_fusion.8
  429.1 3.7 convolution_convert_fusion.6
  432.8 50.2 %shard_map.216 = (f32[2,64,1024]{2,1,0:T(8,128)S(1)}, f32[1,1024]{1,0:T(1,128)S(1)}, bf16[2,512,1024]{2,1,0:T(8,128)(2,1)S(1)}, bf16[256,704]{1,0:T(8,128)(2,1)S(1)}, bf16[176,512]{1,0:T(8,128)(2,1)S(1)}) custom-call(bf16[2,512,1024]{2,1,0:T(8,128)(2,1)S(1)} %bitcast.392, f32[2,64,1024]{2,1,0:T(8,128)S(1)} %copy-done.5, ...), custom_call_target="tpu_custom_call" | custom-call | tf_op jit(solution)/shard_map/pallas_call | solution.py:931
  516.7 36.9 %shard_map.217 = (bf16[2,64,1024]{2,1,0:T(8,128)(2,1)S(1)}, f32[1,1024]{1,0:T(1,128)S(1)}, bf16[256,512]{1,0:T(8,128)(2,1)S(1)}, bf16[128,1024]{1,0:T(8,128)(2,1)S(1)}) custom-call(bf16[2,512,1024]{2,1,0:T(8,128)(2,1)S(1)} %bitcast.388, f32[2,64,1024]{2,1,0:T(8,128)S(1)} %bitcast_convert_fusion.2.rows_ref.refs_1_, ...), custom_call_target="tpu_custom_call" | custom-call | tf_op jit(solution)/shard_map/pallas_call | solution.py:931
  556.9 23.1 %shard_map.213.refs_10_ = bf16[2,64,1024]{2,1,0:T(8,128)(2,1)S(1)} custom-call(bf16[2,512,1024]{2,1,0:T(8,128)(2,1)S(1)} %bitcast.390, f32[2,64,1024]{2,1,0:T(8,128)S(1)} %copy-done.12, f32[1,1024]{1,0:T(1,128)S(1)} %get-tuple-element.329.gain_ref.refs_2_), custom_call_target="tpu_custom_call" | custom-call | tf_op jit(solution)/shard_map/pallas_call | solution.py:931
  586.9 68.7 %shard_map.218 = (bf16[2,4,256,512]{3,2,1,0:T(8,128)(2,1)S(1)}, bf16[2,4,256,704]{3,2,1,0:T(8,128)(2,1)S(1)}, bf16[2,4,176,512]{3,2,1,0:T(8,128)(2,1)S(1)}, bf16...) custom-call(bf16[256,512]{1,0:T(8,128)(2,1)S(1)} %copy-done.29, ...), custom_call_target="tpu_custom_call" | custom-call | tf_op jit(solution)/shard_map/pallas_call | solution.py:953
  667.6 5.7 shard_map.219
  (528 shorter events, 153.5 us)
Async XLA Ops:
  8.0 74.5 %all-reduce.4.cloned.1.call-start = ((), (), s32[]{:S(2)}) async-start(), calls=%async_computation.6 | async-start | bytes 532480
  12.4 121.6 %all-gather.12.cloned.1.call-start = ((), (), s32[]{:S(2)}) async-start(), calls=%async_computation.1 | async-start | bytes 1310720 | tf_op jit(solution)/shard_map/all_gather | solution.py:1049
  13.3 122.4 %all-gather.10.cloned.1.call-start = ((), (), s32[]{:S(2)}) async-start(), calls=%async_computation | async-start | bytes 1310720 | tf_op jit(solution)/shard_map/all_gather | solution.py:1056
  16.7 8.2 %collective-permute-start = (bf16[256,512]{0,1:T(8,128)(2,1)S(1)}, bf16[256,512]{0,1:T(8,128)(2,1)S(1)}, u32[]{:S(2)}, u32[]{:S(2)}) collective-permute-start(bf16[256,512]{0,1:T(8,128)(2,1)S(1)} %bitcast.424), channel_id=1, source_target_pairs={{0,16},{16,0},{1,17},{17,1},{2,18},{18,2},{3,19},{19,3},{4,20},{20... | collective-permute-start | bytes 786440 | tf_op jit(solution)/shard_map/ppermute | solution.py:1045
  25.7 160.3 %all-gather.14.cloned.1.call-start = ((), (), s32[]{:S(2)}) async-start(), calls=%async_computation.2 | async-start | bytes 1802240 | tf_op jit(solution)/shard_map/all_gather | solution.py:1056
  29.0 9.1 %collective-permute-start.2 = (bf16[256,704]{0,1:T(8,128)(2,1)S(1)}, bf16[256,704]{0,1:T(8,128)(2,1)S(1)}, u32[]{:S(2)}, u32[]{:S(2)}) collective-permute-start(bf16[256,704]{0,1:T(8,128)(2,1)S(1)} %bitcast.423), channel_id=1, source_target_pairs={{0,16},{16,0},{1,17},{17,1},{2,18},{18,2},{3,19},{19,3},{4,20},{20... | collective-permute-start | bytes 1081352 | tf_op jit(solution)/shard_map/ppermute | solution.py:1045
  39.1 190.6 %all-gather.16.cloned.1.call-start = ((), (), s32[]{:S(2)}) async-start(), calls=%async_computation.3 | async-start | bytes 1310720 | tf_op jit(solution)/shard_map/all_gather | solution.py:1056
  39.8 244.4 %all-gather.18.cloned.1.call-start = ((), (), s32[]{:S(2)}) async-start(), calls=%async_computation.4 | async-start | bytes 1802240 | tf_op jit(solution)/shard_map/all_gather | solution.py:1056
  40.6 249.0 %all-gather.20.cloned.1.call-start = ((), (), s32[]{:S(2)}) async-start(), calls=%async_computation.5 | async-start | bytes 2621440 | tf_op jit(solution)/shard_map/all_gather | solution.py:1077
  41.6 44.5 %collective-permute-start.3 = (bf16[88,1024]{1,0:T(8,128)(2,1)S(1)}, bf16[88,1024]{1,0:T(8,128)(2,1)S(1)}, u32[]{:S(2)}, u32[]{:S(2)}) collective-permute-start(bf16[88,1024]{1,0:T(8,128)(2,1)S(1)} %dynamic-slice_bitcast_fusion.1), channel_id=1, source_target_pairs={{0,16},{16,0},{1,17},{17,1},{2,18},{18,2},{3,19},{19,3},{4,20},{20... | collective-permute-start | bytes 540680 | tf_op jit(solution)/shard_map/ppermute | solution.py:1045
  59.9 82.4 %copy-start.116 = (s32[1,1,512]{2,1,0:T(1,128)}, s32[1,1,512]{2,1,0:T(1,128)S(1)}, u32[]{:S(2)}) copy-start(s32[1,1,512]{2,1,0:T(1,128)S(1)} %get-tuple-element.332) | copy-start | bytes 6148
  82.5 53.2 %copy-start.6 = (bf16[2,512,1024]{2,1,0:T(8,128)(2,1)}, bf16[2,512,1024]{2,1,0:T(8,128)(2,1)S(1)}, u32[]{:S(2)}) copy-start(bf16[2,512,1024]{2,1,0:T(8,128)(2,1)S(1)} %shard_map.209) | copy-start | bytes 6291460
  84.1 62.8 %copy-start.108 = (bf16[2,1,2,16,1,128]{5,3,4,2,1,0:T(8,128)(2,1)}, bf16[2,1,2,16,1,128]{5,3,4,2,1,0:T(8,128)(2,1)S(1)}, u32[]{:S(2)}) copy-start(bf16[2,1,2,16,1,128]{5,3,4,2,1,0:T(8,128)(2,1)S(1)} %copy.213) | copy-start | bytes 49156
  135.7 17.8 %collective-permute-start.1 = (bf16[128,1024]{1,0:T(8,128)(2,1)}, bf16[128,1024]{1,0:T(8,128)(2,1)S(1)}, u32[]{:S(2)}, u32[]{:S(2)}) collective-permute-start(bf16[128,1024]{1,0:T(8,128)(2,1)} %dynamic-slice_bitcast_fusion), channel_id=1, source_target_pairs={{0,16},{16,0},{1,17},{17,1},{2,18},{18,2},{3,19},{19,3},{4,20},{20... | collective-permute-start | bytes 786440 | tf_op jit(solution)/shard_map/ppermute | solution.py:1051
  241.0 131.2 %copy-start.63 = (bf16[1,512,1,128]{3,1,2,0:T(8,128)(2,1)}, bf16[1,512,1,128]{3,1,2,0:T(8,128)(2,1)S(1)}, u32[]{:S(2)}) copy-start(bf16[1,512,1,128]{3,1,2,0:T(8,128)(2,1)S(1)} %copy.207) | copy-start | bytes 393220
  241.2 127.1 %copy-start.71 = (f32[512,16]{0,1:T(8,128)}, f32[512,16]{0,1:T(8,128)S(1)}, u32[]{:S(2)}) copy-start(f32[512,16]{0,1:T(8,128)S(1)} %get-tuple-element.345) | copy-start | bytes 98308
  244.4 123.9 %copy-start.132 = (f32[512]{0:T(512)}, f32[512]{0:T(512)S(1)}, u32[]{:S(2)}) copy-start(f32[512]{0:T(512)S(1)} %get-tuple-element.289) | copy-start | bytes 6148
  311.9 46.0 %copy-start.82 = (bf16[128,1024]{1,0:T(8,128)(2,1)S(1)}, bf16[128,1024]{1,0:T(8,128)(2,1)}, u32[]{:S(2)}) copy-start(bf16[128,1024]{1,0:T(8,128)(2,1)} %copy-done.80) | copy-start | bytes 786436
  311.9 46.0 %copy-start.126 = (bf16[512,128]{0,1:T(8,128)(2,1)S(1)}, bf16[512,128]{0,1:T(8,128)(2,1)}, u32[]{:S(2)}) copy-start(bf16[512,128]{0,1:T(8,128)(2,1)} %copy-done.125) | copy-start | bytes 393220
  312.0 46.0 %copy-start.128 = (bf16[512,128]{0,1:T(8,128)(2,1)S(1)}, bf16[512,128]{0,1:T(8,128)(2,1)}, u32[]{:S(2)}) copy-start(bf16[512,128]{0,1:T(8,128)(2,1)} %copy-done.127) | copy-start | bytes 393220
  377.0 40.5 %copy-start.87 = (bf16[1024,352]{0,1:T(8,128)(2,1)S(1)}, bf16[1024,352]{0,1:T(8,128)(2,1)}, u32[]{:S(2)}) copy-start(bf16[1024,352]{0,1:T(8,128)(2,1)} %copy-done.86) | copy-start | bytes 2162692
  432.8 50.2 %copy-start.83 = (bf16[128,1024]{1,0:T(8,128)(2,1)S(1)}, bf16[128,1024]{1,0:T(8,128)(2,1)}, u32[]{:S(2)}) copy-start(bf16[128,1024]{1,0:T(8,128)(2,1)} %copy-done.80) | copy-start | bytes 786436
  432.8 50.2 %copy-start.122 = (bf16[512,128]{0,1:T(8,128)(2,1)S(1)}, bf16[512,128]{0,1:T(8,128)(2,1)}, u32[]{:S(2)}) copy-start(bf16[512,128]{0,1:T(8,128)(2,1)} %copy-done.121) | copy-start | bytes 393220
  432.8 50.2 %copy-start.124 = (bf16[512,128]{0,1:T(8,128)(2,1)S(1)}, bf16[512,128]{0,1:T(8,128)(2,1)}, u32[]{:S(2)}) copy-start(bf16[512,128]{0,1:T(8,128)(2,1)} %copy-done.123) | copy-start | bytes 393220
  (141 other events, 583.8 us)
Sparse Core Ops, SparseCore 0:
  12.6 54.2 all-reduce.3
Sparse Core Ops, SparseCore 1:
  15.0 28.7 all-gather.11
  45.8 28.9 all-gather.9
  76.8 52.7 all-gather.13
  131.8 29.4 all-gather.15
  163.4 34.8 all-gather.17
  199.9 33.6 all-gather.19

commit v3 on v2

--- a/solution.py
+++ b/solution.py
@@ -1,5 +1,7 @@
 import functools
 import math
+import types
+from typing import Any, NamedTuple
 
 import jax
 import jax.numpy as jnp
@@ -666,6 +668,46 @@
     pl.semaphore_wait(barrier, len(others))
 
 
+def nn(left, right):
+    return jnp.dot(left, right, preferred_element_type=F32)
+
+
+def nt(left, right):
+    return lax.dot_general(left, right, (((1,), (1,)), ((), ())), preferred_element_type=F32)
+
+
+def tn(left, right):
+    return lax.dot_general(left, right, (((0,), (0,)), ((), ())), preferred_element_type=F32)
+
+
+def in_blocks(length, size, body):
+    def step(index, carry):
+        body(pl.ds(pl.multiple_of(index * size, size), size), index * size)
+        return carry
+
+    lax.fori_loop(0, length // size, step, 0)
+
+
+def weights_of_scores(query, keys, pkeys, seg_rows, seg_cols, begin, rate):
+    scale = 1.0 / math.sqrt(HD)
+    inner = nt(query, keys)
+    per_scores = nt(query, pkeys) * scale
+    row_places = begin + lax.broadcasted_iota(jnp.int32, inner.shape, 0)
+    col_places = lax.broadcasted_iota(jnp.int32, inner.shape, 1)
+    allowed = (seg_rows == seg_cols) & (col_places <= row_places)
+    distance = jnp.maximum(row_places - col_places, 0).astype(F32)
+    decay_w = jnp.where(allowed, jnp.exp(-rate * distance) * (1.0 / HD), 0.0)
+    seq_scores = jnp.where(allowed, inner * scale, -jnp.inf)
+    top = jnp.maximum(
+        jnp.max(per_scores, axis=1, keepdims=True), jnp.max(seq_scores, axis=1, keepdims=True)
+    )
+    per_exp = jnp.exp(per_scores - top)
+    seq_exp = jnp.exp(seq_scores - top)
+    denom = jnp.sum(per_exp, axis=1, keepdims=True) + jnp.sum(seq_exp, axis=1, keepdims=True)
+    share = 1.0 / denom
+    return inner, decay_w, distance, seq_exp * share, per_exp * share
+
+
 def start_kernel(rows_ref, gain_ref, full_ref, gsend, grecv):
     meet()
     gathers = [Gather(full_ref, batch, gsend, grecv) for batch in range(2)]
@@ -678,82 +720,394 @@
         gather.finish()
 
 
-def forward_kernel(low, last, part_ref, rows_ref, gain_ref, own_ref, *rest):
-    if last:
-        pair, away, near, ssend, srecv = rest
-    else:
-        full_ref, pair, away, near, ssend, srecv, gsend, grecv = rest
+class ForwardIn(NamedTuple):
+    normed: Any
+    rows: Any
+    gain_two: Any
+    gain_next: Any
+    gu: Any
+    down: Any
+    mix: Any
+    out: Any
+    pkeys: Any
+    pvalues: Any
+    rate: Any
+    seg_rows: Any
+    seg_cols: Any
+
+
+class ForwardOut(NamedTuple):
+    qkv: Any
+    gate: Any
+    recalled: Any
+    combined: Any
+    mid: Any
+    normed_two: Any
+    gate_up: Any
+    hidden: Any
+    out_rows: Any
+    normed_next: Any
+
+
+class BackwardIn(NamedTuple):
+    grad_full: Any
+    grad_rows: Any
+    rows: Any
+    normed: Any
+    gain_one: Any
+    gain_two: Any
+    gu: Any
+    down: Any
+    mix: Any
+    out: Any
+    pkeys: Any
+    pvalues: Any
+    rate: Any
+    seg_rows: Any
+    seg_cols: Any
+    qkv: Any
+    gate: Any
+    recalled: Any
+    combined: Any
+    mid: Any
+    normed_two: Any
+    gate_up: Any
+    hidden: Any
+
+
+class BackwardOut(NamedTuple):
+    grad_mix: Any
+    grad_out: Any
+    gains: Any
+    grad_persist: Any
+    grad_rate: Any
+    gu_sum: Any
+    down_sum: Any
+    grad_h: Any
+
+
+class PlaneScratch(NamedTuple):
+    part: Any
+    pair: Any
+    away: Any
+    near: Any
+    ssend: Any
+    srecv: Any
+    gsend: Any
+    grecv: Any
+
+
+class BackwardScratch(NamedTuple):
+    grad_gu: Any
+    grad_proj: Any
+    grad_keys: Any
+    grad_values: Any
+    own_gu: Any
+    own_down: Any
+    branch: Any
+    grad_mid: Any
+    gu_slots: Any
+    down_slots: Any
+    csend: Any
+    crecv: Any
+
+
+class EarlyIn(NamedTuple):
+    early_mix: Any
+    early_out: Any
+
+
+class EarlyOut(NamedTuple):
+    mix_sum: Any
+    out_sum: Any
+
+
+class EarlyScratch(NamedTuple):
+    mix_slots: Any
+    root_slots: Any
+    rsend: Any
+    rrecv: Any
+
+
+class NextOut(NamedTuple):
+    grad_next: Any
+
+
+def fields(*kinds):
+    return tuple(name for kind in kinds for name in kind._fields)
+
+
+def named(names, refs):
+    return types.SimpleNamespace(**dict(zip(names, refs, strict=True)))
+
+
+def forward_layer(ins, outs, *refs):
+    r = named(ins + outs + fields(PlaneScratch), refs)
+    length = r.part.shape[1]
+    last = not hasattr(r, "normed_next")
+
+    def project(batch):
+        def block(rows, begin):
+            proj = nn(r.normed[batch, rows, :], r.mix[...])
+            r.qkv[batch, rows, :] = proj[:, : 3 * HD].astype(BF)
+            r.gate[batch, rows, :] = jax.nn.sigmoid(proj[:, 3 * HD :])
+
+        in_blocks(length, 256, block)
+
+    def mixer(batch):
+        def block(rows, begin):
+            values = r.qkv[batch, :, 2 * HD :]
+            inner, decay_w, _, probs, per_probs = weights_of_scores(
+                r.qkv[batch, rows, :HD],
+                r.qkv[batch, :, HD : 2 * HD],
+                r.pkeys[...],
+                r.seg_rows[batch, rows, :],
+                r.seg_cols[batch],
+                begin,
+                r.rate[...],
+            )
+            attended = nn(probs.astype(BF), values) + nn(per_probs.astype(BF), r.pvalues[...])
+            recalled = nn((inner * decay_w).astype(BF), values).astype(BF)
+            r.recalled[batch, rows, :] = recalled
+            combined = attended.astype(BF).astype(F32)
+            combined = combined + r.gate[batch, rows, :] * recalled.astype(F32)
+            combined = combined.astype(BF)
+            r.combined[batch, rows, :] = combined
+            r.part[batch, rows, :] = nn(combined, r.out[...]).astype(BF)
+
+        in_blocks(length, 128, block)
+
+    def feed(batch):
+        def block(rows, begin):
+            gate_up = nn(r.normed_two[batch, rows, :], r.gu[...])
+            r.gate_up[batch, rows, :] = gate_up
+            half = gate_up.shape[1] // 2
+            hidden = (jax.nn.silu(gate_up[:, :half]) * gate_up[:, half:]).astype(BF)
+            r.hidden[batch, rows, :] = hidden
+            r.part[batch, rows, :] = nn(hidden, r.down[...]).astype(BF)
+
+        in_blocks(length, 256, block)
+
+    def scatter(batch):
+        return Scatter(r.part, batch, r.pair, r.away, r.near, r.ssend, r.srecv)
+
+    def send_normed(batch, own, gain, full):
+        gather = Gather(full, batch, r.gsend, r.grecv)
+        gather.start((own * rms_scale(own) * gain[...]).astype(BF))
+        return gather
+
     meet()
-    scatters = [Scatter(part_ref, b, pair, away, near, ssend, srecv) for b in range(2)]
-    for scatter in scatters:
-        scatter.start()
-    for scatter in scatters:
-        scatter.forward()
+    first, second = (scatter(batch) for batch in range(2))
+    project(0)
+    mixer(0)
+    first.start()
+    first.forward()
+    project(1)
+    mixer(1)
+    second.start()
+    second.forward()
     gathers = []
-    for batch, scatter in enumerate(scatters):
-        own = (rows_ref[batch] + scatter.finish()).astype(own_ref.dtype)
-        own_ref[batch] = own
+    for batch, part in enumerate((first, second)):
+        mid = r.rows[batch] + part.finish()
+        r.mid[batch] = mid
+        gathers.append(send_normed(batch, mid, r.gain_two, r.normed_two))
+    first, second = (scatter(batch) for batch in range(2))
+    for batch, part in enumerate((first, second)):
+        gathers[batch].forward()
+        gathers[batch].finish()
+        feed(batch)
+        part.start()
+        part.forward()
+    gathers = []
+    for batch, part in enumerate((first, second)):
+        own = (r.mid[batch] + part.finish()).astype(BF)
+        r.out_rows[batch] = own
         if not last:
-            own = own.astype(F32)
-            gather = Gather(full_ref, batch, gsend, grecv)
-            gather.start((own * rms_scale(own) * gain_ref[...]).astype(BF))
-            gathers.append(gather)
+            gathers.append(
+                send_normed(batch, own.astype(F32), r.gain_next, r.normed_next)
+            )
     for gather in gathers:
         gather.forward()
     for gather in gathers:
         gather.finish()
 
 
-def backward_kernel(last, rooted, *refs):
-    part_ref, rows_ref, gain_ref, grad_ref, *refs = refs
-    columns = 2
-    owns, refs = refs[:columns], refs[columns:]
-    own_ref, gains_ref, *refs = refs
-    if not last:
-        full_ref, *refs = refs
-    outs, refs = refs[:columns], refs[columns:]
-    pair, away, near, ssend, srecv, *refs = refs
-    if not last:
-        gsend, grecv, *refs = refs
-    slots, refs = refs[:columns], refs[columns:]
-    csend, crecv, *refs = refs
-    sums_of = [ColumnSum(owns[0], slots[0], outs[0], csend, crecv, 0)]
-    if rooted:
-        sums_of.append(RootSum(owns[1], slots[1], outs[1], *refs))
-    else:
-        sums_of.append(ColumnSum(owns[1], slots[1], outs[1], csend, crecv, 1))
+def backward_layer(ins, outs, *refs):
+    scratch = fields(PlaneScratch, BackwardScratch)
+    earlier = len(outs) == len(fields(BackwardOut, EarlyOut))
+    if earlier:
+        scratch += fields(EarlyScratch)
+    r = named(ins + outs + scratch, refs)
+    length = r.part.shape[1]
+    last = not hasattr(r, "grad_next")
+    sums = [
+        ColumnSum(r.own_gu, r.gu_slots, r.gu_sum, r.csend, r.crecv, 0),
+        ColumnSum(r.own_down, r.down_slots, r.down_sum, r.csend, r.crecv, 1),
+    ]
+    early = []
+    if earlier:
+        early = [
+            ColumnSum(r.early_mix, r.mix_slots, r.mix_sum, r.csend, r.crecv, 2),
+            RootSum(r.early_out, r.root_slots, r.out_sum, r.rsend, r.rrecv),
+        ]
+
+    def feed_back(batch):
+        def block(rows, begin):
+            grad_hidden = nt(r.grad_full[batch, rows, :], r.down[...])
+            half = grad_hidden.shape[1]
+            gate_part = r.gate_up[batch, rows, :half]
+            up_part = r.gate_up[batch, rows, half:]
+            sig_part = jax.nn.sigmoid(gate_part)
+            silu = gate_part * sig_part
+            grad_gate = grad_hidden * up_part * (sig_part + silu * (1.0 - sig_part))
+            r.grad_gu[batch, rows, :half] = grad_gate.astype(BF)
+            r.grad_gu[batch, rows, half:] = (grad_hidden * silu).astype(BF)
+            r.part[batch, rows, :] = nt(r.grad_gu[batch, rows, :], r.gu[...]).astype(BF)
+
+        in_blocks(length, 256, block)
+
+    def feed_weights():
+        def down(cols, begin):
+            grad = tn(r.hidden[0], r.grad_full[0, :, cols])
+            grad = grad + tn(r.hidden[1], r.grad_full[1, :, cols])
+            grad = grad.reshape(4, grad.shape[0] // 4, grad.shape[1])
+            r.own_down[:, :, cols] = grad.astype(BF)
+
+        in_blocks(D, 256, down)
+        product(r.own_gu, r.normed_two, r.grad_gu)
+
+    def product(out, left, right):
+        for owner in range(4):
+            cols = slice(owner * (D // 4), (owner + 1) * (D // 4))
+            grad = tn(left[0, :, cols], right[0]) + tn(left[1, :, cols], right[1])
+            out[owner] = grad.astype(BF)
+
+    def mixer_back(batch):
+        scale = 1.0 / math.sqrt(HD)
+        r.grad_keys[...] = jnp.zeros_like(r.grad_keys)
+        r.grad_values[...] = jnp.zeros_like(r.grad_values)
+
+        def block(rows, begin):
+            grad_combined = nt(r.branch[batch, rows, :], r.out[...])
+            gate = r.gate[batch, rows, :]
+            recalled = r.recalled[batch, rows, :].astype(F32)
+            attn_rows = grad_combined.astype(BF)
+            memory_rows = (grad_combined * gate).astype(BF)
+            grad_pre = grad_combined * recalled * gate * (1.0 - gate)
+            r.grad_proj[batch, rows, 3 * HD :] = grad_pre.astype(BF)
+            query = r.qkv[batch, rows, :HD]
+            keys = r.qkv[batch, :, HD : 2 * HD]
+            values = r.qkv[batch, :, 2 * HD :]
+            inner, decay_w, distance, probs, per_probs = weights_of_scores(
+                query,
+                keys,
+                r.pkeys[...],
+                r.seg_rows[batch, rows, :],
+                r.seg_cols[batch],
+                begin,
+                r.rate[...],
+            )
+            per_dp = nt(attn_rows, r.pvalues[...])
+            seq_dp = nt(attn_rows, values)
+            delta = jnp.sum(per_probs * per_dp, axis=1, keepdims=True) + jnp.sum(
+                probs * seq_dp, axis=1, keepdims=True
+            )
+            per_ds = (per_probs * (per_dp - delta)).astype(BF)
+            seq_ds = (probs * (seq_dp - delta)).astype(BF)
+            weighted = nt(memory_rows, values) * decay_w
+            grad_inner = weighted.astype(BF)
+            memory = inner * decay_w
+            rate_terms = weighted * inner * distance
+            r.grad_rate[...] -= jnp.sum(rate_terms, axis=0, keepdims=True)
+            grad_query = (nn(per_ds, r.pkeys[...]) + nn(seq_ds, keys)) * scale
+            grad_query = grad_query + nn(grad_inner, keys)
+            r.grad_proj[batch, rows, :HD] = grad_query.astype(BF)
+            r.grad_keys[...] += tn(seq_ds, query) * scale + tn(grad_inner, query)
+            r.grad_values[...] += tn(probs.astype(BF), attn_rows) + tn(
+                memory.astype(BF), memory_rows
+            )
+            r.grad_persist[0] += tn(per_ds, query) * scale
+            r.grad_persist[1] += tn(per_probs.astype(BF), attn_rows)
+
+        in_blocks(length, 128, block)
+        r.grad_proj[batch, :, HD : 2 * HD] = r.grad_keys[...].astype(BF)
+        r.grad_proj[batch, :, 2 * HD : 3 * HD] = r.grad_values[...].astype(BF)
+
+        def back(rows, begin):
+            r.part[batch, rows, :] = nt(r.grad_proj[batch, rows, :], r.mix[...]).astype(BF)
+
+        in_blocks(length, 256, back)
+
+    def scatter(batch):
+        return Scatter(r.part, batch, r.pair, r.away, r.near, r.ssend, r.srecv)
+
+    def through_norm(batch, part, rows, gain):
+        grad_normed = part.finish()
+        inverse = rms_scale(rows)
+        return norm_back(grad_normed, rows * inverse, inverse, gain[...])
+
     meet(True)
-    scatters = [Scatter(part_ref, b, pair, away, near, ssend, srecv) for b in range(2)]
-    for scatter in scatters:
-        scatter.start()
-    for column in sums_of:
+    r.grad_rate[...] = jnp.zeros_like(r.grad_rate)
+    r.grad_persist[...] = jnp.zeros_like(r.grad_persist)
+    for column in early:
         column.start()
-    for scatter in scatters:
-        scatter.forward()
+    first, second = (scatter(batch) for batch in range(2))
+    for batch, part in enumerate((first, second)):
+        feed_back(batch)
+        part.start()
+        part.forward()
+    feed_weights()
     gathers = []
-    sums = jnp.zeros((1, D), F32)
-    for batch, scatter in enumerate(scatters):
-        grad_normed = scatter.finish()
-        rows = rows_ref[batch]
-        inverse = rms_scale(rows)
-        grad_rows, gain_sum = norm_back(grad_normed, rows * inverse, inverse, gain_ref[...])
-        sums = sums + gain_sum[None]
-        own = (grad_ref[batch] + grad_rows).astype(own_ref.dtype)
-        own_ref[batch] = own
+    gain_sums = []
+    for batch, part in enumerate((first, second)):
+        grad_mid, gain_sum = through_norm(batch, part, r.mid[batch], r.gain_two)
+        gain_sums.append(gain_sum[None])
+        grad_mid = grad_mid + r.grad_rows[batch]
+        r.grad_mid[batch] = grad_mid
+        gather = Gather(r.branch, batch, r.gsend, r.grecv)
+        gather.start(grad_mid.astype(BF))
+        gathers.append(gather)
+    r.gains[1:2] = gain_sums[0] + gain_sums[1]
+    for column in early:
+        column.hop(1)
+    for column in early:
+        column.hop(2)
+    for column in sums:
+        column.start()
+    first, second = (scatter(batch) for batch in range(2))
+    for batch, part in enumerate((first, second)):
+        gathers[batch].forward()
+        gathers[batch].finish()
+        mixer_back(batch)
+        part.start()
+        part.forward()
+        if batch == 0:
+            for column in early:
+                column.finish()
+            for column in sums:
+                column.hop(1)
+    product(r.grad_mix, r.normed, r.grad_proj)
+    grad_out = tn(r.combined[0], r.branch[0]) + tn(r.combined[1], r.branch[1])
+    r.grad_out[...] = grad_out.astype(BF)
+    gathers = []
+    gain_sums = []
+    for batch, part in enumerate((first, second)):
+        grad_h, gain_sum = through_norm(batch, part, r.rows[batch], r.gain_one)
+        gain_sums.append(gain_sum[None])
+        grad_h = (grad_h + r.grad_mid[batch]).astype(BF)
+        r.grad_h[batch] = grad_h
         if not last:
-            gather = Gather(full_ref, batch, gsend, grecv)
-            gather.start(own.astype(BF))
+            gather = Gather(r.grad_next, batch, r.gsend, r.grecv)
+            gather.start(grad_h)
             gathers.append(gather)
-    gains_ref[...] = sums
-    for column in sums_of:
-        column.hop(1)
+    r.gains[0:1] = gain_sums[0] + gain_sums[1]
+    for column in sums:
+        column.hop(2)
     for gather in gathers:
         gather.forward()
-    for column in sums_of:
-        column.hop(2)
     for gather in gathers:
         gather.finish()
-    for column in sums_of:
+    for column in sums:
         column.finish()
 
 
@@ -762,11 +1116,18 @@
     x, s, z = place
     sibling, beside, partner = (peer(place, 0, True), peer(place, 2, False), peer(place, 1, False))
     across = peer(place, 3, False)
-    by_layer = [refs[0:6], refs[6:12]]
+    by_layer = [list(refs[0:6]), list(refs[6:12])]
     small_ref = refs[12]
     bufs = refs[13:16]
     out_buf, rows_buf, grads_buf, plane_buf = refs[16:20]
-    column_buf, psend, precv, osend, orecv, rsend, rrecv, zsend, zrecv, ssend, srecv = refs[20:]
+    column_buf, mix_sum, out_sum, mix_slots, root_slots, *sems = refs[20:]
+    psend, precv, osend, orecv, rsend, rrecv, zsend, zrecv, ssend, srecv, *sems = sems
+    csend, crecv, hsend, hrecv = sems
+    columns = [
+        ColumnSum(by_layer[0][0], mix_slots, mix_sum, csend, crecv, 0),
+        RootSum(by_layer[0][3], root_slots, out_sum, hsend, hrecv),
+    ]
+    by_layer[0][0], by_layer[0][3] = mix_sum, out_sum
 
     def copy(source, landing, sems, index, target):
         return pltpu.make_async_remote_copy(
@@ -807,19 +1168,35 @@
 
     mine = (x, s)
     turned = (1 - x, s)
+
+    def send(indices):
+        for layer in (0, 1):
+            own, theirs = by_layer[layer], by_layer[1 - layer]
+
+            @pl.when(x == layer)
+            def _():
+                for index in indices:
+                    piece(index, 2, mine, partner, theirs[index]).start()
+                    piece(index, 0, mine, beside, own[index]).start()
+                    piece(index, 1, mine, sibling, own[index]).start()
+                for index in indices:
+                    bufs[index][mine] = own[index][...]
+
+    def turn(indices):
+        for index in indices:
+            piece(index, 2, turned, partner).wait_recv()
+            piece(index, 3, turned, beside).start()
+            piece(index, 4, turned, sibling).start()
+
+    for column in columns:
+        column.start()
+    send((1, 2))
     for layer in (0, 1):
-        own, theirs = by_layer[layer], by_layer[1 - layer]
 
         @pl.when(x == layer)
         def _():
-            for index in range(3):
-                piece(index, 2, mine, partner, theirs[index]).start()
-                piece(index, 0, mine, beside, own[index]).start()
-                piece(index, 1, mine, sibling, own[index]).start()
-            copy(theirs[4], rows_buf, (rsend, rrecv), 0, partner).start()
-            copy(theirs[5], grads_buf, (rsend, rrecv), 1, partner).start()
-            for index in range(3):
-                bufs[index][mine] = own[index][...]
+            copy(by_layer[1 - layer][4], rows_buf, (rsend, rrecv), 0, partner).start()
+            copy(by_layer[1 - layer][5], grads_buf, (rsend, rrecv), 1, partner).start()
 
     total = small_ref[z]
     for dz in (1, 2, 3):
@@ -828,6 +1205,14 @@
     plane_buf[x * 4 + s] = total
     for index in range(7):
         to_plane(index).start()
+    for column in columns:
+        column.hop(1)
+    for column in columns:
+        column.hop(2)
+    turn((1, 2))
+    for column in columns:
+        column.finish()
+    send((0,))
 
     core = s % 2
     root = z == 2 * x + s // 2
@@ -855,16 +1240,13 @@
 
     out_copy(0, sibling).start()
 
-    for index in range(3):
-        piece(index, 2, turned, partner).wait_recv()
-        piece(index, 3, turned, beside).start()
-        piece(index, 4, turned, sibling).start()
+    turn((0,))
     far = (x, (s + 2) % 4)
     far_turned = (1 - x, (s + 2) % 4)
-    for index in range(3):
+    for index in (1, 2, 0):
         piece(index, 0, far, beside).wait_recv()
         piece(index, 5, far, sibling).start()
-    for index in range(3):
+    for index in (1, 2, 0):
         piece(index, 3, far_turned, beside).wait_recv()
         piece(index, 6, far_turned, sibling).start()
     twin = sibling[1]
@@ -897,36 +1279,7 @@
             out_copy(index, sibling).wait_send()
 
 
-def plane_call(kernel, number, operands, outs, scatter, gather, sums=(), root=None):
-    _, length, width = outs["full"].shape
-    size = length // 8
-    scratch = []
-    outs = dict(outs)
-    if scatter:
-        scratch += [
-            pltpu.VMEM((2, 4, size, width), BF),
-            pltpu.VMEM((2, 3, size, width), BF),
-            pltpu.VMEM((2, 3, size, width), BF),
-            pltpu.SemaphoreType.DMA((2, 7)),
-            pltpu.SemaphoreType.DMA((2, 7)),
-        ]
-    if gather:
-        scratch += [pltpu.SemaphoreType.DMA((2, 7)), pltpu.SemaphoreType.DMA((2, 7))]
-    else:
-        del outs["full"]
-    outs = list(outs.values())
-    for part in sums:
-        outs.append(jax.ShapeDtypeStruct(part.shape[1:], BF))
-        scratch.append(pltpu.VMEM((2, 3) + part.shape[1:], BF))
-    if root is not None:
-        outs.append(jax.ShapeDtypeStruct(root.shape, BF))
-        scratch.append(pltpu.VMEM((2,) + root.shape, BF))
-        sums = (*sums, root)
-    if sums:
-        scratch += [pltpu.SemaphoreType.DMA((2, 2, 3)), pltpu.SemaphoreType.DMA((2, 2, 3))]
-    if root is not None:
-        scratch += [pltpu.SemaphoreType.DMA((2,)), pltpu.SemaphoreType.DMA((2,))]
-    operands = (*operands, *sums)
+def kernel_call(kernel, number, operands, outs, scratch):
     vmem = pl.BlockSpec(memory_space=pltpu.VMEM)
     return pl.pallas_call(
         kernel,
@@ -935,37 +1288,117 @@
         out_specs=[vmem] * len(outs),
         scratch_shapes=scratch,
         compiler_params=pltpu.CompilerParams(
-            collective_id=number, has_side_effects=True, vmem_limit_bytes=40 * 2**20
+            collective_id=number, has_side_effects=True, vmem_limit_bytes=58 * 2**20
         ),
     )(*operands)
 
 
+def pairs_of(*sizes):
+    return [pltpu.SemaphoreType.DMA(size) for size in sizes for _ in range(2)]
+
+
+def scatter_scratch(length):
+    size = length // 8
+    return [
+        pltpu.VMEM((2, length, D), BF),
+        pltpu.VMEM((2, 4, size, D), BF),
+        pltpu.VMEM((2, 3, size, D), BF),
+        pltpu.VMEM((2, 3, size, D), BF),
+        *pairs_of((2, 7), (2, 7)),
+    ]
+
+
+def forward_call(number, given, last):
+    count, length, _ = given.normed.shape
+    half = given.down.shape[0]
+    shape = jax.ShapeDtypeStruct
+    outs = dict(
+        qkv=shape((count, length, 3 * HD), BF),
+        gate=shape((count, length, HD), F32),
+        recalled=shape((count, length, HD), BF),
+        combined=shape((count, length, HD), BF),
+        mid=shape((count, length // 8, D), F32),
+        normed_two=shape((count, length, D), BF),
+        gate_up=shape((count, length, 2 * half), F32),
+        hidden=shape((count, length, half), BF),
+        out_rows=shape((count, length // 8, D), BF),
+        normed_next=shape((count, length, D), BF),
+    )
+    if last:
+        del outs[ForwardOut._fields[-1]]
+    operands = [getattr(given, name) for name in ForwardIn._fields]
+    kernel = functools.partial(forward_layer, ForwardIn._fields, tuple(outs))
+    found = kernel_call(kernel, number, operands, list(outs.values()), scatter_scratch(length))
+    return named(outs, found)
+
+
+def backward_call(number, given, last):
+    count, length, _ = given.normed.shape
+    half = given.down.shape[0]
+    depth = D // 4
+    shape = jax.ShapeDtypeStruct
+    outs = dict(
+        grad_mix=shape((4, depth, 4 * HD), BF),
+        grad_out=shape((HD, D), BF),
+        gains=shape((2, D), F32),
+        grad_persist=shape((2,) + given.pkeys.shape, F32),
+        grad_rate=shape((1, length), F32),
+        gu_sum=shape((depth, 2 * half), BF),
+        down_sum=shape((half // 4, D), BF),
+        grad_h=shape((count, length // 8, D), BF),
+    )
+    ins = BackwardIn._fields
+    if last:
+        ins += EarlyIn._fields
+        outs |= dict(mix_sum=shape((depth, 4 * HD), BF), out_sum=shape((HD, D), BF))
+    else:
+        outs |= dict(grad_next=shape((count, length, D), BF))
+    scratch = scatter_scratch(length) + [
+        pltpu.VMEM((count, length, 2 * half), BF),
+        pltpu.VMEM((count, length, 4 * HD), BF),
+        pltpu.VMEM((length, HD), F32),
+        pltpu.VMEM((length, HD), F32),
+        pltpu.VMEM((4, depth, 2 * half), BF),
+        pltpu.VMEM((4, half // 4, D), BF),
+        pltpu.VMEM((count, length, D), BF),
+        pltpu.VMEM((count, length // 8, D), F32),
+        pltpu.VMEM((2, 3, depth, 2 * half), BF),
+        pltpu.VMEM((2, 3, half // 4, D), BF),
+        *pairs_of((3, 2, 3)),
+    ]
+    if last:
+        scratch += [
+            pltpu.VMEM((2, 3, depth, 4 * HD), BF),
+            pltpu.VMEM((2, HD, D), BF),
+            *pairs_of((2,)),
+        ]
+    kernel = functools.partial(backward_layer, ins, tuple(outs))
+    operands = [getattr(given, name) for name in ins]
+    found = kernel_call(kernel, number, operands, list(outs.values()), scratch)
+    return named(outs, found)
+
+
 def final_call(number, by_layer, small):
     operands = (*by_layer[0], *by_layer[1], small)
-    outs = [jax.ShapeDtypeStruct((2, 4) + part.shape, BF) for part in by_layer[0][:3]]
-    outs.append(jax.ShapeDtypeStruct((2,) + by_layer[0][3].shape, BF))
-    outs += [jax.ShapeDtypeStruct(part.shape, BF) for part in by_layer[0][4:]]
+    mix, gu, down, out, *rows = by_layer[1]
+    outs = [jax.ShapeDtypeStruct((2, 4) + part.shape, BF) for part in (mix, gu, down)]
+    outs.append(jax.ShapeDtypeStruct((2,) + out.shape, BF))
+    outs += [jax.ShapeDtypeStruct(part.shape, BF) for part in rows]
     outs.append(jax.ShapeDtypeStruct((8,) + small.shape[1:], F32))
-    sizes = [(3, 7), (4,), (2,), (3,), (7,)]
-    scratch = [pltpu.VMEM((3,) + small.shape[1:], F32)]
-    scratch += [pltpu.SemaphoreType.DMA(size) for size in sizes for _ in range(2)]
-    vmem = pl.BlockSpec(memory_space=pltpu.VMEM)
-    return pl.pallas_call(
-        final_kernel,
-        out_shape=outs,
-        in_specs=[vmem] * len(operands),
-        out_specs=[vmem] * len(outs),
-        scratch_shapes=scratch,
-        compiler_params=pltpu.CompilerParams(
-            collective_id=number, has_side_effects=True, vmem_limit_bytes=40 * 2**20
-        ),
-    )(*operands)
-
-
-def assemble_kernel(mix_buf, gu_buf, down_buf, mix_ref, gu_ref, down_ref):
-    unit = down_buf.shape[2] // 2
+    scratch = [
+        pltpu.VMEM((3,) + small.shape[1:], F32),
+        pltpu.VMEM(mix.shape, BF),
+        pltpu.VMEM(out.shape, BF),
+        pltpu.VMEM((2, 3) + mix.shape, BF),
+        pltpu.VMEM((2,) + out.shape, BF),
+        *pairs_of((3, 7), (4,), (2,), (3,), (7,), (1, 2, 3), (2,)),
+    ]
+    return kernel_call(final_kernel, number, operands, outs, scratch)
+
+
+def assemble_kernel(unit, mix_buf, gu_buf, down_buf, mix_ref, gu_ref, down_ref):
+    padded = down_buf.shape[2]
     half = gu_buf.shape[3] // 2
-    width = 4 * HD
     for which in range(8):
         slot = (which // 4, which % 4)
         mix = mix_buf[slot].astype(F32)
@@ -974,36 +1407,34 @@
             mix_ref[0, :, begin : begin + HD] = mix[:, kind * HD : (kind + 1) * HD]
         part = gu_buf[slot].astype(F32)
         for side in range(2):
-            for owner in range(half // unit):
+            for owner in range(half // padded):
                 begin = side * FF + (owner * 8 + which) * unit
-                source = side * half + owner * unit
+                source = side * half + owner * padded
                 gu_ref[0, :, begin : begin + unit] = part[:, source : source + unit]
     for pair in range(2):
         down = down_buf[0, pair].astype(F32)
-        down_ref[0, pair * unit : (pair + 1) * unit, :width] = down[:unit]
-        down_ref[0, pair * unit : (pair + 1) * unit, width:] = down[unit:]
-
-
-def assemble_call(mix_buf, gu_buf, down_buf):
-    depth, unit = mix_buf.shape[2], down_buf.shape[2] // 2
+        down_ref[0, pair * unit : (pair + 1) * unit, :] = down[:unit]
+
+
+def assemble_call(unit, mix_buf, gu_buf, down_buf):
+    depth, padded = mix_buf.shape[2], down_buf.shape[2]
     rows = depth // 4
-    wide = gu_buf.shape[3] * 8
     return pl.pallas_call(
-        assemble_kernel,
+        functools.partial(assemble_kernel, unit),
         grid=(4,),
         out_shape=[
             jax.ShapeDtypeStruct((1, depth, 4 * D), F32),
-            jax.ShapeDtypeStruct((1, depth, wide), F32),
+            jax.ShapeDtypeStruct((1, depth, 2 * FF), F32),
             jax.ShapeDtypeStruct((1, 8 * unit, D), F32),
         ],
         in_specs=[
             pl.BlockSpec((2, 4, rows, 4 * HD), lambda i: (0, 0, i, 0)),
-            pl.BlockSpec((2, 4, rows, wide // 8), lambda i: (0, 0, i, 0)),
-            pl.BlockSpec((1, 2, 2 * unit, D // 2), lambda i: (i // 2, i % 2, 0, 0)),
+            pl.BlockSpec((2, 4, rows, gu_buf.shape[3]), lambda i: (0, 0, i, 0)),
+            pl.BlockSpec((1, 2, padded, D), lambda i: (i // 2, i % 2, 0, 0)),
         ],
         out_specs=[
             pl.BlockSpec((1, rows, 4 * D), lambda i: (0, i, 0)),
-            pl.BlockSpec((1, rows, wide), lambda i: (0, i, 0)),
+            pl.BlockSpec((1, rows, 2 * FF), lambda i: (0, i, 0)),
             pl.BlockSpec((1, 2 * unit, D), lambda i: (0, i, 0)),
         ],
         compiler_params=pltpu.CompilerParams(vmem_limit_bytes=40 * 2**20),
@@ -1028,14 +1459,16 @@
     heads = w_mix[0].reshape(depth, 4, H, HD)
     halves = w_gu[0].reshape(depth, 2, nz, width, unit)
     downs = w_down[0].reshape(width, unit, D)
+    more = -unit % 32
 
     def pick(which):
+        both = lax.dynamic_index_in_dim(halves, which, 3, keepdims=False)
+        both = jnp.pad(both, ((0, 0), (0, 0), (0, 0), (0, more)))
+        down = lax.dynamic_index_in_dim(downs, which, 0, keepdims=False)
         return (
             lax.dynamic_index_in_dim(heads, which, 2, keepdims=False).reshape(depth, 4 * HD),
-            lax.dynamic_index_in_dim(halves, which, 3, keepdims=False).reshape(
-                depth, 2 * nz * unit
-            ),
-            lax.dynamic_index_in_dim(downs, which, 0, keepdims=False),
+            both.reshape(depth, 2 * nz * (unit + more)),
+            jnp.pad(down, ((0, more), (0, 0))),
         )
 
     def layers(own, got):
@@ -1069,178 +1502,68 @@
     def own_rows(whole):
         return lax.dynamic_slice_in_dim(whole[:, 0], x * size, size, 1).astype(F32)
 
-    full = jax.ShapeDtypeStruct((count, length, D), BF)
-    own32 = jax.ShapeDtypeStruct((count, size, D), F32)
-    own16 = jax.ShapeDtypeStruct((count, size, D), BF)
-    sums = jax.ShapeDtypeStruct((1, D), F32)
-
     cot_full = lax.all_gather(cotangent[:, 0], "seq", axis=1, tiled=True)
     rows = own_rows(inputs)
-    (normed,) = plane_call(
-        start_kernel, 0, (rows, gains[0, :, :, 0]), {"full": full}, False, True
-    )
-    kept = []
+    full = jax.ShapeDtypeStruct((count, length, D), BF)
+    (normed,) = kernel_call(
+        start_kernel, 0, (rows, gains[0, :, :, 0]), [full], pairs_of((2, 7))
+    )
+    of_layer = [
+        dict(
+            mix=mix_w[layer],
+            out=out_w[layer],
+            gu=gu_w[layer],
+            down=down_w[layer],
+            gain_one=gains[layer, :, :, 0],
+            gain_two=gains[layer, :, :, 1],
+            gain_next=gains[1, :, :, 0],
+            pkeys=persist[layer, 0],
+            pvalues=persist[layer, 1],
+            rate=rates[layer].reshape(1, 1),
+            seg_rows=segment_ids[:, 0, :, None],
+            seg_cols=segment_ids,
+        )
+        for layer in range(2)
+    ]
     outputs = []
-    flat = count * length
     for layer in range(2):
-        proj = jnp.dot(normed.reshape(flat, D), mix_w[layer], preferred_element_type=F32)
-        qkv = proj[:, : 3 * HD].astype(BF).reshape(count, length, 3, HD)
-        gate = jax.nn.sigmoid(proj[:, 3 * HD :])
-        results = [
-            head_forward(
-                qkv[b, :, 0],
-                qkv[b, :, 1],
-                qkv[b, :, 2],
-                persist[layer, 0],
-                persist[layer, 1],
-                rates[layer],
-                segment_ids[b, 0],
-            )
-            for b in range(count)
-        ]
-        attended = jnp.concatenate([r[0] for r in results], 0).astype(BF).astype(F32)
-        recalled = jnp.concatenate([r[1] for r in results], 0).astype(BF).astype(F32)
-        combined = (attended + gate * recalled).astype(BF)
-        partial = jnp.dot(combined, out_w[layer], preferred_element_type=F32).astype(BF)
-        mid, normed_two = plane_call(
-            functools.partial(forward_kernel, False, False),
-            1 + 2 * layer,
-            (partial.reshape(count, length, D), rows, gains[layer, :, :, 1]),
-            {"own": own32, "full": full},
-            True,
-            True,
-        )
-        gate_up = jnp.dot(normed_two.reshape(flat, D), gu_w[layer], preferred_element_type=F32)
-        half = gate_up.shape[1] // 2
-        hidden = (jax.nn.silu(gate_up[:, :half]) * gate_up[:, half:]).astype(BF)
-        partial = jnp.dot(hidden, down_w[layer], preferred_element_type=F32).astype(BF)
-        kept.append(
-            (rows, normed, qkv, gate, [r[2] for r in results], recalled, combined, mid)
-            + (normed_two, gate_up, hidden)
-        )
-        last = layer == 1
-        found = plane_call(
-            functools.partial(forward_kernel, True, last),
-            2 + 2 * layer,
-            (partial.reshape(count, length, D), mid, gains[1, :, :, 0]),
-            {"own": own16, "full": full},
-            True,
-            not last,
-        )
-        outputs.append(found[0])
-        if not last:
-            rows = found[0].astype(F32)
-            normed = found[1]
-
-    grad_full = cot_full
-    grad_own = own_rows(cotangent)
-    pieces, gain_sums, memory_terms, grads = ([None] * 2, [None] * 2, [None] * 2, [None] * 2)
-    for layer in (1, 0):
-        (
-            rows,
-            normed,
-            qkv,
-            gate,
-            lse,
-            recalled,
-            combined,
-            mid,
-            normed_two,
-            gate_up,
-            hidden,
-        ) = kept[layer]
-        grad_f = grad_full.reshape(flat, D)
-        grad_hidden = jnp.dot(grad_f, down_w[layer].T, preferred_element_type=F32)
-        half = gate_up.shape[1] // 2
-        gate_part = gate_up[:, :half]
-        up_part = gate_up[:, half:]
-        sig_part = jax.nn.sigmoid(gate_part)
-        grad_gate_up = jnp.concatenate(
-            [
-                grad_hidden * up_part * sig_part * (1.0 + gate_part * (1.0 - sig_part)),
-                grad_hidden * gate_part * sig_part,
-            ],
-            1,
-        ).astype(BF)
-        partial = jnp.dot(grad_gate_up, gu_w[layer].T, preferred_element_type=F32).astype(BF)
-        grad_down = jnp.einsum("tf,td->fd", hidden, grad_f, preferred_element_type=F32)
-        grad_gu = jnp.einsum(
-            "td,tf->df", normed_two.reshape(flat, D), grad_gate_up, preferred_element_type=F32
-        )
-        halves_of_down = grad_down.astype(BF).reshape(nz, unit, 2, D // 2)
-        sent = (
-            grad_gu.astype(BF).reshape(nz, depth, 2 * nz * unit),
-            halves_of_down.transpose(0, 2, 1, 3).reshape(nz, 2 * unit, D // 2),
-        )
-        grad_mid, gain_two, branch, gu_sum, down_sum = plane_call(
-            functools.partial(backward_kernel, False, False),
-            5 + 2 * (1 - layer),
-            (partial.reshape(count, length, D), mid, gains[layer, :, :, 1], grad_own),
-            {"own": own32, "sums": sums, "full": full},
-            True,
-            True,
-            sent,
-        )
-        branch = branch.reshape(flat, D)
-        grad_combined = jnp.dot(branch, out_w[layer].T, preferred_element_type=F32)
-        grad_out = jnp.einsum("td,te->de", combined, branch, preferred_element_type=F32)
-        grad_attended = grad_combined.astype(BF).reshape(count, length, HD)
-        grad_recalled = (grad_combined * gate).astype(BF).reshape(count, length, HD)
-        grad_gate_pre = grad_combined * recalled * gate * (1.0 - gate)
-        found = [
-            head_backward(
-                qkv[b, :, 0],
-                qkv[b, :, 1],
-                qkv[b, :, 2],
-                persist[layer, 0],
-                persist[layer, 1],
-                rates[layer],
-                segment_ids[b, 0],
-                lse[b],
-                grad_attended[b],
-                grad_recalled[b],
-            )
-            for b in range(count)
-        ]
-        grad_heads = jnp.concatenate([jnp.concatenate(f[:3], 1) for f in found], 0)
-        grad_proj = jnp.concatenate([grad_heads, grad_gate_pre], 1).astype(BF)
-        memory_terms[layer] = (
-            jnp.stack([sum(f[3] for f in found), sum(f[4] for f in found)], 0),
-            sum(f[5] for f in found),
-        )
-        partial = jnp.dot(grad_proj, mix_w[layer].T, preferred_element_type=F32).astype(BF)
-        grad_mix = jnp.einsum(
-            "td,tf->df", normed.reshape(flat, D), grad_proj, preferred_element_type=F32
-        )
-        last = layer == 0
-        found = plane_call(
-            functools.partial(backward_kernel, last, True),
-            6 + 2 * (1 - layer),
-            (partial.reshape(count, length, D), rows, gains[layer, :, :, 0], grad_mid),
-            {"own": own16, "sums": sums, "full": full},
-            True,
-            not last,
-            (grad_mix.astype(BF).reshape(nz, depth, 4 * HD),),
-            grad_out.astype(BF),
-        )
-        grads[layer] = found[0]
-        gain_sums[layer] = jnp.concatenate([found[1], gain_two], 0)
-        if not last:
-            grad_own = found[0].astype(F32)
-            grad_full = found[2]
-        pieces[layer] = (found[-2], gu_sum, down_sum, found[-1])
-
-    memory_all = jnp.stack([m[0] for m in memory_terms], 0).reshape(-1, HD)
-    rate_all = jnp.pad(jnp.stack([m[1] for m in memory_terms])[None], ((0, 7), (0, HD - 2)))
+        of_layer[layer] |= dict(normed=normed, rows=rows)
+        found = forward_call(1 + layer, types.SimpleNamespace(**of_layer[layer]), layer == 1)
+        of_layer[layer] |= vars(found)
+        outputs.append(found.out_rows)
+        if layer == 0:
+            normed = found.normed_next
+            rows = found.out_rows.astype(F32)
+    given = dict(of_layer[1], grad_full=cot_full, grad_rows=own_rows(cotangent))
+    later = backward_call(3, types.SimpleNamespace(**given), False)
+    given = dict(
+        of_layer[0],
+        grad_full=later.grad_next,
+        grad_rows=later.grad_h.astype(F32),
+        early_mix=later.grad_mix,
+        early_out=later.grad_out,
+    )
+    earlier = backward_call(4, types.SimpleNamespace(**given), True)
+    by_layer = [
+        (earlier.grad_mix, earlier.gu_sum, earlier.down_sum, earlier.grad_out),
+        (earlier.mix_sum, later.gu_sum, later.down_sum, earlier.out_sum),
+    ]
+    both = (earlier, later)
+    grads = [found.grad_h for found in both]
+    gain_sums = [found.gains for found in both]
+
+    memory_all = jnp.stack([found.grad_persist for found in both], 0).reshape(-1, HD)
+    rate_all = jnp.stack([jnp.sum(found.grad_rate) for found in both])
+    rate_all = jnp.pad(rate_all[None], ((0, 7), (0, HD - 2)))
     gain_all = jnp.stack(gain_sums, 0).reshape(4, nz, 2, HD).transpose(1, 0, 2, 3)
     memory_all = jnp.concatenate([memory_all, rate_all], 0)
     small = jnp.concatenate(
         [jnp.broadcast_to(memory_all[None], (nz,) + memory_all.shape), gain_all.reshape(nz, 8, HD)],
         1,
     )
-    by_layer = [(*pieces[layer], outputs[layer], grads[layer]) for layer in range(2)]
+    by_layer = [(*by_layer[layer], outputs[layer], grads[layer]) for layer in range(2)]
     mix_all, gu_all, down_all, out_all, rows_got, grads_got, plane_all = final_call(
-        9, by_layer, small
+        5, by_layer, small
     )
 
     def whole_rows(of_layer, got):
@@ -1249,14 +1572,14 @@
 
     section_out = whole_rows(outputs, rows_got)
     section_grad = whole_rows(grads, grads_got).astype(F32)
-    grad_mix, grad_gu, grad_down = assemble_call(mix_all, gu_all, down_all)
+    grad_mix, grad_gu, grad_down = assemble_call(unit, mix_all, gu_all, down_all)
     grad_out = out_all.astype(F32).reshape(1, 2 * HD, D)
 
     heads_of = lax.dynamic_slice_in_dim(plane_all, 2 * s, 2, 0)
-    of_layer = lax.dynamic_index_in_dim(
+    of_section = lax.dynamic_index_in_dim(
         heads_of[:, :64].reshape(2, 2, 2, -1, HD), x, 1, keepdims=False
     )
-    grad_persist = of_layer.transpose(1, 2, 0, 3).reshape(1, 2, -1, 2 * HD)
+    grad_persist = of_section.transpose(1, 2, 0, 3).reshape(1, 2, -1, 2 * HD)
     grad_rate = lax.dynamic_index_in_dim(heads_of[:, 64], x, 1, keepdims=False)[None]
     gain_all = jnp.sum(plane_all[:, 72:], 0).reshape(2, 2, depth)
     grad_gain = lax.dynamic_index_in_dim(gain_all, x, 0).transpose(0, 2, 1)

time: 686 us -> 574 us (0.84)
  matrix products: 101 us -> 0 us
  local copies, waits for them, and re-layouts: 65.3 us -> 25.3 us
  Pallas kernels: 390 us -> 418 us
    dot_general x92 -> x0, matrix products: 101 us -> none  [the longest x2 9.3 us: tensor_parallel(): jnp.dot(normed_two.reshape(flat, D), gu_w[layer], preferred_element_type=...]
    unnamed x326 -> x43, local copies, waits for them, and re-layouts: 41.5 us -> 9.26 us
    pallas_call x11 -> x7, Pallas kernels: 390 us -> 418 us  [the longest x6 412 us: kernel_call(): pl.pallas_call(kernel, out_shape=outs, in_specs=[vmem] * len(operands), o...]
    reshape x7 -> x3, local copies, waits for them, and re-layouts: 8.83 us -> 0.98 us  [the longest x1 0.64 us: tensor_parallel(): grad_persist = of_section.transpose(1, 2, 0, 3).reshape(1, 2, -1, 2 * HD)]
  transfers between devices with their start and end apart: 11 -> 11, of which waited for: 2 -> 2; matrix products, arithmetic and copies ran while one was open for 9% -> 4% of each run, Pallas kernels for 17% -> 27%
where the time goes in v3:
time: 574 us; the launch traced here: 568 us
  Pallas kernels  418 us (73%)
  blocking collectives  64.6 us (11%)
  local copies, waits for them, and re-layouts  25.3 us (4%)
  other arithmetic  21.8 us (4%)
  waiting for transfers between devices  17.2 us (3%)
  between operations  16.8 us (3%)
    pallas_call x6, Pallas kernels, kernel_call(): pl.pallas_call(kernel, out_shape=outs, in_specs=[vmem] * len(operands), o...  412 us
    all_gather x2, blocking collectives, tensor_parallel(): lax.all_gather(part[layer], 'shard', axis=0, tiled=True)  48.9 us
    all_gather x1, blocking collectives, tensor_parallel(): lax.all_gather(norm_gains[0], ('section', 'shard'), axis=0, tiled=True)  15.6 us
    ppermute x3, waiting for transfers between devices, tensor_parallel(): lax.ppermute(g, 'section', swap)  15 us
  transfers between devices with their start and end apart: 11, of which 2 were waited for; matrix products, arithmetic and copies ran while one was open for 4% of the time, Pallas kernels for 27%

profile of v3, /device:TPU:3, one launch (start us, length us, event | category | flops | bytes accessed | tf_op | source)
XLA Modules:
  0.0 568.0 jit_solution(7680199772949959259)
XLA Ops:
  13.3 2.1 copy.88
  15.4 3.3 dynamic-slice_reduce_fusion.1
  18.9 7.8 %collective-permute-done.2 = bf16[256,512]{1,0:T(8,128)(2,1)S(1)} collective-permute-done((bf16[256,512]{1,0:T(8,128)(2,1)S(1)}, bf16[256,512]{1,0:T(8,128)(2,1)S(1)}, u32[]{:S(2)}, u32[]{:S(2)}) %collective-permute-start.2) | collective-permute-done | bytes 262176 | tf_op jit(solution)/shard_map/ppermute | solution.py:1478
  27.6 3.1 copy.66
  31.7 1.4 collective-permute-start
  34.4 7.2 %collective-permute-done = bf16[256,768]{1,0:T(8,128)(2,1)S(1)} collective-permute-done((bf16[256,768]{1,0:T(8,128)(2,1)S(1)}, bf16[256,768]{1,0:T(8,128)(2,1)S(1)}, u32[]{:S(2)}, u32[]{:S(2)}) %collective-permute-start) | collective-permute-done | bytes 393248 | tf_op jit(solution)/shard_map/ppermute | solution.py:1478
  45.9 2.1 collective-permute-start.1
  47.9 15.6 %all-gather = bf16[1,2048,2]{1,2,0:T(2,128)(2,1)S(1)} all-gather(bf16[1,256,2]{1,2,0:T(2,128)(2,1)S(1)} %copy-done.17), channel_id=2, replica_groups=mesh['section'=2,'seq'=4,'shard'=4] {'section','shard'}, dimensions={1}, use_global_device_ids=true | all-gather | bytes 9216 | tf_op jit(solution)/shard_map/all_gather | solution.py:1499
  66.1 24.0 %shard_map.169.refs_0_.refs_3_ = bf16[2,512,1024]{2,1,0:T(8,128)(2,1)} custom-call(f32[2,64,1024]{2,1,0:T(8,128)} %bitcast_convert_fusion.2.rows_ref.refs_1_.refs_2_, f32[1,1024]{1,0:T(1,128)} %get-tuple-element.166.gain_ref.refs_4_), custom_call_target="tpu_custom_call" | custom-call | tf_op jit(solution)/shard_map/pallas_call | solution.py:1284
  93.7 29.3 %all_gather.36.refs_5_.refs_7_ = bf16[384,1024]{1,0:T(8,128)(2,1)} all-gather(bf16[96,1024]{1,0:T(8,128)(2,1)S(1)} %get-tuple-element.158), channel_id=1, replica_groups=mesh['section'=2,'seq'=4,'shard'=4] {'shard'}, dimensions={0}, use_global_device_ids=true | all-gather | bytes 983040 | tf_op jit(solution)/shard_map/all_gather | solution.py:1489
  124.6 19.7 %all_gather.42.refs_5_.refs_7_ = bf16[384,1024]{1,0:T(8,128)(2,1)} all-gather(bf16[96,1024]{1,0:T(8,128)(2,1)S(1)} %get-tuple-element.157), channel_id=1, replica_groups=mesh['section'=2,'seq'=4,'shard'=4] {'shard'}, dimensions={0}, use_global_device_ids=true | all-gather | bytes 983040 | tf_op jit(solution)/shard_map/all_gather | solution.py:1489
  144.3 1.8 bitcast_select_fusion.2
  146.1 75.8 %shard_map.170 = (bf16[2,512,384]{2,1,0:T(8,128)(2,1)}, f32[2,512,128]{2,1,0:T(8,128)}, bf16[2,512,128]{2,1,0:T(8,128)(2,1)}, bf16[2,512,128]{2,1,0:T(8,128)(2,1...) custom-call(bf16[2,512,1024]{2,1,0:T(8,128)(2,1)} %shard_map.169.ref, ...), custom_call_target="tpu_custom_call" | custom-call | tf_op jit(solution)/shard_map/pallas_call | solution.py:1284
  221.9 1.8 convert_element_type.48.refs_1_.refs_2_
  223.7 51.8 %shard_map.171 = (bf16[2,512,384]{2,1,0:T(8,128)(2,1)}, f32[2,512,128]{2,1,0:T(8,128)}, bf16[2,512,128]{2,1,0:T(8,128)(2,1)}, bf16[2,512,128]{2,1,0:T(8,128)(2,1...) custom-call(bf16[2,512,1024]{2,1,0:T(8,128)(2,1)} %get-tuple-element, ...), custom_call_target="tpu_custom_call" | custom-call | tf_op jit(solution)/shard_map/pallas_call | solution.py:1284
  275.5 90.6 %shard_map.172 = (bf16[4,256,512]{2,1,0:T(8,128)(2,1)}, bf16[128,1024]{1,0:T(8,128)(2,1)}, f32[2,1024]{1,0:T(2,128)}, f32[2,16,128]{2,1,0:T(8,128)}, f32[1,512]{...) custom-call(bf16[2,512,1024]{2,1,0:T(8,128)(2,1)} %bitcast.106, ...), custom_call_target="tpu_custom_call" | custom-call | tf_op jit(solution)/shard_map/pallas_call | solution.py:1284
  366.1 1.8 convert_element_type.51.refs_1_
  367.9 97.4 %shard_map.173 = (bf16[4,256,512]{2,1,0:T(8,128)(2,1)}, bf16[128,1024]{1,0:T(8,128)(2,1)}, f32[2,1024]{1,0:T(2,128)}, f32[2,16,128]{2,1,0:T(8,128)}, f32[1,512]{...) custom-call(bf16[2,512,1024]{2,1,0:T(8,128)(2,1)} %get-tuple-element, ...), custom_call_target="tpu_custom_call" | custom-call | tf_op jit(solution)/shard_map/pallas_call | solution.py:1284
  465.3 1.3 reduce_sum.27
  468.7 1.4 maximum_bitcast_fusion.2
  470.8 72.6 %shard_map.174 = (bf16[2,4,256,512]{3,2,1,0:T(8,128)(2,1)}, bf16[2,4,256,768]{3,2,1,0:T(8,128)(2,1)}, bf16[2,4,96,1024]{3,2,1,0:T(8,128)(2,1)}, bf16[2,128,1024]...) custom-call(bf16[4,256,512]{2,1,0:T(8,128)(2,1)} %get-tuple-element.80.refs_, ...), custom_call_target="tpu_custom_call" | custom-call | tf_op jit(solution)/shard_map/pallas_call | solution.py:1284
  551.4 1.4 dynamic-slice_reduce_fusion.2
  552.8 1.9 copy-done.2
  554.7 5.6 shard_map.175
  (114 shorter events, 30.4 us)
Async XLA Ops:
  8.0 83.0 %all-reduce.8.cloned.1.call-start = ((), (), s32[]{:S(2)}) async-start(), calls=%async_computation.6 | async-start | bytes 532480
  12.4 110.5 %all-gather.14.cloned.1.call-start = ((), (), s32[]{:S(2)}) async-start(), calls=%async_computation.2 | async-start | bytes 1310720 | tf_op jit(solution)/shard_map/all_gather | solution.py:1482
  13.3 132.8 %all-gather.12.cloned.1.call-start = ((), (), s32[]{:S(2)}) async-start(), calls=%async_computation.1 | async-start | bytes 1310720 | tf_op jit(solution)/shard_map/all_gather | solution.py:1489
  18.8 7.8 %collective-permute-start.2 = (bf16[256,512]{1,0:T(8,128)(2,1)S(1)}, bf16[256,512]{1,0:T(8,128)(2,1)S(1)}, u32[]{:S(2)}, u32[]{:S(2)}) collective-permute-start(bf16[256,512]{1,0:T(8,128)(2,1)S(1)} %bitcast.115), channel_id=1, source_target_pairs={{0,16},{16,0},{1,17},{17,1},{2,18},{18,2},{3,19},{19,3},{4,20},{20... | collective-permute-start | bytes 786440 | tf_op jit(solution)/shard_map/ppermute | solution.py:1478
  27.5 118.6 %all-gather.10.cloned.1.call-start = ((), (), s32[]{:S(2)}) async-start(), calls=%async_computation | async-start | bytes 1966080 | tf_op jit(solution)/shard_map/all_gather | solution.py:1489
  31.7 9.9 %collective-permute-start = (bf16[256,768]{1,0:T(8,128)(2,1)S(1)}, bf16[256,768]{1,0:T(8,128)(2,1)S(1)}, u32[]{:S(2)}, u32[]{:S(2)}) collective-permute-start(bf16[256,768]{1,0:T(8,128)(2,1)S(1)} %copy.67), channel_id=1, source_target_pairs={{0,16},{16,0},{1,17},{17,1},{2,18},{18,2},{3,19},{19,3},{4,20},{20... | collective-permute-start | bytes 1179656 | tf_op jit(solution)/shard_map/ppermute | solution.py:1478
  34.3 13.6 %copy-start.17 = (bf16[1,256,2]{1,2,0:T(2,128)(2,1)S(1)}, bf16[1,256,2]{1,2,0:T(2,128)(2,1)}, u32[]{:S(2)}) copy-start(bf16[1,256,2]{1,2,0:T(2,128)(2,1)} %param.17) | copy-start | bytes 3076
  34.4 29.3 %copy-start.13 = (s32[2,1,512]{2,1,0:T(1,128)S(1)}, s32[2,1,512]{2,1,0:T(1,128)}, u32[]{:S(2)}) copy-start(s32[2,1,512]{2,1,0:T(1,128)} %refs_14_.3) | copy-start | bytes 12292
  34.4 30.3 %copy-start.12 = (bf16[2,1,128,1024]{3,2,1,0:T(8,128)(2,1)S(1)}, bf16[2,1,128,1024]{3,2,1,0:T(8,128)(2,1)}, u32[]{:S(2)}) copy-start(bf16[2,1,128,1024]{3,2,1,0:T(8,128)(2,1)} %param.10) | copy-start | bytes 1572868
  42.6 181.1 %all-gather.18.cloned.1.call-start = ((), (), s32[]{:S(2)}) async-start(), calls=%async_computation.4 | async-start | bytes 1310720 | tf_op jit(solution)/shard_map/all_gather | solution.py:1489
  43.3 180.4 %all-gather.16.cloned.1.call-start = ((), (), s32[]{:S(2)}) async-start(), calls=%async_computation.3 | async-start | bytes 1966080 | tf_op jit(solution)/shard_map/all_gather | solution.py:1489
  44.1 231.5 %all-gather.20.cloned.1.call-start = ((), (), s32[]{:S(2)}) async-start(), calls=%async_computation.5 | async-start | bytes 2621440 | tf_op jit(solution)/shard_map/all_gather | solution.py:1505
  45.9 44.3 %copy-start.7 = (bf16[2,1,128,1024]{3,2,1,0:T(8,128)(2,1)S(1)}, bf16[2,1,128,1024]{3,2,1,0:T(8,128)(2,1)}, u32[]{:S(2)}) copy-start(bf16[2,1,128,1024]{3,2,1,0:T(8,128)(2,1)} %param.12) | copy-start | bytes 1572868
  45.9 47.7 %collective-permute-start.1 = (bf16[96,1024]{1,0:T(8,128)(2,1)S(1)}, bf16[96,1024]{1,0:T(8,128)(2,1)S(1)}, u32[]{:S(2)}, u32[]{:S(2)}) collective-permute-start(bf16[96,1024]{1,0:T(8,128)(2,1)S(1)} %pad.21), channel_id=1, source_target_pairs={{0,16},{16,0},{1,17},{17,1},{2,18},{18,2},{3,19},{19,3},{4,20},{20... | collective-permute-start | bytes 589832 | tf_op jit(solution)/shard_map/ppermute | solution.py:1478
  123.9 20.4 %collective-permute-start.3 = (bf16[128,1024]{1,0:T(8,128)(2,1)S(1)}, bf16[128,1024]{1,0:T(8,128)(2,1)S(1)}, u32[]{:S(2)}, u32[]{:S(2)}) collective-permute-start(bf16[128,1024]{1,0:T(8,128)(2,1)S(1)} %dynamic-slice_bitcast_fusion.2), channel_id=1, source_target_pairs={{0,16},{16,0},{1,17},{17,1},{2,18},{18,2},{3,19},{19,3},{4,20},{20... | collective-permute-start | bytes 786440 | tf_op jit(solution)/shard_map/ppermute | solution.py:1484
  367.9 98.7 %copy-start.16 = (f32[1,512]{1,0:T(1,128)S(1)}, f32[1,512]{1,0:T(1,128)}, u32[]{:S(2)}) copy-start(f32[1,512]{1,0:T(1,128)} %get-tuple-element.92) | copy-start | bytes 6148
  367.9 99.3 %copy-start.15 = (f32[2,1024]{1,0:T(2,128)S(1)}, f32[2,1024]{1,0:T(2,128)}, u32[]{:S(2)}) copy-start(f32[2,1024]{1,0:T(2,128)} %get-tuple-element.94) | copy-start | bytes 24580
  367.9 100.1 %copy-start.14 = (f32[2,16,128]{2,1,0:T(8,128)S(1)}, f32[2,16,128]{2,1,0:T(8,128)}, u32[]{:S(2)}) copy-start(f32[2,16,128]{2,1,0:T(8,128)} %get-tuple-element.90) | copy-start | bytes 49156
  470.8 72.6 %copy-start.6 = (bf16[2,64,1024]{2,1,0:T(8,128)(2,1)S(1)}, bf16[2,64,1024]{2,1,0:T(8,128)(2,1)}, u32[]{:S(2)}) copy-start(bf16[2,64,1024]{2,1,0:T(8,128)(2,1)} %get-tuple-element.69.refs_11_) | copy-start | bytes 786436
  470.8 72.6 %copy-start.10 = (bf16[2,64,1024]{2,1,0:T(8,128)(2,1)S(1)}, bf16[2,64,1024]{2,1,0:T(8,128)(2,1)}, u32[]{:S(2)}) copy-start(bf16[2,64,1024]{2,1,0:T(8,128)(2,1)} %get-tuple-element.84.refs_5_) | copy-start | bytes 786436
  470.8 73.7 %copy-start.5 = (bf16[2,64,1024]{2,1,0:T(8,128)(2,1)S(1)}, bf16[2,64,1024]{2,1,0:T(8,128)(2,1)}, u32[]{:S(2)}) copy-start(bf16[2,64,1024]{2,1,0:T(8,128)(2,1)} %get-tuple-element.57.refs_4_) | copy-start | bytes 786436
  470.8 73.7 %copy-start.9 = (bf16[2,64,1024]{2,1,0:T(8,128)(2,1)S(1)}, bf16[2,64,1024]{2,1,0:T(8,128)(2,1)}, u32[]{:S(2)}) copy-start(bf16[2,64,1024]{2,1,0:T(8,128)(2,1)} %get-tuple-element.59.refs_10_) | copy-start | bytes 786436
  545.5 7.3 %copy-start.3 = (bf16[2,4,256,512]{3,2,1,0:T(8,128)(2,1)S(1)}, bf16[2,4,256,512]{3,2,1,0:T(8,128)(2,1)}, u32[]{:S(2)}) copy-start(bf16[2,4,256,512]{3,2,1,0:T(8,128)(2,1)} %get-tuple-element.97.mix_buf) | copy-start | bytes 6291460
  552.8 7.6 %copy-start.1 = (bf16[1,256,1024]{2,1,0:T(8,128)(2,1)S(1)}, bf16[1,256,1024]{2,1,0:T(8,128)(2,1)}, u32[]{:S(2)}) copy-start(bf16[1,256,1024]{2,1,0:T(8,128)(2,1)} %param.14) | copy-start | bytes 1572868
  (5 other events, 13.1 us)
Sparse Core Ops, SparseCore 0:
  12.6 54.3 all-reduce.7
Sparse Core Ops, SparseCore 1:
  14.5 28.7 all-gather.13
  44.7 27.3 all-gather.11
  74.1 49.0 all-gather.9
  124.7 33.6 all-gather.17
  160.6 35.1 all-gather.15
  197.4 28.2 all-gather.19

commit v4 on v3

--- a/solution.py
+++ b/solution.py
@@ -680,6 +680,11 @@
     return lax.dot_general(left, right, (((0,), (0,)), ((), ())), preferred_element_type=F32)
 
 
+def flat(ref):
+    value = ref[...]
+    return value.reshape(-1, value.shape[-1])
+
+
 def in_blocks(length, size, body):
     def step(index, carry):
         body(pl.ds(pl.multiple_of(index * size, size), size), index * size)
@@ -708,30 +713,62 @@
     return inner, decay_w, distance, seq_exp * share, per_exp * share
 
 
-def start_kernel(rows_ref, gain_ref, full_ref, gsend, grecv):
-    meet()
-    gathers = [Gather(full_ref, batch, gsend, grecv) for batch in range(2)]
-    for batch, gather in enumerate(gathers):
-        rows = rows_ref[batch]
-        gather.start((rows * rms_scale(rows) * gain_ref[...]).astype(BF))
-    for gather in gathers:
-        gather.forward()
-    for gather in gathers:
-        gather.finish()
+class SetupIn(NamedTuple):
+    inputs: Any
+    small: Any
+    gain_rows: Any
+    w_mix: Any
+    w_out: Any
+    w_gu: Any
+    w_down: Any
+
+
+class SetupOut(NamedTuple):
+    rows: Any
+    normed: Any
+    gains: Any
+    persist: Any
+    rates: Any
+    mix: Any
+    mix_next: Any
+    out: Any
+    out_next: Any
+    gu: Any
+    gu_next: Any
+    down: Any
+    down_next: Any
+
+
+class SetupScratch(NamedTuple):
+    gain_all: Any
+    small_all: Any
+    mix_away: Any
+    gu_away: Any
+    down_away: Any
+    zsend: Any
+    zrecv: Any
+    psend: Any
+    precv: Any
+    xsend: Any
+    xrecv: Any
+    gsend: Any
+    grecv: Any
+    csend: Any
+    crecv: Any
+    rsend: Any
+    rrecv: Any
 
 
 class ForwardIn(NamedTuple):
     normed: Any
     rows: Any
-    gain_two: Any
-    gain_next: Any
-    gu: Any
-    down: Any
+    gu_block: Any
+    down_block: Any
+    gains: Any
     mix: Any
     out: Any
-    pkeys: Any
-    pvalues: Any
-    rate: Any
+    persist: Any
+    rates: Any
     seg_rows: Any
     seg_cols: Any
 
@@ -745,8 +782,30 @@
     normed_two: Any
     gate_up: Any
     hidden: Any
+    gu: Any
+    down: Any
     out_rows: Any
     normed_next: Any
+
+
+class ForwardScratch(NamedTuple):
+    csend: Any
+    crecv: Any
+
+
+class NextIn(NamedTuple):
+    mix_block: Any
+    out_block: Any
+
+
+class NextWeights(NamedTuple):
+    mix_next: Any
+    out_next: Any
+
+
+class NextScratch(NamedTuple):
+    rsend: Any
+    rrecv: Any
 
 
 class BackwardIn(NamedTuple):
@@ -754,15 +813,13 @@
     grad_rows: Any
     rows: Any
     normed: Any
-    gain_one: Any
-    gain_two: Any
     gu: Any
     down: Any
+    gains: Any
     mix: Any
     out: Any
-    pkeys: Any
-    pvalues: Any
-    rate: Any
+    persist: Any
+    rates: Any
     seg_rows: Any
     seg_cols: Any
     qkv: Any
@@ -778,7 +835,7 @@
 class BackwardOut(NamedTuple):
     grad_mix: Any
     grad_out: Any
-    gains: Any
+    gain_sums: Any
     grad_persist: Any
     grad_rate: Any
     gu_sum: Any
@@ -841,14 +898,307 @@
     return types.SimpleNamespace(**dict(zip(names, refs, strict=True)))
 
 
-def forward_layer(ins, outs, *refs):
-    r = named(ins + outs + fields(PlaneScratch), refs)
+def remote(source, landing, sems, index, target):
+    return pltpu.make_async_remote_copy(
+        src_ref=source,
+        dst_ref=landing,
+        send_sem=sems[0].at[index],
+        recv_sem=sems[1].at[index],
+        device_id=target,
+        device_id_type=MESH,
+    )
+
+
+class ColumnGather:
+    def __init__(self, full, send, recv, index):
+        self.place = here()
+        self.full, self.send, self.recv, self.index = full, send, recv, index
+
+    def copy(self, block, down):
+        x, s, z = self.place
+        return pltpu.make_async_remote_copy(
+            src_ref=self.full.at[block],
+            dst_ref=self.full.at[block],
+            send_sem=self.send.at[self.index, down, block],
+            recv_sem=self.recv.at[self.index, block],
+            device_id=(x, s, (z + 3) % 4 if down else (z + 1) % 4),
+            device_id_type=MESH,
+        )
+
+    def at_each(self, body):
+        for at in range(4):
+
+            @pl.when(self.place[2] == at)
+            def _():
+                body(at)
+
+    def start(self):
+        def body(at):
+            for down in (0, 1):
+                if at != 3 * (1 - down):
+                    self.copy(at, down).start()
+
+        self.at_each(body)
+
+    def hop(self, number):
+        def body(at):
+            if at - number >= 0:
+                self.copy(at - number, 0).wait_recv()
+                if at < 3:
+                    self.copy(at - number, 0).start()
+            if at + number <= 3:
+                self.copy(at + number, 1).wait_recv()
+                if at > 0:
+                    self.copy(at + number, 1).start()
+
+        self.at_each(body)
+
+    def finish(self):
+        self.hop(3)
+
+        def body(at):
+            for block in range(4):
+                if block <= at < 3:
+                    self.copy(block, 0).wait_send()
+                if block >= at > 0:
+                    self.copy(block, 1).wait_send()
+
+        self.at_each(body)
+
+
+class RootGather:
+    def __init__(self, block, send, recv):
+        self.place = here()
+        x, s, z = self.place
+        self.away = z - (2 * x + s // 2)
+        self.block, self.send, self.recv = block, send, recv
+
+    def copy(self, down):
+        x, s, z = self.place
+        return pltpu.make_async_remote_copy(
+            src_ref=self.block,
+            dst_ref=self.block,
+            send_sem=self.send.at[down],
+            recv_sem=self.recv.at[0],
+            device_id=(x, s, (z + 3) % 4 if down else (z + 1) % 4),
+            device_id_type=MESH,
+        )
+
+    def sends(self, down):
+        z = self.place[2]
+        return (self.away <= 0) & (z > 0) if down else (self.away >= 0) & (z < 3)
+
+    def start(self):
+        for down in (0, 1):
+
+            @pl.when((self.away == 0) & self.sends(down))
+            def _():
+                self.copy(down).start()
+
+    def hop(self, number):
+        for down in (0, 1):
+
+            @pl.when(self.away == (-number if down else number))
+            def _():
+                self.copy(down).wait_recv()
+
+                @pl.when(self.sends(down))
+                def _():
+                    self.copy(down).start()
+
+    def finish(self):
+        self.hop(3)
+        for down in (0, 1):
+
+            @pl.when(self.sends(down))
+            def _():
+                self.copy(down).wait_send()
+
+
+def setup_kernel(unit, *refs):
+    r = named(fields(SetupIn, SetupOut, SetupScratch), refs)
+    place = here()
+    x, s, z = place
+    size = r.rows.shape[1]
+    partner = peer(place, 1, False)
+    flips = [(dx, ds) for dx in (0, 1) for ds in range(4) if dx or ds]
+    plane = [((x + dx) % 2, (s + ds) % 4, z) for dx, ds in flips]
+    column = [(x, s, (z + dz) % 4) for dz in (1, 2, 3)]
+    barrier = pltpu.get_barrier_semaphore()
+    for other in plane + column:
+        pl.semaphore_signal(barrier, inc=1, device_id=other, device_id_type=MESH)
+    pl.semaphore_wait(barrier, len(plane) + len(column))
+
+    zsems, psems, xsems = (r.zsend, r.zrecv), (r.psend, r.precv), (r.xsend, r.xrecv)
+    for dz in (1, 2, 3):
+        remote(r.gain_rows, r.gain_all.at[0, z], zsems, dz - 1, column[dz - 1]).start()
+    r.gain_all[0, z] = r.gain_rows[...]
+    for index in range(7):
+        remote(r.small, r.small_all.at[x, s], psems, index, plane[index]).start()
+    r.small_all[x, s] = r.small[...]
+
+    mine, other = x * 4 + s, (1 - x) * 4 + s
+
+    def mix_part(which):
+        heads = [pl.ds(pl.multiple_of(kind * D + which * HD, HD), HD) for kind in range(4)]
+        return jnp.concatenate([r.w_mix[0, :, cols] for cols in heads], 1)
+
+    out_rows = pl.ds(pl.multiple_of(s % 2 * HD, HD), HD)
+    root = z == 2 * x + s // 2
+    rooted = z == 2 * (1 - x) + s // 2
+    mixes = (r.mix.at[z], r.mix_next)
+    outs = (r.out, r.out_next)
+    gus = (r.gu, r.gu_next)
+    downs = (r.down, r.down_next)
+    for layer in (0, 1):
+
+        @pl.when(x == layer)
+        def _():
+            r.mix_away[...] = mix_part(other)
+            remote(r.mix_away, mixes[layer], xsems, 0, partner).start()
+            mixes[layer][...] = mix_part(mine)
+
+            @pl.when(rooted)
+            def _():
+                remote(r.w_out.at[0, out_rows], outs[layer], xsems, 1, partner).start()
+
+            @pl.when(root)
+            def _():
+                outs[layer][...] = r.w_out[0, out_rows, :]
+
+    for dz in (1, 2, 3):
+        remote(r.gain_rows, r.gain_all.at[0, z], zsems, dz - 1, column[dz - 1]).wait_recv()
+    remote(r.gain_all.at[0], r.gain_all.at[1], xsems, 4, partner).start()
+
+    padded = r.down_away.shape[0]
+    width = 8 * unit + 64
+
+    def select(which, offset):
+        begin = lax.broadcasted_iota(jnp.int32, (width, 128), 0) - offset
+        col = lax.broadcasted_iota(jnp.int32, (width, 128), 1)
+        return jnp.where((begin == which * unit + col) & (col < unit), 1.0, 0.0).astype(BF)
+
+    def gu_part(which, out):
+        for owner in range(4):
+            base = owner * 8 * unit
+            offset = base % 128
+            chosen = select(which, offset)
+            for side in range(2):
+                begin = side * FF + base - offset
+                part = nn(r.w_gu[0, :, begin : begin + width], chosen).astype(BF)
+                at = side * 4 * padded + owner * padded
+                out[:, at : at + padded] = part[:, :padded]
+
+    def down_part(which, out):
+        row = lax.broadcasted_iota(jnp.int32, (padded, 8 * unit), 0)
+        col = lax.broadcasted_iota(jnp.int32, (padded, 8 * unit), 1)
+        chosen = jnp.where((col == which * unit + row) & (row < unit), 1.0, 0.0).astype(BF)
+        out[...] = nn(chosen, r.w_down[0]).astype(BF)
+
+    gu_part(other, r.gu_away)
+    down_part(other, r.down_away)
+    for layer in (0, 1):
+
+        @pl.when(x == layer)
+        def _():
+            remote(r.gu_away, gus[layer], xsems, 2, partner).start()
+            remote(r.down_away, downs[layer], xsems, 3, partner).start()
+
+    remote(r.gain_all.at[0], r.gain_all.at[1], xsems, 4, partner).wait_recv()
+    for place_of, layer in ((0, x), (1, 1 - x)):
+        for owner in range(4):
+            for kind in range(2):
+                for half in range(2):
+                    begin = owner * 2 * HD + half * HD
+                    row = 2 * kind + half
+                    r.gains[layer, kind : kind + 1, begin : begin + HD] = r.gain_all[
+                        place_of, owner, row : row + 1, :
+                    ]
+    gathers = [Gather(r.normed, batch, r.gsend, r.grecv) for batch in range(2)]
+    for batch, gather in enumerate(gathers):
+        rows = r.inputs[batch, 0, pl.ds(pl.multiple_of(x * size, size), size), :]
+        r.rows[batch] = rows
+        rows = rows.astype(F32)
+        gather.start((rows * rms_scale(rows) * r.gains[0, 0:1, :]).astype(BF))
+
+    remote(r.mix_away, r.mix_next, xsems, 0, partner).wait_recv()
+
+    @pl.when(root)
+    def _():
+        remote(r.out, r.out_next, xsems, 1, partner).wait_recv()
+
+    columns = [ColumnGather(r.mix, r.csend, r.crecv, 0), RootGather(r.out, r.rsend, r.rrecv)]
+    for part in columns:
+        part.start()
+    for layer in (0, 1):
+
+        @pl.when(x == layer)
+        def _():
+            gu_part(mine, gus[layer])
+            down_part(mine, downs[layer])
+
+    for part in columns:
+        part.hop(1)
+    for gather in gathers:
+        gather.forward()
+    for part in columns:
+        part.hop(2)
+    for index in range(7):
+        dx, ds = flips[index]
+        landing = r.small_all.at[(x + dx) % 2, (s + 4 - ds) % 4]
+        remote(r.small, landing, psems, index, plane[index]).wait_recv()
+    holder = 2 * x + s // 2
+    for layer in range(2):
+        begin = pl.multiple_of(s % 2 * 32, 32)
+        rows = r.small_all[layer, holder, pl.ds(begin, 32), :]
+        r.persist[layer] = rows.astype(BF).reshape(2, 16, HD)
+        begin = pl.multiple_of(64 + s % 2 * 8, 8)
+        r.rates[layer] = r.small_all[layer, holder, pl.ds(begin, 8), :]
+    for gather in gathers:
+        gather.finish()
+    for part in columns:
+        part.finish()
+    remote(r.gu_away, r.gu_next, xsems, 2, partner).wait()
+    remote(r.down_away, r.down_next, xsems, 3, partner).wait()
+    remote(r.mix_away, r.mix_next, xsems, 0, partner).wait_send()
+    remote(r.gain_all.at[0], r.gain_all.at[1], xsems, 4, partner).wait_send()
+
+    @pl.when(rooted)
+    def _():
+        remote(r.out, r.out_next, xsems, 1, partner).wait_send()
+
+    for dz in (1, 2, 3):
+        remote(r.gain_rows, r.gain_all.at[0, z], zsems, dz - 1, column[dz - 1]).wait_send()
+    for index in range(7):
+        remote(r.small, r.small_all.at[x, s], psems, index, plane[index]).wait_send()
+
+
+def forward_layer(layer, ins, outs, *refs):
+    scratch = fields(PlaneScratch, ForwardScratch)
+    last = len(ins) == len(ForwardIn._fields)
+    if not last:
+        scratch += NextScratch._fields
+    r = named(ins + outs + scratch, refs)
     length = r.part.shape[1]
-    last = not hasattr(r, "normed_next")
+    z = lax.axis_index("shard")
+    own = [
+        ColumnGather(r.gu, r.csend, r.crecv, 0),
+        ColumnGather(r.down, r.csend, r.crecv, 1),
+    ]
+    following = []
+    if not last:
+        following = [
+            ColumnGather(r.mix_next, r.csend, r.crecv, 2),
+            RootGather(r.out_next, r.rsend, r.rrecv),
+        ]
+
+    def each(parts, act):
+        for part in parts:
+            act(part)
 
     def project(batch):
         def block(rows, begin):
-            proj = nn(r.normed[batch, rows, :], r.mix[...])
+            proj = nn(r.normed[batch, rows, :], flat(r.mix))
             r.qkv[batch, rows, :] = proj[:, : 3 * HD].astype(BF)
             r.gate[batch, rows, :] = jax.nn.sigmoid(proj[:, 3 * HD :])
 
@@ -860,13 +1210,13 @@
             inner, decay_w, _, probs, per_probs = weights_of_scores(
                 r.qkv[batch, rows, :HD],
                 r.qkv[batch, :, HD : 2 * HD],
-                r.pkeys[...],
+                r.persist[layer, 0],
                 r.seg_rows[batch, rows, :],
                 r.seg_cols[batch],
                 begin,
-                r.rate[...],
+                r.rates[layer, 0:1, 0:1],
             )
-            attended = nn(probs.astype(BF), values) + nn(per_probs.astype(BF), r.pvalues[...])
+            attended = nn(probs.astype(BF), values) + nn(per_probs.astype(BF), r.persist[layer, 1])
             recalled = nn((inner * decay_w).astype(BF), values).astype(BF)
             r.recalled[batch, rows, :] = recalled
             combined = attended.astype(BF).astype(F32)
@@ -879,12 +1229,12 @@
 
     def feed(batch):
         def block(rows, begin):
-            gate_up = nn(r.normed_two[batch, rows, :], r.gu[...])
+            gate_up = nn(r.normed_two[batch, rows, :], flat(r.gu))
             r.gate_up[batch, rows, :] = gate_up
             half = gate_up.shape[1] // 2
             hidden = (jax.nn.silu(gate_up[:, :half]) * gate_up[:, half:]).astype(BF)
             r.hidden[batch, rows, :] = hidden
-            r.part[batch, rows, :] = nn(hidden, r.down[...]).astype(BF)
+            r.part[batch, rows, :] = nn(hidden, flat(r.down)).astype(BF)
 
         in_blocks(length, 256, block)
 
@@ -893,10 +1243,20 @@
 
     def send_normed(batch, own, gain, full):
         gather = Gather(full, batch, r.gsend, r.grecv)
-        gather.start((own * rms_scale(own) * gain[...]).astype(BF))
+        gather.start((own * rms_scale(own) * gain).astype(BF))
         return gather
 
-    meet()
+    meet(True)
+    r.gu[z] = r.gu_block[...]
+    r.down[z] = r.down_block[...]
+    each(own, lambda part: part.start())
+    if not last:
+        r.mix_next[z] = r.mix_block[...]
+
+        @pl.when(following[1].away == 0)
+        def _():
+            r.out_next[...] = r.out_block[...]
+
     first, second = (scatter(batch) for batch in range(2))
     project(0)
     mixer(0)
@@ -906,33 +1266,40 @@
     mixer(1)
     second.start()
     second.forward()
+    each(own, lambda part: part.hop(1))
     gathers = []
     for batch, part in enumerate((first, second)):
-        mid = r.rows[batch] + part.finish()
+        mid = r.rows[batch].astype(F32) + part.finish()
         r.mid[batch] = mid
-        gathers.append(send_normed(batch, mid, r.gain_two, r.normed_two))
+        gathers.append(send_normed(batch, mid, r.gains[layer, 1:2, :], r.normed_two))
+    each(own, lambda part: part.hop(2))
     first, second = (scatter(batch) for batch in range(2))
     for batch, part in enumerate((first, second)):
         gathers[batch].forward()
         gathers[batch].finish()
+        if batch == 0:
+            each(own, lambda part: part.finish())
+            each(following, lambda part: part.start())
         feed(batch)
         part.start()
         part.forward()
+    each(following, lambda part: part.hop(1))
     gathers = []
     for batch, part in enumerate((first, second)):
-        own = (r.mid[batch] + part.finish()).astype(BF)
-        r.out_rows[batch] = own
+        rows = (r.mid[batch] + part.finish()).astype(BF)
+        r.out_rows[batch] = rows
         if not last:
-            gathers.append(
-                send_normed(batch, own.astype(F32), r.gain_next, r.normed_next)
-            )
+            gain = r.gains[layer + 1, 0:1, :]
+            gathers.append(send_normed(batch, rows.astype(F32), gain, r.normed_next))
+    each(following, lambda part: part.hop(2))
     for gather in gathers:
         gather.forward()
     for gather in gathers:
         gather.finish()
-
-
-def backward_layer(ins, outs, *refs):
+    each(following, lambda part: part.finish())
+
+
+def backward_layer(layer, ins, outs, *refs):
     scratch = fields(PlaneScratch, BackwardScratch)
     earlier = len(outs) == len(fields(BackwardOut, EarlyOut))
     if earlier:
@@ -953,7 +1320,7 @@
 
     def feed_back(batch):
         def block(rows, begin):
-            grad_hidden = nt(r.grad_full[batch, rows, :], r.down[...])
+            grad_hidden = nt(r.grad_full[batch, rows, :], flat(r.down))
             half = grad_hidden.shape[1]
             gate_part = r.gate_up[batch, rows, :half]
             up_part = r.gate_up[batch, rows, half:]
@@ -962,7 +1329,7 @@
             grad_gate = grad_hidden * up_part * (sig_part + silu * (1.0 - sig_part))
             r.grad_gu[batch, rows, :half] = grad_gate.astype(BF)
             r.grad_gu[batch, rows, half:] = (grad_hidden * silu).astype(BF)
-            r.part[batch, rows, :] = nt(r.grad_gu[batch, rows, :], r.gu[...]).astype(BF)
+            r.part[batch, rows, :] = nt(r.grad_gu[batch, rows, :], flat(r.gu)).astype(BF)
 
         in_blocks(length, 256, block)
 
@@ -1001,13 +1368,13 @@
             inner, decay_w, distance, probs, per_probs = weights_of_scores(
                 query,
                 keys,
-                r.pkeys[...],
+                r.persist[layer, 0],
                 r.seg_rows[batch, rows, :],
                 r.seg_cols[batch],
                 begin,
-                r.rate[...],
+                r.rates[layer, 0:1, 0:1],
             )
-            per_dp = nt(attn_rows, r.pvalues[...])
+            per_dp = nt(attn_rows, r.persist[layer, 1])
             seq_dp = nt(attn_rows, values)
             delta = jnp.sum(per_probs * per_dp, axis=1, keepdims=True) + jnp.sum(
                 probs * seq_dp, axis=1, keepdims=True
@@ -1019,7 +1386,7 @@
             memory = inner * decay_w
             rate_terms = weighted * inner * distance
             r.grad_rate[...] -= jnp.sum(rate_terms, axis=0, keepdims=True)
-            grad_query = (nn(per_ds, r.pkeys[...]) + nn(seq_ds, keys)) * scale
+            grad_query = (nn(per_ds, r.persist[layer, 0]) + nn(seq_ds, keys)) * scale
             grad_query = grad_query + nn(grad_inner, keys)
             r.grad_proj[batch, rows, :HD] = grad_query.astype(BF)
             r.grad_keys[...] += tn(seq_ds, query) * scale + tn(grad_inner, query)
@@ -1034,7 +1401,7 @@
         r.grad_proj[batch, :, 2 * HD : 3 * HD] = r.grad_values[...].astype(BF)
 
         def back(rows, begin):
-            r.part[batch, rows, :] = nt(r.grad_proj[batch, rows, :], r.mix[...]).astype(BF)
+            r.part[batch, rows, :] = nt(r.grad_proj[batch, rows, :], flat(r.mix)).astype(BF)
 
         in_blocks(length, 256, back)
 
@@ -1044,7 +1411,7 @@
     def through_norm(batch, part, rows, gain):
         grad_normed = part.finish()
         inverse = rms_scale(rows)
-        return norm_back(grad_normed, rows * inverse, inverse, gain[...])
+        return norm_back(grad_normed, rows * inverse, inverse, gain)
 
     meet(True)
     r.grad_rate[...] = jnp.zeros_like(r.grad_rate)
@@ -1060,14 +1427,14 @@
     gathers = []
     gain_sums = []
     for batch, part in enumerate((first, second)):
-        grad_mid, gain_sum = through_norm(batch, part, r.mid[batch], r.gain_two)
+        grad_mid, gain_sum = through_norm(batch, part, r.mid[batch], r.gains[layer, 1:2, :])
         gain_sums.append(gain_sum[None])
-        grad_mid = grad_mid + r.grad_rows[batch]
+        grad_mid = grad_mid + r.grad_rows[batch].astype(F32)
         r.grad_mid[batch] = grad_mid
         gather = Gather(r.branch, batch, r.gsend, r.grecv)
         gather.start(grad_mid.astype(BF))
         gathers.append(gather)
-    r.gains[1:2] = gain_sums[0] + gain_sums[1]
+    r.gain_sums[1:2] = gain_sums[0] + gain_sums[1]
     for column in early:
         column.hop(1)
     for column in early:
@@ -1092,7 +1459,9 @@
     gathers = []
     gain_sums = []
     for batch, part in enumerate((first, second)):
-        grad_h, gain_sum = through_norm(batch, part, r.rows[batch], r.gain_one)
+        grad_h, gain_sum = through_norm(
+            batch, part, r.rows[batch].astype(F32), r.gains[layer, 0:1, :]
+        )
         gain_sums.append(gain_sum[None])
         grad_h = (grad_h + r.grad_mid[batch]).astype(BF)
         r.grad_h[batch] = grad_h
@@ -1100,7 +1469,7 @@
             gather = Gather(r.grad_next, batch, r.gsend, r.grecv)
             gather.start(grad_h)
             gathers.append(gather)
-    r.gains[0:1] = gain_sums[0] + gain_sums[1]
+    r.gain_sums[0:1] = gain_sums[0] + gain_sums[1]
     for column in sums:
         column.hop(2)
     for gather in gathers:
@@ -1308,9 +1677,48 @@
     ]
 
 
-def forward_call(number, given, last):
+def setup_call(number, inputs, small, gain_rows, w_mix, w_out, w_gu, w_down):
+    count, _, tokens, _ = inputs.shape
+    depth, length = w_mix.shape[1], 4 * tokens
+    unit = w_down.shape[1] // 8
+    padded = -(-unit // 32) * 32
+    shape = jax.ShapeDtypeStruct
+    outs = dict(
+        rows=shape((count, length // 8, D), BF),
+        normed=shape((count, length, D), BF),
+        gains=shape((2, 2, D), F32),
+        persist=shape((2, 2, 16, HD), BF),
+        rates=shape((2, 8, HD), F32),
+        mix=shape((4, depth, 4 * HD), BF),
+        mix_next=shape((depth, 4 * HD), BF),
+        out=shape((HD, D), BF),
+        out_next=shape((HD, D), BF),
+        gu=shape((depth, 8 * padded), BF),
+        gu_next=shape((depth, 8 * padded), BF),
+        down=shape((padded, D), BF),
+        down_next=shape((padded, D), BF),
+    )
+    scratch = [
+        pltpu.VMEM((2, 4, 8, HD), F32),
+        pltpu.VMEM((2, 4) + small.shape, F32),
+        pltpu.VMEM((depth, 4 * HD), BF),
+        pltpu.VMEM((depth, 8 * padded), BF),
+        pltpu.VMEM((padded, D), BF),
+        *pairs_of((3,), (7,), (5,), (2, 7)),
+        pltpu.SemaphoreType.DMA((1, 2, 4)),
+        pltpu.SemaphoreType.DMA((1, 4)),
+        pltpu.SemaphoreType.DMA((2,)),
+        pltpu.SemaphoreType.DMA((1,)),
+    ]
+    operands = (inputs, small, gain_rows, w_mix, w_out, w_gu, w_down)
+    kernel = functools.partial(setup_kernel, unit)
+    return named(outs, kernel_call(kernel, number, operands, list(outs.values()), scratch))
+
+
+def forward_call(number, layer, given):
     count, length, _ = given.normed.shape
-    half = given.down.shape[0]
+    depth, half = D // 4, 4 * given.down_block.shape[0]
+    last = layer == 1
     shape = jax.ShapeDtypeStruct
     outs = dict(
         qkv=shape((count, length, 3 * HD), BF),
@@ -1321,27 +1729,36 @@
         normed_two=shape((count, length, D), BF),
         gate_up=shape((count, length, 2 * half), F32),
         hidden=shape((count, length, half), BF),
+        gu=shape((4, depth, 2 * half), BF),
+        down=shape((4, half // 4, D), BF),
         out_rows=shape((count, length // 8, D), BF),
         normed_next=shape((count, length, D), BF),
     )
+    scratch = scatter_scratch(length)
+    scratch += [pltpu.SemaphoreType.DMA((3, 2, 4)), pltpu.SemaphoreType.DMA((3, 4))]
+    ins = ForwardIn._fields
     if last:
         del outs[ForwardOut._fields[-1]]
-    operands = [getattr(given, name) for name in ForwardIn._fields]
-    kernel = functools.partial(forward_layer, ForwardIn._fields, tuple(outs))
-    found = kernel_call(kernel, number, operands, list(outs.values()), scatter_scratch(length))
-    return named(outs, found)
-
-
-def backward_call(number, given, last):
+    else:
+        ins += NextIn._fields
+        outs |= dict(mix_next=shape((4, depth, 4 * HD), BF), out_next=shape((HD, D), BF))
+        scratch += [pltpu.SemaphoreType.DMA((2,)), pltpu.SemaphoreType.DMA((1,))]
+    operands = [getattr(given, name) for name in ins]
+    kernel = functools.partial(forward_layer, layer, ins, tuple(outs))
+    return named(outs, kernel_call(kernel, number, operands, list(outs.values()), scratch))
+
+
+def backward_call(number, layer, given):
     count, length, _ = given.normed.shape
-    half = given.down.shape[0]
+    half = 4 * given.down.shape[1]
+    last = layer == 0
     depth = D // 4
     shape = jax.ShapeDtypeStruct
     outs = dict(
         grad_mix=shape((4, depth, 4 * HD), BF),
         grad_out=shape((HD, D), BF),
-        gains=shape((2, D), F32),
-        grad_persist=shape((2,) + given.pkeys.shape, F32),
+        gain_sums=shape((2, D), F32),
+        grad_persist=shape(given.persist.shape[1:], F32),
         grad_rate=shape((1, length), F32),
         gu_sum=shape((depth, 2 * half), BF),
         down_sum=shape((half // 4, D), BF),
@@ -1372,10 +1789,9 @@
             pltpu.VMEM((2, HD, D), BF),
             *pairs_of((2,)),
         ]
-    kernel = functools.partial(backward_layer, ins, tuple(outs))
+    kernel = functools.partial(backward_layer, layer, ins, tuple(outs))
     operands = [getattr(given, name) for name in ins]
-    found = kernel_call(kernel, number, operands, list(outs.values()), scratch)
-    return named(outs, found)
+    return named(outs, kernel_call(kernel, number, operands, list(outs.values()), scratch))
 
 
 def final_call(number, by_layer, small):
@@ -1454,103 +1870,67 @@
     length = tokens * ns
     size = length // width
     depth = w_mix.shape[1]
-    unit = w_down.shape[1] // width
-
-    heads = w_mix[0].reshape(depth, 4, H, HD)
-    halves = w_gu[0].reshape(depth, 2, nz, width, unit)
-    downs = w_down[0].reshape(width, unit, D)
-    more = -unit % 32
-
-    def pick(which):
-        both = lax.dynamic_index_in_dim(halves, which, 3, keepdims=False)
-        both = jnp.pad(both, ((0, 0), (0, 0), (0, 0), (0, more)))
-        down = lax.dynamic_index_in_dim(downs, which, 0, keepdims=False)
-        return (
-            lax.dynamic_index_in_dim(heads, which, 2, keepdims=False).reshape(depth, 4 * HD),
-            both.reshape(depth, 2 * nz * (unit + more)),
-            jnp.pad(down, ((0, more), (0, 0))),
-        )
+    unit = w_down.shape[1] // (nx * ns)
 
     def layers(own, got):
         return (jnp.where(first, own, got), jnp.where(first, got, own))
 
-    swap = [(0, 1), (1, 0)]
-    parts = [layers(o, lax.ppermute(g, "section", swap)) for o, g in zip(pick(mine), pick(other))]
-    out_rows = lax.dynamic_index_in_dim(
-        w_out[0].reshape(2, HD, D), lax.rem(s, 2), 0, keepdims=False
-    )
-    out_all = lax.all_gather(out_rows, "shard", axis=0)
-    out_own = lax.dynamic_index_in_dim(out_all, mine // 2, 0, keepdims=False)
-    out_got = lax.ppermute(
-        lax.dynamic_index_in_dim(out_all, other // 2, 0, keepdims=False), "section", swap
-    )
-    out_w = layers(out_own, out_got)
-    mix_w, gu_w, down_w = (
-        [lax.all_gather(part[layer], "shard", axis=0, tiled=True) for layer in range(2)]
-        for part in parts
-    )
-
-    small = jnp.concatenate([persist_kv[0].reshape(-1).astype(F32), memory_decay[0]])
-    small = lax.all_gather(small, ("section", "seq"), axis=0)
-    rates = small[:, -2:].reshape(2, H)[:, mine]
-    persist = small[:, :-2].astype(BF).reshape(2, ns, 2, persist_kv.shape[2], 2, HD)
-    persist = lax.dynamic_index_in_dim(persist, mine // 2, 1, keepdims=False)
-    persist = lax.dynamic_index_in_dim(persist, lax.rem(mine, 2), 3, keepdims=False)
-    gains = lax.all_gather(norm_gains[0], ("section", "shard"), axis=0, tiled=True)
-    gains = gains.astype(F32).reshape(2, 1, D, 2)
-
-    def own_rows(whole):
-        return lax.dynamic_slice_in_dim(whole[:, 0], x * size, size, 1).astype(F32)
-
+    small = persist_kv[0].reshape(-1, 2, HD).transpose(1, 0, 2).reshape(-1, HD).astype(F32)
+    rates = jnp.broadcast_to(memory_decay[0][:, None, None], (2, 8, HD)).reshape(-1, HD)
+    gain_rows = norm_gains[0].astype(F32).T.reshape(-1, HD)
+    gain_rows = jnp.pad(gain_rows, ((0, 8 - gain_rows.shape[0]), (0, 0)))
+    ready = setup_call(
+        0, inputs, jnp.concatenate([small, rates], 0), gain_rows, w_mix, w_out, w_gu, w_down
+    )
+    shared = dict(
+        gains=ready.gains,
+        persist=ready.persist,
+        rates=ready.rates,
+        seg_rows=segment_ids[:, 0, :, None],
+        seg_cols=segment_ids,
+    )
+    lower = dict(
+        shared,
+        normed=ready.normed,
+        rows=ready.rows,
+        mix=ready.mix,
+        out=ready.out,
+        gu_block=ready.gu,
+        down_block=ready.down,
+        mix_block=ready.mix_next,
+        out_block=ready.out_next,
+    )
+    below = forward_call(1, 0, types.SimpleNamespace(**lower))
+    upper = dict(
+        shared,
+        normed=below.normed_next,
+        rows=below.out_rows,
+        mix=below.mix_next,
+        out=below.out_next,
+        gu_block=ready.gu_next,
+        down_block=ready.down_next,
+    )
+    above = forward_call(2, 1, types.SimpleNamespace(**upper))
+    outputs = [below.out_rows, above.out_rows]
     cot_full = lax.all_gather(cotangent[:, 0], "seq", axis=1, tiled=True)
-    rows = own_rows(inputs)
-    full = jax.ShapeDtypeStruct((count, length, D), BF)
-    (normed,) = kernel_call(
-        start_kernel, 0, (rows, gains[0, :, :, 0]), [full], pairs_of((2, 7))
-    )
-    of_layer = [
-        dict(
-            mix=mix_w[layer],
-            out=out_w[layer],
-            gu=gu_w[layer],
-            down=down_w[layer],
-            gain_one=gains[layer, :, :, 0],
-            gain_two=gains[layer, :, :, 1],
-            gain_next=gains[1, :, :, 0],
-            pkeys=persist[layer, 0],
-            pvalues=persist[layer, 1],
-            rate=rates[layer].reshape(1, 1),
-            seg_rows=segment_ids[:, 0, :, None],
-            seg_cols=segment_ids,
-        )
-        for layer in range(2)
-    ]
-    outputs = []
-    for layer in range(2):
-        of_layer[layer] |= dict(normed=normed, rows=rows)
-        found = forward_call(1 + layer, types.SimpleNamespace(**of_layer[layer]), layer == 1)
-        of_layer[layer] |= vars(found)
-        outputs.append(found.out_rows)
-        if layer == 0:
-            normed = found.normed_next
-            rows = found.out_rows.astype(F32)
-    given = dict(of_layer[1], grad_full=cot_full, grad_rows=own_rows(cotangent))
-    later = backward_call(3, types.SimpleNamespace(**given), False)
-    given = dict(
-        of_layer[0],
+    cot_rows = lax.dynamic_slice_in_dim(cotangent[:, 0], x * size, size, 1)
+    upper |= dict(vars(above), grad_full=cot_full, grad_rows=cot_rows)
+    later = backward_call(3, 1, types.SimpleNamespace(**upper))
+    lower |= dict(
+        vars(below),
         grad_full=later.grad_next,
-        grad_rows=later.grad_h.astype(F32),
+        grad_rows=later.grad_h,
         early_mix=later.grad_mix,
         early_out=later.grad_out,
     )
-    earlier = backward_call(4, types.SimpleNamespace(**given), True)
+    earlier = backward_call(4, 0, types.SimpleNamespace(**lower))
     by_layer = [
         (earlier.grad_mix, earlier.gu_sum, earlier.down_sum, earlier.grad_out),
         (earlier.mix_sum, later.gu_sum, later.down_sum, earlier.out_sum),
     ]
     both = (earlier, later)
     grads = [found.grad_h for found in both]
-    gain_sums = [found.gains for found in both]
+    gain_sums = [found.gain_sums for found in both]
 
     memory_all = jnp.stack([found.grad_persist for found in both], 0).reshape(-1, HD)
     rate_all = jnp.stack([jnp.sum(found.grad_rate) for found in both])

time: 574 us -> 512 us (0.89)
  blocking collectives: 64.6 us -> 0 us
  Pallas kernels: 418 us -> 464 us
  waiting for transfers between devices: 17.2 us -> 0.68 us
  local copies, waits for them, and re-layouts: 25.3 us -> 10.6 us
    all_gather x3 -> x0, blocking collectives: 64.6 us -> none  [the longest x2 48.9 us: tensor_parallel(): lax.all_gather(part[layer], 'shard', axis=0, tiled=True)]
    pallas_call x6, Pallas kernels: 412 us -> 458 us  [kernel_call(): pl.pallas_call(kernel, out_shape=outs, in_specs=[vmem] * len(operands), o...]
    ppermute x4 -> x0, waiting for transfers between devices: 15 us -> none  [the longest x3 15 us: tensor_parallel(): lax.ppermute(g, 'section', swap)]
    unnamed x43 -> x24, local copies, waits for them, and re-layouts: 9.26 us -> 3.04 us
    convert_element_type x5 -> x0, other arithmetic: 6.05 us -> none  [the longest x1 1.79 us: tensor_parallel(): later.grad_h.astype(F32)]
  transfers between devices with their start and end apart: 11 -> 1, of which waited for: 2 -> 0; matrix products, arithmetic and copies ran while one was open for 4% -> 1% of each run, Pallas kernels for 27% -> 40%
where the time goes in v4:
time: 512 us; the launch traced here: 506 us
  Pallas kernels  464 us (91%)
  other arithmetic  16.9 us (3%)
  between operations  14.4 us (3%)
  local copies, waits for them, and re-layouts  10.6 us (2%)
    pallas_call x6, Pallas kernels, kernel_call(): pl.pallas_call(kernel, out_shape=outs, in_specs=[vmem] * len(operands), o...  458 us
  transfers between devices with their start and end apart: 1, of which 0 were waited for; matrix products, arithmetic and copies ran while one was open for 1% of the time, Pallas kernels for 40%

profile of v4, /device:TPU:3, one launch (start us, length us, event | category | flops | bytes accessed | tf_op | source)
XLA Modules:
  0.0 506.4 jit_solution(2245402625226404385)
XLA Ops:
  7.9 0.7 reshape.103
  8.7 0.7 broadcast_in_dim.28
  10.9 1.0 broadcast_in_dim_squeeze.5.refs_9_.refs_11_
  13.2 50.9 %shard_map.169 = (bf16[2,64,1024]{2,1,0:T(8,128)(2,1)}, bf16[2,512,1024]{2,1,0:T(8,128)(2,1)}, f32[2,2,1024]{2,1,0:T(2,128)}, bf16[2,2,16,128]{3,2,1,0:T(8,128)(...) custom-call(bf16[2,1,128,1024]{3,2,1,0:T(8,128)(2,1)} %refs_0_.1, ...), custom_call_target="tpu_custom_call" | custom-call | tf_op jit(solution)/shard_map/pallas_call | solution.py:1653
  64.2 83.9 %shard_map.170 = (bf16[2,512,384]{2,1,0:T(8,128)(2,1)}, f32[2,512,128]{2,1,0:T(8,128)}, bf16[2,512,128]{2,1,0:T(8,128)(2,1)}, bf16[2,512,128]{2,1,0:T(8,128)(2,1...) custom-call(bf16[2,512,1024]{2,1,0:T(8,128)(2,1)} %get-tuple-element, ...), custom_call_target="tpu_custom_call" | custom-call | tf_op jit(solution)/shard_map/pallas_call | solution.py:1653
  148.1 65.4 %shard_map.171 = (bf16[2,512,384]{2,1,0:T(8,128)(2,1)}, f32[2,512,128]{2,1,0:T(8,128)}, bf16[2,512,128]{2,1,0:T(8,128)(2,1)}, bf16[2,512,128]{2,1,0:T(8,128)(2,1...) custom-call(bf16[2,512,1024]{2,1,0:T(8,128)(2,1)} %get-tuple-element, ...), custom_call_target="tpu_custom_call" | custom-call | tf_op jit(solution)/shard_map/pallas_call | solution.py:1653
  213.5 0.7 dynamic-slice_bitcast_fusion.refs_1_
  214.2 90.2 %shard_map.172 = (bf16[4,256,512]{2,1,0:T(8,128)(2,1)}, bf16[128,1024]{1,0:T(8,128)(2,1)}, f32[2,1024]{1,0:T(2,128)}, f32[2,16,128]{2,1,0:T(8,128)}, f32[1,512]{...) custom-call(bf16[2,512,1024]{2,1,0:T(8,128)(2,1)} %bitcast.52, ...), custom_call_target="tpu_custom_call" | custom-call | tf_op jit(solution)/shard_map/pallas_call | solution.py:1653
  304.5 94.4 %shard_map.173 = (bf16[4,256,512]{2,1,0:T(8,128)(2,1)}, bf16[128,1024]{1,0:T(8,128)(2,1)}, f32[2,1024]{1,0:T(2,128)}, f32[2,16,128]{2,1,0:T(8,128)}, f32[1,512]{...) custom-call(bf16[2,512,1024]{2,1,0:T(8,128)(2,1)} %get-tuple-element, ...), custom_call_target="tpu_custom_call" | custom-call | tf_op jit(solution)/shard_map/pallas_call | solution.py:1653
  398.8 1.3 reduce_sum.27
  401.5 0.7 pad_maximum_fusion.2
  402.2 1.4 maximum_bitcast_fusion.2
  404.3 73.4 %shard_map.174 = (bf16[2,4,256,512]{3,2,1,0:T(8,128)(2,1)}, bf16[2,4,256,768]{3,2,1,0:T(8,128)(2,1)}, bf16[2,4,96,1024]{3,2,1,0:T(8,128)(2,1)}, bf16[2,128,1024]...) custom-call(bf16[4,256,512]{2,1,0:T(8,128)(2,1)} %get-tuple-element.118.refs, ...), custom_call_target="tpu_custom_call" | custom-call | tf_op jit(solution)/shard_map/pallas_call | solution.py:1653
  477.7 1.8 select_bitcast_fusion.1
  479.5 1.8 broadcast_select_fusion.2
  481.3 1.1 bitcast_convert_fusion
  482.4 1.0 slice_reduce_fusion
  483.4 0.8 constant_dynamic-slice_fusion
  485.5 2.0 fusion
  487.5 1.9 maximum_bitcast_fusion
  489.4 1.4 dynamic-slice_reduce_fusion
  490.8 1.6 copy-done.1
  492.4 1.4 copy-done.2
  493.8 5.6 %shard_map.175 = (f32[1,256,4096]{2,1,0:T(8,128)}, f32[1,256,5632]{2,1,0:T(8,128)}, f32[1,704,1024]{2,1,0:T(8,128)}) custom-call(bf16[2,4,256,512]{3,2,1,0:T(8,128)(2,1)S(1)} %copy-done.1, bf16[2,4,256,768]{3,2,1,0:T(8,128)(2,1)S(1)} %copy-done, bf16[2,4,96,1024]{3,2,1,0:T(8,128)(2,1)S(1)} %copy-done.2), custom_call_target="tpu_custom_call" | custom-call | tf_op jit(solution)/shard_map/pallas_call | solution.py:1838
  (44 shorter events, 6.9 us)
Async XLA Ops:
  7.2 207.0 %all-gather.3.cloned.1.call-start = ((), (), s32[]{:S(2)}) async-start(), calls=%async_computation | async-start | bytes 2621440 | tf_op jit(solution)/shard_map/all_gather | solution.py:1915
  148.1 65.4 %copy-start.5 = (bf16[2,1,128,1024]{3,2,1,0:T(8,128)(2,1)S(1)}, bf16[2,1,128,1024]{3,2,1,0:T(8,128)(2,1)}, u32[]{:S(2)}) copy-start(bf16[2,1,128,1024]{3,2,1,0:T(8,128)(2,1)} %param.12) | copy-start | bytes 1572868
  304.4 95.7 %copy-start.11 = (f32[1,512]{1,0:T(1,128)S(1)}, f32[1,512]{1,0:T(1,128)}, u32[]{:S(2)}) copy-start(f32[1,512]{1,0:T(1,128)} %get-tuple-element.130) | copy-start | bytes 6148
  304.4 96.3 %copy-start.10 = (f32[2,1024]{1,0:T(2,128)S(1)}, f32[2,1024]{1,0:T(2,128)}, u32[]{:S(2)}) copy-start(f32[2,1024]{1,0:T(2,128)} %get-tuple-element.132) | copy-start | bytes 24580
  304.5 97.0 %copy-start.9 = (f32[2,16,128]{2,1,0:T(8,128)S(1)}, f32[2,16,128]{2,1,0:T(8,128)}, u32[]{:S(2)}) copy-start(f32[2,16,128]{2,1,0:T(8,128)} %get-tuple-element.128) | copy-start | bytes 49156
  404.3 73.4 %copy-start.4 = (bf16[2,64,1024]{2,1,0:T(8,128)(2,1)S(1)}, bf16[2,64,1024]{2,1,0:T(8,128)(2,1)}, u32[]{:S(2)}) copy-start(bf16[2,64,1024]{2,1,0:T(8,128)(2,1)} %get-tuple-element.105.refs_1_.refs_11_) | copy-start | bytes 786436
  404.3 73.4 %copy-start.7 = (bf16[2,64,1024]{2,1,0:T(8,128)(2,1)S(1)}, bf16[2,64,1024]{2,1,0:T(8,128)(2,1)}, u32[]{:S(2)}) copy-start(bf16[2,64,1024]{2,1,0:T(8,128)(2,1)} %get-tuple-element.122.refs_5_) | copy-start | bytes 786436
  404.3 75.2 %copy-start.3 = (bf16[2,64,1024]{2,1,0:T(8,128)(2,1)S(1)}, bf16[2,64,1024]{2,1,0:T(8,128)(2,1)}, u32[]{:S(2)}) copy-start(bf16[2,64,1024]{2,1,0:T(8,128)(2,1)} %get-tuple-element.87.refs_1_.refs_2_.refs_4_) | copy-start | bytes 786436
  404.3 75.2 %copy-start.6 = (bf16[2,64,1024]{2,1,0:T(8,128)(2,1)S(1)}, bf16[2,64,1024]{2,1,0:T(8,128)(2,1)}, u32[]{:S(2)}) copy-start(bf16[2,64,1024]{2,1,0:T(8,128)(2,1)} %get-tuple-element.93.refs_10_) | copy-start | bytes 786436
  477.7 3.6 copy-start.8
  481.3 9.5 %copy-start = (bf16[2,4,256,768]{3,2,1,0:T(8,128)(2,1)S(1)}, bf16[2,4,256,768]{3,2,1,0:T(8,128)(2,1)}, u32[]{:S(2)}) copy-start(bf16[2,4,256,768]{3,2,1,0:T(8,128)(2,1)} %get-tuple-element.136.gu_buf) | copy-start | bytes 9437188
  490.8 1.6 copy-start.1
  492.4 1.4 copy-start.2
Sparse Core Ops, SparseCore 0:
  9.6 30.4 all-gather.2

commit v5 on v3

--- a/solution.py
+++ b/solution.py
@@ -530,130 +530,181 @@
         return total
 
 
-class ColumnSum:
-    def __init__(self, own, slots, out, send, recv, index):
+class Column:
+    def __init__(self, send, recv):
         self.place = here()
+        self.send, self.recv = send, recv
+
+    def copy(self, source, landing, sent, received, plane):
+        x, s, _ = self.place
+        return pltpu.make_async_remote_copy(
+            src_ref=source,
+            dst_ref=landing,
+            send_sem=self.send.at[sent],
+            recv_sem=self.recv.at[received],
+            device_id=(x, s, plane),
+            device_id_type=MESH,
+        )
+
+    def at_each(self, body):
+        for at in range(4):
+
+            @pl.when(self.place[2] == at)
+            def _():
+                body(at)
+
+
+class ColumnSum(Column):
+    RELAYED = ((3, 1), None, None, (0, 2))
+    DIRECT = ((2, 1), (2, 0), (1, 3), (1, 2))
+    SOURCES = ((1, 2), (0, 2, 3), (0, 1, 3), (1, 2))
+
+    def __init__(self, own, slots, out, send, recv):
+        super().__init__(send, recv)
         self.own, self.slots, self.out = own, slots, out
-        self.send, self.recv, self.index = send, recv, index
-
-    def copy(self, down, owner, source=None):
+
+    def first(self, at):
+        block, plane = self.RELAYED[at]
+        return self.copy(self.own.at[block], self.slots.at[plane], at, plane, plane)
+
+    def direct(self, at, plane):
+        return self.copy(self.own.at[plane], self.slots.at[at], plane, at, plane)
+
+    def relayed(self, at):
+        end = 3 if at == 1 else 0
+        return self.copy(self.slots.at[at], self.slots.at[at], end, at, end)
+
+    def start(self):
+        def body(at):
+            if self.RELAYED[at]:
+                self.first(at).start()
+            for plane in self.DIRECT[at]:
+                self.direct(at, plane).start()
+
+        self.at_each(body)
+
+    def hop(self):
+        for at, block in ((1, 3), (2, 0)):
+
+            @pl.when(self.place[2] == at)
+            def _():
+                self.relayed(at).wait_recv()
+                self.slots[at] = (
+                    self.slots[at].astype(F32) + self.own[block].astype(F32)
+                ).astype(BF)
+                self.relayed(at).start()
+
+    def finish(self):
+        def body(at):
+            total = self.own[at].astype(F32)
+            for plane in self.SOURCES[at]:
+                self.direct(plane, at).wait_recv()
+                total = total + self.slots[plane].astype(F32)
+            self.out[...] = total.astype(BF)
+            if self.RELAYED[at]:
+                self.first(at).wait_send()
+            else:
+                self.relayed(at).wait_send()
+            for plane in self.DIRECT[at]:
+                self.direct(at, plane).wait_send()
+
+        self.at_each(body)
+
+
+class ColumnGather(Column):
+    TARGETS = ((2, 1), (3, 2, 0), (0, 1, 3), (1, 2))
+
+    def __init__(self, full, send, recv):
+        super().__init__(send, recv)
+        self.full = full
+
+    def block(self, at, plane):
+        return self.copy(self.full.at[at], self.full.at[at], plane, at, plane)
+
+    def relayed(self, at):
+        block, plane = (3, 0) if at == 1 else (0, 3)
+        return self.copy(self.full.at[block], self.full.at[block], at, block, plane)
+
+    def start(self):
+        def body(at):
+            for plane in self.TARGETS[at]:
+                self.block(at, plane).start()
+
+        self.at_each(body)
+
+    def hop(self):
+        for at in (1, 2):
+
+            @pl.when(self.place[2] == at)
+            def _():
+                self.relayed(at).wait_recv()
+                self.relayed(at).start()
+
+    def finish(self):
+        def body(at):
+            for plane in range(4):
+                if plane != at and (at, plane) not in ((1, 3), (2, 0)):
+                    self.block(plane, at).wait_recv()
+            for plane in self.TARGETS[at]:
+                self.block(at, plane).wait_send()
+            if at in (1, 2):
+                self.relayed(at).wait_send()
+
+        self.at_each(body)
+
+
+class Root(Column):
+    def __init__(self, send, recv):
+        super().__init__(send, recv)
         x, s, z = self.place
-        slot = owner if down else owner - 1
-        target = (x, s, (z + 3) % 4 if down else (z + 1) % 4)
-        landing = self.slots.at[down, slot]
-        return pltpu.make_async_remote_copy(
-            src_ref=landing if source is None else source,
-            dst_ref=landing,
-            send_sem=self.send.at[self.index, down, slot],
-            recv_sem=self.recv.at[self.index, down, slot],
-            device_id=target,
-            device_id_type=MESH,
-        )
+        self.root = 2 * x + s // 2
+        self.low = self.root < 2
+        self.between = jnp.where(self.low, 2, 1)
+        self.end = jnp.where(self.low, 3, 0)
+        self.is_root = z == self.root
+
+
+class RootSum(Root):
+    def __init__(self, own, slots, out, send, recv):
+        super().__init__(send, recv)
+        self.own, self.slots, self.out = own, slots, out
+
+    def toward(self, slot, plane, source=None):
+        landing = self.slots.at[slot]
+        return self.copy(landing if source is None else source, landing, 0, slot, plane)
 
     def start(self):
         z = self.place[2]
-        for down in (0, 1):
-
-            @pl.when(z == 3 * down)
-            def _():
-                for owner in (0, 1, 2) if down else (3, 2, 1):
-                    self.copy(down, owner, self.own.at[owner]).start()
-
-    def relay(self, down, owner, at):
-        @pl.when(self.place[2] == at)
+
+        @pl.when(z == self.end)
         def _():
-            self.copy(down, owner).wait_recv()
-            slot = owner if down else owner - 1
-            self.slots[down, slot] = (
-                self.slots[down, slot].astype(F32) + self.own[owner].astype(F32)
-            ).astype(BF)
-            self.copy(down, owner).start()
-
-    def hop(self, number):
-        if number == 1:
-            self.relay(0, 3, 1)
-            self.relay(1, 0, 2)
-        else:
-            self.relay(0, 2, 1)
-            self.relay(1, 1, 2)
-            self.relay(0, 3, 2)
-            self.relay(1, 0, 1)
+            self.toward(0, self.between, self.own).start()
+
+        @pl.when((z != self.end) & (z != self.between) & (z != self.root))
+        def _():
+            self.toward(1, self.root, self.own).start()
+
+    def hop(self):
+        @pl.when(self.place[2] == self.between)
+        def _():
+            self.toward(0, self.root).wait_recv()
+            self.slots[0] = (self.slots[0].astype(F32) + self.own[...].astype(F32)).astype(BF)
+            self.toward(0, self.root).start()
 
     def finish(self):
-        z = self.place[2]
-        for at in range(4):
-
-            @pl.when(z == at)
-            def _():
-                total = self.own[at].astype(F32)
-                if at > 0:
-                    self.copy(0, at).wait_recv()
-                    total = total + self.slots[0, at - 1].astype(F32)
-                if at < 3:
-                    self.copy(1, at).wait_recv()
-                    total = total + self.slots[1, at].astype(F32)
-                self.out[...] = total.astype(BF)
-                for owner in range(at + 1, 4):
-                    self.copy(0, owner).wait_send()
-                for owner in range(at):
-                    self.copy(1, owner).wait_send()
-
-
-class RootSum:
-    def __init__(self, own, slots, out, send, recv):
-        self.place = here()
-        x, s, _ = self.place
-        self.root = 2 * x + s // 2
-        self.own, self.slots, self.out = own, slots, out
-        self.send, self.recv = send, recv
-
-    def copy(self, down, source=None):
-        x, s, z = self.place
-        landing = self.slots.at[down]
-        return pltpu.make_async_remote_copy(
-            src_ref=landing if source is None else source,
-            dst_ref=landing,
-            send_sem=self.send.at[down],
-            recv_sem=self.recv.at[down],
-            device_id=(x, s, (z + 3) % 4 if down else (z + 1) % 4),
-            device_id_type=MESH,
-        )
-
-    def sends(self, down):
-        z = self.place[2]
-        return z > self.root if down else z < self.root
-
-    def start(self):
-        for down in (0, 1):
-
-            @pl.when((self.place[2] == 3 * down) & self.sends(down))
-            def _():
-                self.copy(down, self.own).start()
-
-    def relay(self, down, at):
-        @pl.when((self.place[2] == at) & self.sends(down))
+        self.out[...] = self.own[...]
+
+        @pl.when(self.is_root)
         def _():
-            self.copy(down).wait_recv()
-            self.slots[down] = (self.slots[down].astype(F32) + self.own[...].astype(F32)).astype(BF)
-            self.copy(down).start()
-
-    def hop(self, number):
-        self.relay(0, number)
-        self.relay(1, 3 - number)
-
-    def finish(self):
-        z = self.place[2]
-        self.out[...] = self.own[...]
-        for down in (0, 1):
-
-            @pl.when((z == self.root) & (z < 3 if down else z > 0))
-            def _():
-                self.copy(down).wait_recv()
-                self.out[...] = (self.out[...].astype(F32) + self.slots[down].astype(F32)).astype(BF)
-
-            @pl.when(self.sends(down))
-            def _():
-                self.copy(down).wait_send()
+            total = self.own[...].astype(F32)
+            for slot in (0, 1):
+                self.toward(slot, self.root).wait_recv()
+                total = total + self.slots[slot].astype(F32)
+            self.out[...] = total.astype(BF)
+
+        @pl.when(jnp.logical_not(self.is_root))
+        def _():
+            self.toward(0, self.root).wait_send()
 
 
 def meet(column=False):
@@ -661,7 +712,7 @@
     x, s, z = place
     others = [peer(place, chip, chip == 0) for chip in range(4)]
     if column:
-        others += [(x, s, (z + 1) % 4), (x, s, (z + 3) % 4)]
+        others += [(x, s, (z + dz) % 4) for dz in (1, 2, 3)]
     barrier = pltpu.get_barrier_semaphore()
     for other in others:
         pl.semaphore_signal(barrier, inc=1, device_id=other, device_id_type=MESH)
@@ -678,6 +729,11 @@
 
 def tn(left, right):
     return lax.dot_general(left, right, (((0,), (0,)), ((), ())), preferred_element_type=F32)
+
+
+def flat(ref):
+    value = ref[...]
+    return value.reshape(-1, value.shape[-1])
 
 
 def in_blocks(length, size, body):
@@ -708,61 +764,18 @@
     return inner, decay_w, distance, seq_exp * share, per_exp * share
 
 
-def start_kernel(rows_ref, gain_ref, full_ref, gsend, grecv):
-    meet()
-    gathers = [Gather(full_ref, batch, gsend, grecv) for batch in range(2)]
-    for batch, gather in enumerate(gathers):
-        rows = rows_ref[batch]
-        gather.start((rows * rms_scale(rows) * gain_ref[...]).astype(BF))
-    for gather in gathers:
-        gather.forward()
-    for gather in gathers:
-        gather.finish()
-
-
-class ForwardIn(NamedTuple):
-    normed: Any
-    rows: Any
-    gain_two: Any
-    gain_next: Any
-    gu: Any
-    down: Any
-    mix: Any
-    out: Any
-    pkeys: Any
-    pvalues: Any
-    rate: Any
-    seg_rows: Any
-    seg_cols: Any
-
-
-class ForwardOut(NamedTuple):
-    qkv: Any
-    gate: Any
-    recalled: Any
-    combined: Any
-    mid: Any
-    normed_two: Any
-    gate_up: Any
-    hidden: Any
-    out_rows: Any
-    normed_next: Any
-
-
 class BackwardIn(NamedTuple):
     grad_full: Any
     grad_rows: Any
     rows: Any
     normed: Any
-    gain_one: Any
-    gain_two: Any
     gu: Any
     down: Any
+    gains: Any
     mix: Any
     out: Any
-    pkeys: Any
-    pvalues: Any
-    rate: Any
+    persist: Any
+    rates: Any
     seg_rows: Any
     seg_cols: Any
     qkv: Any
@@ -778,7 +791,7 @@
 class BackwardOut(NamedTuple):
     grad_mix: Any
     grad_out: Any
-    gains: Any
+    gain_sums: Any
     grad_persist: Any
     grad_rate: Any
     gu_sum: Any
@@ -841,50 +854,375 @@
     return types.SimpleNamespace(**dict(zip(names, refs, strict=True)))
 
 
-def forward_layer(ins, outs, *refs):
-    r = named(ins + outs + fields(PlaneScratch), refs)
+def remote(source, landing, sems, index, target):
+    return pltpu.make_async_remote_copy(
+        src_ref=source,
+        dst_ref=landing,
+        send_sem=sems[0].at[index],
+        recv_sem=sems[1].at[index],
+        device_id=target,
+        device_id_type=MESH,
+    )
+
+
+class RootGather(Root):
+    def __init__(self, block, send, recv):
+        super().__init__(send, recv)
+        self.block = block
+
+    def to(self, plane, sent):
+        return self.copy(self.block, self.block, sent, 0, plane)
+
+    def near(self):
+        return jnp.where(self.low, 1 - self.root, 5 - self.root)
+
+    def start(self):
+        @pl.when(self.is_root)
+        def _():
+            self.to(self.between, 0).start()
+            self.to(self.near(), 1).start()
+
+    def hop(self):
+        @pl.when(self.place[2] == self.between)
+        def _():
+            self.to(self.end, 0).wait_recv()
+            self.to(self.end, 0).start()
+
+    def finish(self):
+        z = self.place[2]
+
+        @pl.when((z != self.root) & (z != self.between))
+        def _():
+            self.to(self.end, 0).wait_recv()
+
+        @pl.when((z == self.root) | (z == self.between))
+        def _():
+            self.to(self.end, 0).wait_send()
+
+        @pl.when(self.is_root)
+        def _():
+            self.to(self.end, 1).wait_send()
+
+
+class SeqGather:
+    def __init__(self, full, batch, send, recv):
+        self.place = here()
+        self.full, self.batch, self.send, self.recv = full, batch, send, recv
+        self.size = full.shape[1] // 4
+        self.beside = peer(self.place, 2, False)
+        self.sibling = peer(self.place, 0, True)
+
+    def rows(self, owner):
+        return pl.ds(pl.multiple_of(owner[1] * self.size, self.size), self.size)
+
+    def copy(self, owner, target, sem):
+        block = self.full.at[self.batch, self.rows(owner)]
+        sems = (self.send.at[self.batch], self.recv.at[self.batch])
+        return remote(block, block, sems, sem, target)
+
+    def start(self, value):
+        self.full[self.batch, self.rows(self.place), :] = value
+        self.copy(self.place, self.beside, 0).start()
+        self.copy(self.place, self.sibling, 1).start()
+
+    def forward(self):
+        self.copy(self.beside, self.beside, 0).wait_recv()
+        self.copy(self.beside, self.sibling, 2).start()
+
+    def finish(self):
+        self.copy(self.sibling, self.sibling, 1).wait_recv()
+        self.copy(peer(self.place, 2, True), self.sibling, 2).wait_recv()
+        self.copy(self.place, self.beside, 0).wait_send()
+        self.copy(self.place, self.sibling, 1).wait_send()
+        self.copy(self.beside, self.sibling, 2).wait_send()
+
+
+class ForwardIn(NamedTuple):
+    inputs: Any
+    small: Any
+    gain_rows: Any
+    w_mix: Any
+    w_out: Any
+    w_gu: Any
+    w_down: Any
+    seg_rows: Any
+    seg_cols: Any
+
+
+class ForwardOut(NamedTuple):
+    rows: Any
+    gains: Any
+    persist: Any
+    rates: Any
+
+
+class Kept(NamedTuple):
+    normed: Any
+    mix: Any
+    out: Any
+    gu: Any
+    down: Any
+    qkv: Any
+    gate: Any
+    recalled: Any
+    combined: Any
+    mid: Any
+    normed_two: Any
+    gate_up: Any
+    hidden: Any
+    out_rows: Any
+
+
+class ForwardScratch(NamedTuple):
+    gain_all: Any
+    small_all: Any
+    mix_away: Any
+    gu_away: Any
+    down_away: Any
+    zsend: Any
+    zrecv: Any
+    psend: Any
+    precv: Any
+    xsend: Any
+    xrecv: Any
+    gsend: Any
+    grecv: Any
+    csend: Any
+    crecv: Any
+    hsend: Any
+    hrecv: Any
+    saved: Any
+
+
+def each(parts, act):
+    for part in parts:
+        act(part)
+
+
+def forward_kernel(unit, *refs):
+    count = len(Kept._fields)
+    r, refs = refs[: len(ForwardIn._fields)], refs[len(ForwardIn._fields) :]
+    given = vars(named(ForwardIn._fields, r))
+    r, refs = refs[: len(ForwardOut._fields)], refs[len(ForwardOut._fields) :]
+    given |= vars(named(ForwardOut._fields, r))
+    in_hbm = [refs[:count], refs[count : 2 * count]]
+    refs = refs[2 * count :]
+    in_vmem = [refs[:count], refs[count : 2 * count]]
+    refs = refs[2 * count :]
+    scratch = PlaneScratch._fields[:6] + ForwardScratch._fields
+    r = types.SimpleNamespace(**given, **vars(named(scratch, refs)))
+    views = [types.SimpleNamespace(**vars(named(Kept._fields, part))) for part in in_vmem]
+    views[0].rows, views[1].rows = r.rows, views[0].out_rows
+
+    def save(layer, which):
+        for name in which:
+            index = Kept._fields.index(name)
+            yield pltpu.make_async_copy(
+                in_vmem[layer][index], in_hbm[layer][index], r.saved.at[layer, index]
+            )
+
+    place = here()
+    x, s, z = place
+    partner = peer(place, 1, False)
+    flips = [(dx, ds) for dx in (0, 1) for ds in range(4) if dx or ds]
+    plane = [((x + dx) % 2, (s + ds) % 4, z) for dx, ds in flips]
+    column = [(x, s, (z + dz) % 4) for dz in (1, 2, 3)]
+    column += [(1 - x, s, (z + dz) % 4) for dz in (1, 2, 3)]
+    barrier = pltpu.get_barrier_semaphore()
+    for other in plane + column:
+        pl.semaphore_signal(barrier, inc=1, device_id=other, device_id_type=MESH)
+    pl.semaphore_wait(barrier, len(plane) + len(column))
+
+    zsems, psems, xsems = (r.zsend, r.zrecv), (r.psend, r.precv), (r.xsend, r.xrecv)
+    holders = [*column, partner]
+
+    def gains_to(index):
+        return remote(r.gain_rows, r.gain_all.at[x, z], zsems, index, holders[index])
+
+    for index in range(7):
+        gains_to(index).start()
+    r.gain_all[x, z] = r.gain_rows[...]
+
+    mine, other = x * 4 + s, (1 - x) * 4 + s
+
+    def mix_part(which):
+        heads = [pl.ds(pl.multiple_of(kind * D + which * HD, HD), HD) for kind in range(4)]
+        return jnp.concatenate([r.w_mix[0, :, cols] for cols in heads], 1)
+
+    out_rows = pl.ds(pl.multiple_of(s % 2 * HD, HD), HD)
+    root = z == 2 * x + s // 2
+    rooted = z == 2 * (1 - x) + s // 2
+    for layer in (0, 1):
+        v = views[layer]
+
+        @pl.when(x == layer)
+        def _():
+            r.mix_away[...] = mix_part(other)
+            remote(r.mix_away, v.mix.at[z], xsems, 0, partner).start()
+            v.mix[z] = mix_part(mine)
+
+            @pl.when(rooted)
+            def _():
+                remote(r.w_out.at[0, out_rows], v.out, xsems, 1, partner).start()
+
+            @pl.when(root)
+            def _():
+                v.out[...] = r.w_out[0, out_rows, :]
+
+    for index in range(7):
+        gains_to(index).wait_recv()
+    for layer in range(2):
+        for owner in range(4):
+            for kind in range(2):
+                for half in range(2):
+                    begin = owner * 2 * HD + half * HD
+                    row = 2 * kind + half
+                    r.gains[layer, kind : kind + 1, begin : begin + HD] = r.gain_all[
+                        layer, owner, row : row + 1, :
+                    ]
+    size = r.rows.shape[1]
+    own_half = pl.ds(pl.multiple_of(x * size, size), size)
+    arriving = [SeqGather(views[0].normed, batch, r.gsend, r.grecv) for batch in range(2)]
+    for batch, gather in enumerate(arriving):
+        rows = r.inputs[batch, 0].astype(F32)
+        gather.start((rows * rms_scale(rows) * r.gains[0, 0:1, :]).astype(BF))
+        r.rows[batch] = r.inputs[batch, 0, own_half, :]
+
+    for index in range(7):
+        remote(r.small, r.small_all.at[x, s], psems, index, plane[index]).start()
+    r.small_all[x, s] = r.small[...]
+
+    padded = r.down_away.shape[0]
+    width = 8 * unit + 64
+
+    def select(which, offset):
+        begin = lax.broadcasted_iota(jnp.int32, (width, 128), 0) - offset
+        col = lax.broadcasted_iota(jnp.int32, (width, 128), 1)
+        return jnp.where((begin == which * unit + col) & (col < unit), 1.0, 0.0).astype(BF)
+
+    def gu_part(which, out):
+        for owner in range(4):
+            base = owner * 8 * unit
+            offset = base % 128
+            chosen = select(which, offset)
+            for side in range(2):
+                begin = side * FF + base - offset
+                part = nn(r.w_gu[0, :, begin : begin + width], chosen).astype(BF)
+                at = side * 4 * padded + owner * padded
+                out[:, at : at + padded] = part[:, :padded]
+
+    def down_part(which, out):
+        row = lax.broadcasted_iota(jnp.int32, (padded, 8 * unit), 0)
+        col = lax.broadcasted_iota(jnp.int32, (padded, 8 * unit), 1)
+        chosen = jnp.where((col == which * unit + row) & (row < unit), 1.0, 0.0).astype(BF)
+        out[...] = nn(chosen, r.w_down[0]).astype(BF)
+
+    gu_part(other, r.gu_away)
+    down_part(other, r.down_away)
+    for layer in (0, 1):
+        v = views[layer]
+
+        @pl.when(x == layer)
+        def _():
+            remote(r.gu_away, v.gu.at[z], xsems, 2, partner).start()
+            remote(r.down_away, v.down.at[z], xsems, 3, partner).start()
+            gu_part(mine, v.gu.at[z])
+            down_part(mine, v.down.at[z])
+
+    mixers, feeds = [], []
+    for layer, v in enumerate(views):
+        sems = [(r.csend.at[3 * layer + i], r.crecv.at[3 * layer + i]) for i in range(3)]
+        mixers.append(
+            [
+                ColumnGather(v.mix, *sems[0]),
+                RootGather(v.out, r.hsend.at[layer], r.hrecv.at[layer]),
+            ]
+        )
+        feeds.append([ColumnGather(v.gu, *sems[1]), ColumnGather(v.down, *sems[2])])
+
+    def swapped(layer, index):
+        v = views[layer]
+        landing = [v.mix.at[z], v.out, v.gu.at[z], v.down.at[z]][index]
+        here_from = remote(landing, landing, xsems, index, partner)
+
+        @pl.when((x != layer) & root if index == 1 else x != layer)
+        def _():
+            here_from.wait_recv()
+
+    def start_mixer(layer):
+        for index, part in enumerate(mixers[layer]):
+            swapped(layer, index)
+            part.start()
+
+    def start_feed(layer):
+        for index, part in enumerate(feeds[layer]):
+            swapped(layer, 2 + index)
+            part.start()
+
+    start_mixer(0)
+    arriving[0].forward()
+    each(mixers[0], lambda part: part.hop())
+    start_feed(0)
+    arriving[1].forward()
+
+    for index in range(7):
+        dx, ds = flips[index]
+        landing = r.small_all.at[(x + dx) % 2, (s + 4 - ds) % 4]
+        remote(r.small, landing, psems, index, plane[index]).wait_recv()
+    for layer in range(2):
+        begin = pl.multiple_of(s % 2 * 32, 32)
+        rows = r.small_all[layer, 2 * x + s // 2, pl.ds(begin, 32), :]
+        r.persist[layer] = rows.astype(BF).reshape(2, 16, HD)
+        begin = pl.multiple_of(64 + s % 2 * 8, 8)
+        r.rates[layer] = r.small_all[layer, 2 * x + s // 2, pl.ds(begin, 8), :]
+
     length = r.part.shape[1]
-    last = not hasattr(r, "normed_next")
-
-    def project(batch):
+
+    def project(layer, batch):
+        v = views[layer]
+
         def block(rows, begin):
-            proj = nn(r.normed[batch, rows, :], r.mix[...])
-            r.qkv[batch, rows, :] = proj[:, : 3 * HD].astype(BF)
-            r.gate[batch, rows, :] = jax.nn.sigmoid(proj[:, 3 * HD :])
+            proj = nn(v.normed[batch, rows, :], flat(v.mix))
+            v.qkv[batch, rows, :] = proj[:, : 3 * HD].astype(BF)
+            v.gate[batch, rows, :] = jax.nn.sigmoid(proj[:, 3 * HD :])
 
         in_blocks(length, 256, block)
 
-    def mixer(batch):
+    def mixer(layer, batch):
+        v = views[layer]
+
         def block(rows, begin):
-            values = r.qkv[batch, :, 2 * HD :]
+            values = v.qkv[batch, :, 2 * HD :]
             inner, decay_w, _, probs, per_probs = weights_of_scores(
-                r.qkv[batch, rows, :HD],
-                r.qkv[batch, :, HD : 2 * HD],
-                r.pkeys[...],
+                v.qkv[batch, rows, :HD],
+                v.qkv[batch, :, HD : 2 * HD],
+                r.persist[layer, 0],
                 r.seg_rows[batch, rows, :],
                 r.seg_cols[batch],
                 begin,
-                r.rate[...],
+                r.rates[layer, 0:1, 0:1],
             )
-            attended = nn(probs.astype(BF), values) + nn(per_probs.astype(BF), r.pvalues[...])
+            attended = nn(probs.astype(BF), values) + nn(per_probs.astype(BF), r.persist[layer, 1])
             recalled = nn((inner * decay_w).astype(BF), values).astype(BF)
-            r.recalled[batch, rows, :] = recalled
+            v.recalled[batch, rows, :] = recalled
             combined = attended.astype(BF).astype(F32)
-            combined = combined + r.gate[batch, rows, :] * recalled.astype(F32)
+            combined = combined + v.gate[batch, rows, :] * recalled.astype(F32)
             combined = combined.astype(BF)
-            r.combined[batch, rows, :] = combined
-            r.part[batch, rows, :] = nn(combined, r.out[...]).astype(BF)
+            v.combined[batch, rows, :] = combined
+            r.part[batch, rows, :] = nn(combined, v.out[...]).astype(BF)
 
         in_blocks(length, 128, block)
 
-    def feed(batch):
+    def feed(layer, batch):
+        v = views[layer]
+
         def block(rows, begin):
-            gate_up = nn(r.normed_two[batch, rows, :], r.gu[...])
-            r.gate_up[batch, rows, :] = gate_up
+            gate_up = nn(v.normed_two[batch, rows, :], flat(v.gu))
+            v.gate_up[batch, rows, :] = gate_up
             half = gate_up.shape[1] // 2
             hidden = (jax.nn.silu(gate_up[:, :half]) * gate_up[:, half:]).astype(BF)
-            r.hidden[batch, rows, :] = hidden
-            r.part[batch, rows, :] = nn(hidden, r.down[...]).astype(BF)
+            v.hidden[batch, rows, :] = hidden
+            r.part[batch, rows, :] = nn(hidden, flat(v.down)).astype(BF)
 
         in_blocks(length, 256, block)
 
@@ -893,46 +1231,74 @@
 
     def send_normed(batch, own, gain, full):
         gather = Gather(full, batch, r.gsend, r.grecv)
-        gather.start((own * rms_scale(own) * gain[...]).astype(BF))
+        gather.start((own * rms_scale(own) * gain).astype(BF))
         return gather
 
-    meet()
-    first, second = (scatter(batch) for batch in range(2))
-    project(0)
-    mixer(0)
-    first.start()
-    first.forward()
-    project(1)
-    mixer(1)
-    second.start()
-    second.forward()
-    gathers = []
-    for batch, part in enumerate((first, second)):
-        mid = r.rows[batch] + part.finish()
-        r.mid[batch] = mid
-        gathers.append(send_normed(batch, mid, r.gain_two, r.normed_two))
-    first, second = (scatter(batch) for batch in range(2))
-    for batch, part in enumerate((first, second)):
-        gathers[batch].forward()
-        gathers[batch].finish()
-        feed(batch)
-        part.start()
-        part.forward()
-    gathers = []
-    for batch, part in enumerate((first, second)):
-        own = (r.mid[batch] + part.finish()).astype(BF)
-        r.out_rows[batch] = own
-        if not last:
-            gathers.append(
-                send_normed(batch, own.astype(F32), r.gain_next, r.normed_next)
-            )
-    for gather in gathers:
-        gather.forward()
-    for gather in gathers:
-        gather.finish()
-
-
-def backward_layer(ins, outs, *refs):
+    mixer_names = Kept._fields[:3] + Kept._fields[5:9]
+    for layer, v in enumerate(views):
+        parts = []
+        for batch in range(2):
+            if layer == 1:
+                arriving[batch].forward()
+            arriving[batch].finish()
+            if batch == 0:
+                each(mixers[layer], lambda part: part.finish())
+            project(layer, batch)
+            mixer(layer, batch)
+            part = scatter(batch)
+            part.start()
+            part.forward()
+            parts.append(part)
+        each(save(layer, mixer_names), lambda copy: copy.start())
+        gathers = []
+        for batch, part in enumerate(parts):
+            mid = v.rows[batch].astype(F32) + part.finish()
+            v.mid[batch] = mid
+            gathers.append(send_normed(batch, mid, r.gains[layer, 1:2, :], v.normed_two))
+        each(feeds[layer], lambda part: part.hop())
+        if layer == 0:
+            start_mixer(1)
+        parts = []
+        for batch, gather in enumerate(gathers):
+            gather.forward()
+            gather.finish()
+            if batch == 0:
+                each(feeds[layer], lambda part: part.finish())
+            feed(layer, batch)
+            part = scatter(batch)
+            part.start()
+            part.forward()
+            parts.append(part)
+        if layer == 0:
+            each(mixers[1], lambda part: part.hop())
+            start_feed(1)
+        each(save(layer, Kept._fields[3:5] + Kept._fields[9:13]), lambda copy: copy.start())
+        arriving = []
+        for batch, part in enumerate(parts):
+            rows = (v.mid[batch] + part.finish()).astype(BF)
+            v.out_rows[batch] = rows
+            if layer == 0:
+                gain = r.gains[1, 0:1, :]
+                arriving.append(send_normed(batch, rows.astype(F32), gain, views[1].normed))
+        each(save(layer, Kept._fields[13:]), lambda copy: copy.start())
+
+    for layer in range(2):
+        for copy in save(layer, Kept._fields):
+            copy.wait()
+    remote(r.mix_away, r.mix_away, xsems, 0, partner).wait_send()
+    remote(r.gu_away, r.gu_away, xsems, 2, partner).wait_send()
+    remote(r.down_away, r.down_away, xsems, 3, partner).wait_send()
+
+    @pl.when(rooted)
+    def _():
+        remote(views[0].out, views[0].out, xsems, 1, partner).wait_send()
+
+    for index in range(7):
+        gains_to(index).wait_send()
+        remote(r.small, r.small_all.at[x, s], psems, index, plane[index]).wait_send()
+
+
+def backward_layer(layer, ins, outs, *refs):
     scratch = fields(PlaneScratch, BackwardScratch)
     earlier = len(outs) == len(fields(BackwardOut, EarlyOut))
     if earlier:
@@ -941,19 +1307,19 @@
     length = r.part.shape[1]
     last = not hasattr(r, "grad_next")
     sums = [
-        ColumnSum(r.own_gu, r.gu_slots, r.gu_sum, r.csend, r.crecv, 0),
-        ColumnSum(r.own_down, r.down_slots, r.down_sum, r.csend, r.crecv, 1),
+        ColumnSum(r.own_gu, r.gu_slots, r.gu_sum, r.csend.at[0], r.crecv.at[0]),
+        ColumnSum(r.own_down, r.down_slots, r.down_sum, r.csend.at[1], r.crecv.at[1]),
     ]
     early = []
     if earlier:
         early = [
-            ColumnSum(r.early_mix, r.mix_slots, r.mix_sum, r.csend, r.crecv, 2),
+            ColumnSum(r.early_mix, r.mix_slots, r.mix_sum, r.csend.at[2], r.crecv.at[2]),
             RootSum(r.early_out, r.root_slots, r.out_sum, r.rsend, r.rrecv),
         ]
 
     def feed_back(batch):
         def block(rows, begin):
-            grad_hidden = nt(r.grad_full[batch, rows, :], r.down[...])
+            grad_hidden = nt(r.grad_full[batch, rows, :], flat(r.down))
             half = grad_hidden.shape[1]
             gate_part = r.gate_up[batch, rows, :half]
             up_part = r.gate_up[batch, rows, half:]
@@ -962,7 +1328,7 @@
             grad_gate = grad_hidden * up_part * (sig_part + silu * (1.0 - sig_part))
             r.grad_gu[batch, rows, :half] = grad_gate.astype(BF)
             r.grad_gu[batch, rows, half:] = (grad_hidden * silu).astype(BF)
-            r.part[batch, rows, :] = nt(r.grad_gu[batch, rows, :], r.gu[...]).astype(BF)
+            r.part[batch, rows, :] = nt(r.grad_gu[batch, rows, :], flat(r.gu)).astype(BF)
 
         in_blocks(length, 256, block)
 
@@ -1001,13 +1367,13 @@
             inner, decay_w, distance, probs, per_probs = weights_of_scores(
                 query,
                 keys,
-                r.pkeys[...],
+                r.persist[layer, 0],
                 r.seg_rows[batch, rows, :],
                 r.seg_cols[batch],
                 begin,
-                r.rate[...],
+                r.rates[layer, 0:1, 0:1],
             )
-            per_dp = nt(attn_rows, r.pvalues[...])
+            per_dp = nt(attn_rows, r.persist[layer, 1])
             seq_dp = nt(attn_rows, values)
             delta = jnp.sum(per_probs * per_dp, axis=1, keepdims=True) + jnp.sum(
                 probs * seq_dp, axis=1, keepdims=True
@@ -1019,7 +1385,7 @@
             memory = inner * decay_w
             rate_terms = weighted * inner * distance
             r.grad_rate[...] -= jnp.sum(rate_terms, axis=0, keepdims=True)
-            grad_query = (nn(per_ds, r.pkeys[...]) + nn(seq_ds, keys)) * scale
+            grad_query = (nn(per_ds, r.persist[layer, 0]) + nn(seq_ds, keys)) * scale
             grad_query = grad_query + nn(grad_inner, keys)
             r.grad_proj[batch, rows, :HD] = grad_query.astype(BF)
             r.grad_keys[...] += tn(seq_ds, query) * scale + tn(grad_inner, query)
@@ -1034,7 +1400,7 @@
         r.grad_proj[batch, :, 2 * HD : 3 * HD] = r.grad_values[...].astype(BF)
 
         def back(rows, begin):
-            r.part[batch, rows, :] = nt(r.grad_proj[batch, rows, :], r.mix[...]).astype(BF)
+            r.part[batch, rows, :] = nt(r.grad_proj[batch, rows, :], flat(r.mix)).astype(BF)
 
         in_blocks(length, 256, back)
 
@@ -1044,7 +1410,7 @@
     def through_norm(batch, part, rows, gain):
         grad_normed = part.finish()
         inverse = rms_scale(rows)
-        return norm_back(grad_normed, rows * inverse, inverse, gain[...])
+        return norm_back(grad_normed, rows * inverse, inverse, gain)
 
     meet(True)
     r.grad_rate[...] = jnp.zeros_like(r.grad_rate)
@@ -1056,24 +1422,22 @@
         feed_back(batch)
         part.start()
         part.forward()
+    for column in early:
+        column.hop()
     feed_weights()
+    for column in sums:
+        column.start()
     gathers = []
     gain_sums = []
     for batch, part in enumerate((first, second)):
-        grad_mid, gain_sum = through_norm(batch, part, r.mid[batch], r.gain_two)
+        grad_mid, gain_sum = through_norm(batch, part, r.mid[batch], r.gains[layer, 1:2, :])
         gain_sums.append(gain_sum[None])
-        grad_mid = grad_mid + r.grad_rows[batch]
+        grad_mid = grad_mid + r.grad_rows[batch].astype(F32)
         r.grad_mid[batch] = grad_mid
         gather = Gather(r.branch, batch, r.gsend, r.grecv)
         gather.start(grad_mid.astype(BF))
         gathers.append(gather)
-    r.gains[1:2] = gain_sums[0] + gain_sums[1]
-    for column in early:
-        column.hop(1)
-    for column in early:
-        column.hop(2)
-    for column in sums:
-        column.start()
+    r.gain_sums[1:2] = gain_sums[0] + gain_sums[1]
     first, second = (scatter(batch) for batch in range(2))
     for batch, part in enumerate((first, second)):
         gathers[batch].forward()
@@ -1082,17 +1446,17 @@
         part.start()
         part.forward()
         if batch == 0:
-            for column in early:
-                column.finish()
             for column in sums:
-                column.hop(1)
+                column.hop()
     product(r.grad_mix, r.normed, r.grad_proj)
     grad_out = tn(r.combined[0], r.branch[0]) + tn(r.combined[1], r.branch[1])
     r.grad_out[...] = grad_out.astype(BF)
     gathers = []
     gain_sums = []
     for batch, part in enumerate((first, second)):
-        grad_h, gain_sum = through_norm(batch, part, r.rows[batch], r.gain_one)
+        grad_h, gain_sum = through_norm(
+            batch, part, r.rows[batch].astype(F32), r.gains[layer, 0:1, :]
+        )
         gain_sums.append(gain_sum[None])
         grad_h = (grad_h + r.grad_mid[batch]).astype(BF)
         r.grad_h[batch] = grad_h
@@ -1100,14 +1464,12 @@
             gather = Gather(r.grad_next, batch, r.gsend, r.grecv)
             gather.start(grad_h)
             gathers.append(gather)
-    r.gains[0:1] = gain_sums[0] + gain_sums[1]
-    for column in sums:
-        column.hop(2)
+    r.gain_sums[0:1] = gain_sums[0] + gain_sums[1]
     for gather in gathers:
         gather.forward()
     for gather in gathers:
         gather.finish()
-    for column in sums:
+    for column in early + sums:
         column.finish()
 
 
@@ -1124,7 +1486,7 @@
     psend, precv, osend, orecv, rsend, rrecv, zsend, zrecv, ssend, srecv, *sems = sems
     csend, crecv, hsend, hrecv = sems
     columns = [
-        ColumnSum(by_layer[0][0], mix_slots, mix_sum, csend, crecv, 0),
+        ColumnSum(by_layer[0][0], mix_slots, mix_sum, csend, crecv),
         RootSum(by_layer[0][3], root_slots, out_sum, hsend, hrecv),
     ]
     by_layer[0][0], by_layer[0][3] = mix_sum, out_sum
@@ -1206,9 +1568,7 @@
     for index in range(7):
         to_plane(index).start()
     for column in columns:
-        column.hop(1)
-    for column in columns:
-        column.hop(2)
+        column.hop()
     turn((1, 2))
     for column in columns:
         column.finish()
@@ -1279,13 +1639,14 @@
             out_copy(index, sibling).wait_send()
 
 
-def kernel_call(kernel, number, operands, outs, scratch):
+def kernel_call(kernel, number, operands, outs, scratch, spaces=None):
     vmem = pl.BlockSpec(memory_space=pltpu.VMEM)
+    spaces = spaces or [pltpu.VMEM] * len(outs)
     return pl.pallas_call(
         kernel,
         out_shape=outs,
         in_specs=[vmem] * len(operands),
-        out_specs=[vmem] * len(outs),
+        out_specs=[pl.BlockSpec(memory_space=space) for space in spaces],
         scratch_shapes=scratch,
         compiler_params=pltpu.CompilerParams(
             collective_id=number, has_side_effects=True, vmem_limit_bytes=58 * 2**20
@@ -1308,40 +1669,68 @@
     ]
 
 
-def forward_call(number, given, last):
-    count, length, _ = given.normed.shape
-    half = given.down.shape[0]
+def forward_call(number, *operands):
+    inputs, small, _, w_mix, _, _, w_down, *_ = operands
+    count, _, tokens, _ = inputs.shape
+    depth, length = w_mix.shape[1], 4 * tokens
+    unit = w_down.shape[1] // 8
+    padded = -(-unit // 32) * 32
     shape = jax.ShapeDtypeStruct
-    outs = dict(
+    outs = ForwardOut(
+        rows=shape((count, length // 8, D), BF),
+        gains=shape((2, 2, D), F32),
+        persist=shape((2, 2, 16, HD), BF),
+        rates=shape((2, 8, HD), F32),
+    )
+    kept = Kept(
+        normed=shape((count, length, D), BF),
+        mix=shape((4, depth, 4 * HD), BF),
+        out=shape((HD, D), BF),
+        gu=shape((4, depth, 8 * padded), BF),
+        down=shape((4, padded, D), BF),
         qkv=shape((count, length, 3 * HD), BF),
         gate=shape((count, length, HD), F32),
         recalled=shape((count, length, HD), BF),
         combined=shape((count, length, HD), BF),
         mid=shape((count, length // 8, D), F32),
         normed_two=shape((count, length, D), BF),
-        gate_up=shape((count, length, 2 * half), F32),
-        hidden=shape((count, length, half), BF),
+        gate_up=shape((count, length, 8 * padded), F32),
+        hidden=shape((count, length, 4 * padded), BF),
         out_rows=shape((count, length // 8, D), BF),
-        normed_next=shape((count, length, D), BF),
-    )
-    if last:
-        del outs[ForwardOut._fields[-1]]
-    operands = [getattr(given, name) for name in ForwardIn._fields]
-    kernel = functools.partial(forward_layer, ForwardIn._fields, tuple(outs))
-    found = kernel_call(kernel, number, operands, list(outs.values()), scatter_scratch(length))
-    return named(outs, found)
-
-
-def backward_call(number, given, last):
+    )
+    scratch = [pltpu.VMEM(part.shape, part.dtype) for part in (*kept, *kept)]
+    scratch += scatter_scratch(length)[:6]
+    scratch += [
+        pltpu.VMEM((2, 4, 8, HD), F32),
+        pltpu.VMEM((2, 4) + small.shape, F32),
+        pltpu.VMEM((depth, 4 * HD), BF),
+        pltpu.VMEM((depth, 8 * padded), BF),
+        pltpu.VMEM((padded, D), BF),
+        *pairs_of((7,), (7,), (4,), (2, 7), (6, 4), (2, 2)),
+        pltpu.SemaphoreType.DMA((2, len(kept))),
+    ]
+    kernel = functools.partial(forward_kernel, unit)
+    specs = [pltpu.VMEM] * len(outs) + [pl.ANY] * (2 * len(kept))
+    found = kernel_call(kernel, number, operands, [*outs, *kept, *kept], scratch, specs)
+    own, found = found[: len(outs)], found[len(outs) :]
+    return (
+        named(ForwardOut._fields, own),
+        named(Kept._fields, found[: len(kept)]),
+        named(Kept._fields, found[len(kept) :]),
+    )
+
+
+def backward_call(number, layer, given):
     count, length, _ = given.normed.shape
-    half = given.down.shape[0]
+    half = 4 * given.down.shape[1]
+    last = layer == 0
     depth = D // 4
     shape = jax.ShapeDtypeStruct
     outs = dict(
         grad_mix=shape((4, depth, 4 * HD), BF),
         grad_out=shape((HD, D), BF),
-        gains=shape((2, D), F32),
-        grad_persist=shape((2,) + given.pkeys.shape, F32),
+        gain_sums=shape((2, D), F32),
+        grad_persist=shape(given.persist.shape[1:], F32),
         grad_rate=shape((1, length), F32),
         gu_sum=shape((depth, 2 * half), BF),
         down_sum=shape((half // 4, D), BF),
@@ -1362,20 +1751,19 @@
         pltpu.VMEM((4, half // 4, D), BF),
         pltpu.VMEM((count, length, D), BF),
         pltpu.VMEM((count, length // 8, D), F32),
-        pltpu.VMEM((2, 3, depth, 2 * half), BF),
-        pltpu.VMEM((2, 3, half // 4, D), BF),
-        *pairs_of((3, 2, 3)),
+        pltpu.VMEM((4, depth, 2 * half), BF),
+        pltpu.VMEM((4, half // 4, D), BF),
+        *pairs_of((3, 4)),
     ]
     if last:
         scratch += [
-            pltpu.VMEM((2, 3, depth, 4 * HD), BF),
+            pltpu.VMEM((4, depth, 4 * HD), BF),
             pltpu.VMEM((2, HD, D), BF),
             *pairs_of((2,)),
         ]
-    kernel = functools.partial(backward_layer, ins, tuple(outs))
+    kernel = functools.partial(backward_layer, layer, ins, tuple(outs))
     operands = [getattr(given, name) for name in ins]
-    found = kernel_call(kernel, number, operands, list(outs.values()), scratch)
-    return named(outs, found)
+    return named(outs, kernel_call(kernel, number, operands, list(outs.values()), scratch))
 
 
 def final_call(number, by_layer, small):
@@ -1389,9 +1777,9 @@
         pltpu.VMEM((3,) + small.shape[1:], F32),
         pltpu.VMEM(mix.shape, BF),
         pltpu.VMEM(out.shape, BF),
-        pltpu.VMEM((2, 3) + mix.shape, BF),
+        pltpu.VMEM((4,) + mix.shape, BF),
         pltpu.VMEM((2,) + out.shape, BF),
-        *pairs_of((3, 7), (4,), (2,), (3,), (7,), (1, 2, 3), (2,)),
+        *pairs_of((3, 7), (4,), (2,), (3,), (7,), (4,), (2,)),
     ]
     return kernel_call(final_kernel, number, operands, outs, scratch)
 
@@ -1454,103 +1842,49 @@
     length = tokens * ns
     size = length // width
     depth = w_mix.shape[1]
-    unit = w_down.shape[1] // width
-
-    heads = w_mix[0].reshape(depth, 4, H, HD)
-    halves = w_gu[0].reshape(depth, 2, nz, width, unit)
-    downs = w_down[0].reshape(width, unit, D)
-    more = -unit % 32
-
-    def pick(which):
-        both = lax.dynamic_index_in_dim(halves, which, 3, keepdims=False)
-        both = jnp.pad(both, ((0, 0), (0, 0), (0, 0), (0, more)))
-        down = lax.dynamic_index_in_dim(downs, which, 0, keepdims=False)
-        return (
-            lax.dynamic_index_in_dim(heads, which, 2, keepdims=False).reshape(depth, 4 * HD),
-            both.reshape(depth, 2 * nz * (unit + more)),
-            jnp.pad(down, ((0, more), (0, 0))),
-        )
+    unit = w_down.shape[1] // (nx * ns)
 
     def layers(own, got):
         return (jnp.where(first, own, got), jnp.where(first, got, own))
 
-    swap = [(0, 1), (1, 0)]
-    parts = [layers(o, lax.ppermute(g, "section", swap)) for o, g in zip(pick(mine), pick(other))]
-    out_rows = lax.dynamic_index_in_dim(
-        w_out[0].reshape(2, HD, D), lax.rem(s, 2), 0, keepdims=False
-    )
-    out_all = lax.all_gather(out_rows, "shard", axis=0)
-    out_own = lax.dynamic_index_in_dim(out_all, mine // 2, 0, keepdims=False)
-    out_got = lax.ppermute(
-        lax.dynamic_index_in_dim(out_all, other // 2, 0, keepdims=False), "section", swap
-    )
-    out_w = layers(out_own, out_got)
-    mix_w, gu_w, down_w = (
-        [lax.all_gather(part[layer], "shard", axis=0, tiled=True) for layer in range(2)]
-        for part in parts
-    )
-
-    small = jnp.concatenate([persist_kv[0].reshape(-1).astype(F32), memory_decay[0]])
-    small = lax.all_gather(small, ("section", "seq"), axis=0)
-    rates = small[:, -2:].reshape(2, H)[:, mine]
-    persist = small[:, :-2].astype(BF).reshape(2, ns, 2, persist_kv.shape[2], 2, HD)
-    persist = lax.dynamic_index_in_dim(persist, mine // 2, 1, keepdims=False)
-    persist = lax.dynamic_index_in_dim(persist, lax.rem(mine, 2), 3, keepdims=False)
-    gains = lax.all_gather(norm_gains[0], ("section", "shard"), axis=0, tiled=True)
-    gains = gains.astype(F32).reshape(2, 1, D, 2)
-
-    def own_rows(whole):
-        return lax.dynamic_slice_in_dim(whole[:, 0], x * size, size, 1).astype(F32)
-
+    small = persist_kv[0].reshape(-1, 2, HD).transpose(1, 0, 2).reshape(-1, HD).astype(F32)
+    rates = jnp.broadcast_to(memory_decay[0][:, None, None], (2, 8, HD)).reshape(-1, HD)
+    gain_rows = norm_gains[0].astype(F32).T.reshape(-1, HD)
+    gain_rows = jnp.pad(gain_rows, ((0, 8 - gain_rows.shape[0]), (0, 0)))
+    small = jnp.concatenate([small, rates], 0)
+    segments = (segment_ids[:, 0, :, None], segment_ids)
+    ready, below, above = forward_call(
+        1, inputs, small, gain_rows, w_mix, w_out, w_gu, w_down, *segments
+    )
+    shared = dict(
+        gains=ready.gains,
+        persist=ready.persist,
+        rates=ready.rates,
+        seg_rows=segments[0],
+        seg_cols=segments[1],
+    )
+    lower = dict(shared, rows=ready.rows)
+    upper = dict(shared, rows=below.out_rows)
+    outputs = [below.out_rows, above.out_rows]
     cot_full = lax.all_gather(cotangent[:, 0], "seq", axis=1, tiled=True)
-    rows = own_rows(inputs)
-    full = jax.ShapeDtypeStruct((count, length, D), BF)
-    (normed,) = kernel_call(
-        start_kernel, 0, (rows, gains[0, :, :, 0]), [full], pairs_of((2, 7))
-    )
-    of_layer = [
-        dict(
-            mix=mix_w[layer],
-            out=out_w[layer],
-            gu=gu_w[layer],
-            down=down_w[layer],
-            gain_one=gains[layer, :, :, 0],
-            gain_two=gains[layer, :, :, 1],
-            gain_next=gains[1, :, :, 0],
-            pkeys=persist[layer, 0],
-            pvalues=persist[layer, 1],
-            rate=rates[layer].reshape(1, 1),
-            seg_rows=segment_ids[:, 0, :, None],
-            seg_cols=segment_ids,
-        )
-        for layer in range(2)
-    ]
-    outputs = []
-    for layer in range(2):
-        of_layer[layer] |= dict(normed=normed, rows=rows)
-        found = forward_call(1 + layer, types.SimpleNamespace(**of_layer[layer]), layer == 1)
-        of_layer[layer] |= vars(found)
-        outputs.append(found.out_rows)
-        if layer == 0:
-            normed = found.normed_next
-            rows = found.out_rows.astype(F32)
-    given = dict(of_layer[1], grad_full=cot_full, grad_rows=own_rows(cotangent))
-    later = backward_call(3, types.SimpleNamespace(**given), False)
-    given = dict(
-        of_layer[0],
+    cot_rows = lax.dynamic_slice_in_dim(cotangent[:, 0], x * size, size, 1)
+    upper |= dict(vars(above), grad_full=cot_full, grad_rows=cot_rows)
+    later = backward_call(3, 1, types.SimpleNamespace(**upper))
+    lower |= dict(
+        vars(below),
         grad_full=later.grad_next,
-        grad_rows=later.grad_h.astype(F32),
+        grad_rows=later.grad_h,
         early_mix=later.grad_mix,
         early_out=later.grad_out,
     )
-    earlier = backward_call(4, types.SimpleNamespace(**given), True)
+    earlier = backward_call(4, 0, types.SimpleNamespace(**lower))
     by_layer = [
         (earlier.grad_mix, earlier.gu_sum, earlier.down_sum, earlier.grad_out),
         (earlier.mix_sum, later.gu_sum, later.down_sum, earlier.out_sum),
     ]
     both = (earlier, later)
     grads = [found.grad_h for found in both]
-    gain_sums = [found.gains for found in both]
+    gain_sums = [found.gain_sums for found in both]
 
     memory_all = jnp.stack([found.grad_persist for found in both], 0).reshape(-1, HD)
     rate_all = jnp.stack([jnp.sum(found.grad_rate) for found in both])

time: 574 us -> 468 us (0.82)
  blocking collectives: 64.6 us -> 0 us
  waiting for transfers between devices: 17.2 us -> 0.68 us
  local copies, waits for them, and re-layouts: 25.3 us -> 10.6 us
    all_gather x3 -> x0, blocking collectives: 64.6 us -> none  [the longest x2 48.9 us: tensor_parallel(): lax.all_gather(part[layer], 'shard', axis=0, tiled=True)]
    ppermute x4 -> x0, waiting for transfers between devices: 15 us -> none  [the longest x3 15 us: tensor_parallel(): lax.ppermute(g, 'section', swap)]
    unnamed x43 -> x24, local copies, waits for them, and re-layouts: 9.26 us -> 3.04 us
    convert_element_type x5 -> x0, other arithmetic: 6.05 us -> none  [the longest x1 1.79 us: tensor_parallel(): later.grad_h.astype(F32)]
    pallas_call x6 -> x4, Pallas kernels: 412 us -> 414 us  [kernel_call(): pl.pallas_call(kernel, out_shape=outs, in_specs=[vmem] * len(operands), o...]
  transfers between devices with their start and end apart: 11 -> 1, of which waited for: 2 -> 0; matrix products, arithmetic and copies ran while one was open for 4% -> 1% of each run, Pallas kernels for 27% -> 40%
where the time goes in v5:
time: 468 us; the launch traced here: 462 us
  Pallas kernels  420 us (90%)
  other arithmetic  16.9 us (4%)
  between operations  14.4 us (3%)
  local copies, waits for them, and re-layouts  10.6 us (2%)
    pallas_call x4, Pallas kernels, kernel_call(): pl.pallas_call(kernel, out_shape=outs, in_specs=[vmem] * len(operands), o...  414 us
  transfers between devices with their start and end apart: 1, of which 0 were waited for; matrix products, arithmetic and copies ran while one was open for 1% of the time, Pallas kernels for 40%

profile of v5, /device:TPU:3, one launch (start us, length us, event | category | flops | bytes accessed | tf_op | source)
XLA Modules:
  0.0 462.1 jit_solution(167675907865954637)
XLA Ops:
  7.9 0.7 reduce
  8.6 1.0 broadcast_in_dim_squeeze.5.refs_7_.refs_11_
  9.6 0.7 reshape.103
  10.4 0.7 broadcast_in_dim.28
  13.2 184.7 %shard_map.169 = (bf16[2,64,1024]{2,1,0:T(8,128)(2,1)}, f32[2,2,1024]{2,1,0:T(2,128)}, bf16[2,2,16,128]{3,2,1,0:T(8,128)(2,1)}, f32[2,8,128]{2,1,0:T(8,128)}, bf...) custom-call(bf16[2,1,128,1024]{3,2,1,0:T(8,128)(2,1)} %refs_0_.1, ...), custom_call_target="tpu_custom_call" | custom-call | tf_op jit(solution)/shard_map/pallas_call | solution.py:1645
  198.0 0.7 dynamic-slice_bitcast_fusion.refs_1_
  198.7 68.7 %shard_map.170 = (bf16[4,256,512]{2,1,0:T(8,128)(2,1)}, bf16[128,1024]{1,0:T(8,128)(2,1)}, f32[2,1024]{1,0:T(2,128)}, f32[2,16,128]{2,1,0:T(8,128)}, f32[1,512]{...) custom-call(bf16[2,512,1024]{2,1,0:T(8,128)(2,1)} %bitcast.52, ...), custom_call_target="tpu_custom_call" | custom-call | tf_op jit(solution)/shard_map/pallas_call | solution.py:1645
  267.4 87.3 %shard_map.171 = (bf16[4,256,512]{2,1,0:T(8,128)(2,1)}, bf16[128,1024]{1,0:T(8,128)(2,1)}, f32[2,1024]{1,0:T(2,128)}, f32[2,16,128]{2,1,0:T(8,128)}, f32[1,512]{...) custom-call(bf16[2,512,1024]{2,1,0:T(8,128)(2,1)} %get-tuple-element, ...), custom_call_target="tpu_custom_call" | custom-call | tf_op jit(solution)/shard_map/pallas_call | solution.py:1645
  354.8 1.3 reduce_sum.27
  356.7 0.7 pad_maximum_fusion.3
  357.5 0.7 pad_maximum_fusion.2
  358.2 1.4 maximum_bitcast_fusion.2
  360.3 73.2 %shard_map.172 = (bf16[2,4,256,512]{3,2,1,0:T(8,128)(2,1)}, bf16[2,4,256,768]{3,2,1,0:T(8,128)(2,1)}, bf16[2,4,96,1024]{3,2,1,0:T(8,128)(2,1)}, bf16[2,128,1024]...) custom-call(bf16[4,256,512]{2,1,0:T(8,128)(2,1)} %get-tuple-element.106.refs, ...), custom_call_target="tpu_custom_call" | custom-call | tf_op jit(solution)/shard_map/pallas_call | solution.py:1645
  433.5 1.8 select_bitcast_fusion.1
  435.2 1.8 broadcast_select_fusion.2
  437.0 1.1 bitcast_convert_fusion
  438.1 1.0 slice_reduce_fusion
  439.1 0.8 constant_dynamic-slice_fusion
  441.2 2.0 fusion
  443.3 1.9 maximum_bitcast_fusion
  445.1 1.4 dynamic-slice_reduce_fusion
  446.5 1.6 copy-done.1
  448.1 1.4 copy-done.2
  449.5 5.6 %shard_map.173 = (f32[1,256,4096]{2,1,0:T(8,128)}, f32[1,256,5632]{2,1,0:T(8,128)}, f32[1,704,1024]{2,1,0:T(8,128)}) custom-call(bf16[2,4,256,512]{3,2,1,0:T(8,128)(2,1)S(1)} %copy-done.1, bf16[2,4,256,768]{3,2,1,0:T(8,128)(2,1)S(1)} %copy-done, bf16[2,4,96,1024]{3,2,1,0:T(8,128)(2,1)S(1)} %copy-done.2), custom_call_target="tpu_custom_call" | custom-call | tf_op jit(solution)/shard_map/pallas_call | solution.py:1810
  (42 shorter events, 5.5 us)
Async XLA Ops:
  7.2 191.5 %all-gather.3.cloned.1.call-start = ((), (), s32[]{:S(2)}) async-start(), calls=%async_computation | async-start | bytes 2621440 | tf_op jit(solution)/shard_map/all_gather | solution.py:1869
  13.2 184.7 %copy-start.5 = (bf16[2,1,128,1024]{3,2,1,0:T(8,128)(2,1)S(1)}, bf16[2,1,128,1024]{3,2,1,0:T(8,128)(2,1)}, u32[]{:S(2)}) copy-start(bf16[2,1,128,1024]{3,2,1,0:T(8,128)(2,1)} %param.12) | copy-start | bytes 1572868
  267.4 88.7 %copy-start.11 = (f32[1,512]{1,0:T(1,128)S(1)}, f32[1,512]{1,0:T(1,128)}, u32[]{:S(2)}) copy-start(f32[1,512]{1,0:T(1,128)} %get-tuple-element.118) | copy-start | bytes 6148
  267.4 89.3 %copy-start.10 = (f32[2,1024]{1,0:T(2,128)S(1)}, f32[2,1024]{1,0:T(2,128)}, u32[]{:S(2)}) copy-start(f32[2,1024]{1,0:T(2,128)} %get-tuple-element.120) | copy-start | bytes 24580
  267.4 90.0 %copy-start.9 = (f32[2,16,128]{2,1,0:T(8,128)S(1)}, f32[2,16,128]{2,1,0:T(8,128)}, u32[]{:S(2)}) copy-start(f32[2,16,128]{2,1,0:T(8,128)} %get-tuple-element.116) | copy-start | bytes 49156
  360.2 73.2 %copy-start.4 = (bf16[2,64,1024]{2,1,0:T(8,128)(2,1)S(1)}, bf16[2,64,1024]{2,1,0:T(8,128)(2,1)}, u32[]{:S(2)}) copy-start(bf16[2,64,1024]{2,1,0:T(8,128)(2,1)} %get-tuple-element.89.refs_1_.refs_11_) | copy-start | bytes 786436
  360.2 73.2 %copy-start.7 = (bf16[2,64,1024]{2,1,0:T(8,128)(2,1)S(1)}, bf16[2,64,1024]{2,1,0:T(8,128)(2,1)}, u32[]{:S(2)}) copy-start(bf16[2,64,1024]{2,1,0:T(8,128)(2,1)} %get-tuple-element.110.refs_5_) | copy-start | bytes 786436
  360.3 75.0 %copy-start.3 = (bf16[2,64,1024]{2,1,0:T(8,128)(2,1)S(1)}, bf16[2,64,1024]{2,1,0:T(8,128)(2,1)}, u32[]{:S(2)}) copy-start(bf16[2,64,1024]{2,1,0:T(8,128)(2,1)} %get-tuple-element.70.refs_2_.refs_4_) | copy-start | bytes 786436
  360.3 75.0 %copy-start.6 = (bf16[2,64,1024]{2,1,0:T(8,128)(2,1)S(1)}, bf16[2,64,1024]{2,1,0:T(8,128)(2,1)}, u32[]{:S(2)}) copy-start(bf16[2,64,1024]{2,1,0:T(8,128)(2,1)} %get-tuple-element.71.refs_10_) | copy-start | bytes 786436
  433.4 3.6 copy-start.8
  437.0 9.5 %copy-start = (bf16[2,4,256,768]{3,2,1,0:T(8,128)(2,1)S(1)}, bf16[2,4,256,768]{3,2,1,0:T(8,128)(2,1)}, u32[]{:S(2)}) copy-start(bf16[2,4,256,768]{3,2,1,0:T(8,128)(2,1)} %get-tuple-element.124.gu_buf) | copy-start | bytes 9437188
  446.5 1.6 copy-start.1
  448.1 1.4 copy-start.2
Sparse Core Ops, SparseCore 0:
  9.6 32.3 all-gather.2

commit v6 on v5

--- a/solution.py
+++ b/solution.py
@@ -707,18 +707,6 @@
             self.toward(0, self.root).wait_send()
 
 
-def meet(column=False):
-    place = here()
-    x, s, z = place
-    others = [peer(place, chip, chip == 0) for chip in range(4)]
-    if column:
-        others += [(x, s, (z + dz) % 4) for dz in (1, 2, 3)]
-    barrier = pltpu.get_barrier_semaphore()
-    for other in others:
-        pl.semaphore_signal(barrier, inc=1, device_id=other, device_id_type=MESH)
-    pl.semaphore_wait(barrier, len(others))
-
-
 def nn(left, right):
     return jnp.dot(left, right, preferred_element_type=F32)
 
@@ -768,35 +756,25 @@
     grad_full: Any
     grad_rows: Any
     rows: Any
-    normed: Any
-    gu: Any
-    down: Any
+    out_low: Any
+    out_high: Any
     gains: Any
-    mix: Any
-    out: Any
     persist: Any
     rates: Any
     seg_rows: Any
     seg_cols: Any
-    qkv: Any
-    gate: Any
-    recalled: Any
-    combined: Any
-    mid: Any
-    normed_two: Any
-    gate_up: Any
-    hidden: Any
 
 
 class BackwardOut(NamedTuple):
-    grad_mix: Any
-    grad_out: Any
-    gain_sums: Any
-    grad_persist: Any
-    grad_rate: Any
-    gu_sum: Any
-    down_sum: Any
-    grad_h: Any
+    mix_buf: Any
+    gu_buf: Any
+    down_buf: Any
+    out_buf: Any
+    rows_buf: Any
+    grads_buf: Any
+    plane_buf: Any
+    grad_low: Any
+    grad_high: Any
 
 
 class PlaneScratch(NamedTuple):
@@ -815,35 +793,41 @@
     grad_proj: Any
     grad_keys: Any
     grad_values: Any
+    branch: Any
+    grad_mid: Any
+    grad_next: Any
+    grad_persist: Any
+    grad_rate: Any
+    gain_sums: Any
+    small: Any
+    column_buf: Any
     own_gu: Any
     own_down: Any
-    branch: Any
-    grad_mid: Any
+    grad_mix: Any
+    grad_out: Any
     gu_slots: Any
     down_slots: Any
+    mix_slots: Any
+    root_slots: Any
+    gu_sum: Any
+    down_sum: Any
+    mix_sum: Any
+    out_sum: Any
     csend: Any
     crecv: Any
-
-
-class EarlyIn(NamedTuple):
-    early_mix: Any
-    early_out: Any
-
-
-class EarlyOut(NamedTuple):
-    mix_sum: Any
-    out_sum: Any
-
-
-class EarlyScratch(NamedTuple):
-    mix_slots: Any
-    root_slots: Any
+    hsend: Any
+    hrecv: Any
+    psend: Any
+    precv: Any
+    osend: Any
+    orecv: Any
     rsend: Any
     rrecv: Any
-
-
-class NextOut(NamedTuple):
-    grad_next: Any
+    zsend: Any
+    zrecv: Any
+    qsend: Any
+    qrecv: Any
+    loaded: Any
 
 
 def fields(*kinds):
@@ -1298,28 +1282,58 @@
         remote(r.small, r.small_all.at[x, s], psems, index, plane[index]).wait_send()
 
 
-def backward_layer(layer, ins, outs, *refs):
+def backward_kernel(*refs):
+    saved_names = Kept._fields[:-1]
+    count = len(saved_names)
+    given = vars(named(BackwardIn._fields, refs[: len(BackwardIn._fields)]))
+    refs = refs[len(BackwardIn._fields) :]
+    in_hbm = [refs[:count], refs[count : 2 * count]]
+    refs = refs[2 * count :]
+    given |= vars(named(BackwardOut._fields, refs[: len(BackwardOut._fields)]))
+    refs = refs[len(BackwardOut._fields) :]
+    in_vmem = refs[:count]
+    given |= vars(named(saved_names, in_vmem))
     scratch = fields(PlaneScratch, BackwardScratch)
-    earlier = len(outs) == len(fields(BackwardOut, EarlyOut))
-    if earlier:
-        scratch += fields(EarlyScratch)
-    r = named(ins + outs + scratch, refs)
+    r = types.SimpleNamespace(**given, **vars(named(scratch, refs[count:])))
     length = r.part.shape[1]
-    last = not hasattr(r, "grad_next")
-    sums = [
-        ColumnSum(r.own_gu, r.gu_slots, r.gu_sum, r.csend.at[0], r.crecv.at[0]),
-        ColumnSum(r.own_down, r.down_slots, r.down_sum, r.csend.at[1], r.crecv.at[1]),
-    ]
-    early = []
-    if earlier:
-        early = [
-            ColumnSum(r.early_mix, r.mix_slots, r.mix_sum, r.csend.at[2], r.crecv.at[2]),
-            RootSum(r.early_out, r.root_slots, r.out_sum, r.rsend, r.rrecv),
-        ]
-
-    def feed_back(batch):
+    place = here()
+    x, s, z = place
+
+    def load(layer, which):
+        for name in which:
+            index = saved_names.index(name)
+            yield pltpu.make_async_copy(in_hbm[layer][index], in_vmem[index], r.loaded.at[index])
+
+    feed_names = saved_names[3:5] + saved_names[9:]
+    mixer_names = saved_names[:3] + saved_names[5:9]
+    for which in (feed_names, mixer_names):
+        each(load(1, which), lambda copy: copy.start())
+    feeds, mixers = [], []
+    for layer in range(2):
+        sems = [(r.csend.at[3 * layer + i], r.crecv.at[3 * layer + i]) for i in range(3)]
+        feeds.append(
+            [
+                ColumnSum(r.own_gu, r.gu_slots.at[layer], r.gu_sum.at[layer], *sems[0]),
+                ColumnSum(r.own_down, r.down_slots.at[layer], r.down_sum.at[layer], *sems[1]),
+            ]
+        )
+        mixers.append(
+            [
+                ColumnSum(r.grad_mix, r.mix_slots.at[layer], r.mix_sum.at[layer], *sems[2]),
+                RootSum(
+                    r.grad_out,
+                    r.root_slots.at[layer],
+                    r.out_sum.at[layer],
+                    r.hsend.at[layer],
+                    r.hrecv.at[layer],
+                ),
+            ]
+        )
+    grads = (r.grad_low, r.grad_high)
+
+    def feed_back(full, batch):
         def block(rows, begin):
-            grad_hidden = nt(r.grad_full[batch, rows, :], flat(r.down))
+            grad_hidden = nt(full[batch, rows, :], flat(r.down))
             half = grad_hidden.shape[1]
             gate_part = r.gate_up[batch, rows, :half]
             up_part = r.gate_up[batch, rows, half:]
@@ -1332,10 +1346,10 @@
 
         in_blocks(length, 256, block)
 
-    def feed_weights():
+    def feed_weights(full):
         def down(cols, begin):
-            grad = tn(r.hidden[0], r.grad_full[0, :, cols])
-            grad = grad + tn(r.hidden[1], r.grad_full[1, :, cols])
+            grad = tn(r.hidden[0], full[0, :, cols])
+            grad = grad + tn(r.hidden[1], full[1, :, cols])
             grad = grad.reshape(4, grad.shape[0] // 4, grad.shape[1])
             r.own_down[:, :, cols] = grad.astype(BF)
 
@@ -1348,7 +1362,7 @@
             grad = tn(left[0, :, cols], right[0]) + tn(left[1, :, cols], right[1])
             out[owner] = grad.astype(BF)
 
-    def mixer_back(batch):
+    def mixer_back(layer, batch):
         scale = 1.0 / math.sqrt(HD)
         r.grad_keys[...] = jnp.zeros_like(r.grad_keys)
         r.grad_values[...] = jnp.zeros_like(r.grad_values)
@@ -1384,7 +1398,7 @@
             grad_inner = weighted.astype(BF)
             memory = inner * decay_w
             rate_terms = weighted * inner * distance
-            r.grad_rate[...] -= jnp.sum(rate_terms, axis=0, keepdims=True)
+            r.grad_rate[layer] -= jnp.sum(rate_terms, axis=0, keepdims=True)
             grad_query = (nn(per_ds, r.persist[layer, 0]) + nn(seq_ds, keys)) * scale
             grad_query = grad_query + nn(grad_inner, keys)
             r.grad_proj[batch, rows, :HD] = grad_query.astype(BF)
@@ -1392,8 +1406,8 @@
             r.grad_values[...] += tn(probs.astype(BF), attn_rows) + tn(
                 memory.astype(BF), memory_rows
             )
-            r.grad_persist[0] += tn(per_ds, query) * scale
-            r.grad_persist[1] += tn(per_probs.astype(BF), attn_rows)
+            r.grad_persist[layer, 0] += tn(per_ds, query) * scale
+            r.grad_persist[layer, 1] += tn(per_probs.astype(BF), attn_rows)
 
         in_blocks(length, 128, block)
         r.grad_proj[batch, :, HD : 2 * HD] = r.grad_keys[...].astype(BF)
@@ -1411,95 +1425,6 @@
         grad_normed = part.finish()
         inverse = rms_scale(rows)
         return norm_back(grad_normed, rows * inverse, inverse, gain)
-
-    meet(True)
-    r.grad_rate[...] = jnp.zeros_like(r.grad_rate)
-    r.grad_persist[...] = jnp.zeros_like(r.grad_persist)
-    for column in early:
-        column.start()
-    first, second = (scatter(batch) for batch in range(2))
-    for batch, part in enumerate((first, second)):
-        feed_back(batch)
-        part.start()
-        part.forward()
-    for column in early:
-        column.hop()
-    feed_weights()
-    for column in sums:
-        column.start()
-    gathers = []
-    gain_sums = []
-    for batch, part in enumerate((first, second)):
-        grad_mid, gain_sum = through_norm(batch, part, r.mid[batch], r.gains[layer, 1:2, :])
-        gain_sums.append(gain_sum[None])
-        grad_mid = grad_mid + r.grad_rows[batch].astype(F32)
-        r.grad_mid[batch] = grad_mid
-        gather = Gather(r.branch, batch, r.gsend, r.grecv)
-        gather.start(grad_mid.astype(BF))
-        gathers.append(gather)
-    r.gain_sums[1:2] = gain_sums[0] + gain_sums[1]
-    first, second = (scatter(batch) for batch in range(2))
-    for batch, part in enumerate((first, second)):
-        gathers[batch].forward()
-        gathers[batch].finish()
-        mixer_back(batch)
-        part.start()
-        part.forward()
-        if batch == 0:
-            for column in sums:
-                column.hop()
-    product(r.grad_mix, r.normed, r.grad_proj)
-    grad_out = tn(r.combined[0], r.branch[0]) + tn(r.combined[1], r.branch[1])
-    r.grad_out[...] = grad_out.astype(BF)
-    gathers = []
-    gain_sums = []
-    for batch, part in enumerate((first, second)):
-        grad_h, gain_sum = through_norm(
-            batch, part, r.rows[batch].astype(F32), r.gains[layer, 0:1, :]
-        )
-        gain_sums.append(gain_sum[None])
-        grad_h = (grad_h + r.grad_mid[batch]).astype(BF)
-        r.grad_h[batch] = grad_h
-        if not last:
-            gather = Gather(r.grad_next, batch, r.gsend, r.grecv)
-            gather.start(grad_h)
-            gathers.append(gather)
-    r.gain_sums[0:1] = gain_sums[0] + gain_sums[1]
-    for gather in gathers:
-        gather.forward()
-    for gather in gathers:
-        gather.finish()
-    for column in early + sums:
-        column.finish()
-
-
-def final_kernel(*refs):
-    place = here()
-    x, s, z = place
-    sibling, beside, partner = (peer(place, 0, True), peer(place, 2, False), peer(place, 1, False))
-    across = peer(place, 3, False)
-    by_layer = [list(refs[0:6]), list(refs[6:12])]
-    small_ref = refs[12]
-    bufs = refs[13:16]
-    out_buf, rows_buf, grads_buf, plane_buf = refs[16:20]
-    column_buf, mix_sum, out_sum, mix_slots, root_slots, *sems = refs[20:]
-    psend, precv, osend, orecv, rsend, rrecv, zsend, zrecv, ssend, srecv, *sems = sems
-    csend, crecv, hsend, hrecv = sems
-    columns = [
-        ColumnSum(by_layer[0][0], mix_slots, mix_sum, csend, crecv),
-        RootSum(by_layer[0][3], root_slots, out_sum, hsend, hrecv),
-    ]
-    by_layer[0][0], by_layer[0][3] = mix_sum, out_sum
-
-    def copy(source, landing, sems, index, target):
-        return pltpu.make_async_remote_copy(
-            src_ref=source,
-            dst_ref=landing,
-            send_sem=sems[0].at[index],
-            recv_sem=sems[1].at[index],
-            device_id=target,
-            device_id_type=MESH,
-        )
 
     flips = [(dx, ds) for dx in (0, 1) for ds in range(4) if dx or ds]
     plane = [((x + dx) % 2, (s + ds) % 4, z) for dx, ds in flips]
@@ -1508,21 +1433,122 @@
     for other in plane + column:
         pl.semaphore_signal(barrier, inc=1, device_id=other, device_id_type=MESH)
     pl.semaphore_wait(barrier, len(plane) + len(column))
+    r.grad_rate[...] = jnp.zeros_like(r.grad_rate)
+    r.grad_persist[...] = jnp.zeros_like(r.grad_persist)
+    arriving = None
+    for layer in (1, 0):
+        full = r.grad_next if arriving else r.grad_full
+        above = grads[1] if arriving else r.grad_rows
+        rows_in = r.out_low if layer else r.rows
+        each(load(layer, feed_names), lambda copy: copy.wait())
+        parts = []
+        for batch in range(2):
+            if arriving:
+                arriving[batch].forward()
+                arriving[batch].finish()
+            feed_back(full, batch)
+            part = scatter(batch)
+            part.start()
+            part.forward()
+            parts.append(part)
+        if layer == 0:
+            each(mixers[1], lambda part: part.hop())
+            each(feeds[1], lambda part: part.finish())
+        feed_weights(full)
+        each(feeds[layer], lambda part: part.start())
+        gathers = []
+        gain_sums = []
+        for batch, part in enumerate(parts):
+            grad_mid, gain_sum = through_norm(
+                batch, part, r.mid[batch], r.gains[layer, 1:2, :]
+            )
+            gain_sums.append(gain_sum[None])
+            grad_mid = grad_mid + above[batch].astype(F32)
+            r.grad_mid[batch] = grad_mid
+            gather = Gather(r.branch, batch, r.gsend, r.grecv)
+            gather.start(grad_mid.astype(BF))
+            gathers.append(gather)
+        r.gain_sums[layer, 1:2] = gain_sums[0] + gain_sums[1]
+        if layer == 1:
+            each(load(0, feed_names), lambda copy: copy.start())
+        each(load(layer, mixer_names), lambda copy: copy.wait())
+        parts = []
+        for batch, gather in enumerate(gathers):
+            gather.forward()
+            gather.finish()
+            mixer_back(layer, batch)
+            part = scatter(batch)
+            part.start()
+            part.forward()
+            parts.append(part)
+            if batch == 0:
+                each(feeds[layer], lambda part: part.hop())
+        if layer == 0:
+            each(mixers[1], lambda part: part.finish())
+        product(r.grad_mix, r.normed, r.grad_proj)
+        grad_out = tn(r.combined[0], r.branch[0]) + tn(r.combined[1], r.branch[1])
+        r.grad_out[...] = grad_out.astype(BF)
+        each(mixers[layer], lambda part: part.start())
+        if layer == 1:
+            each(load(0, mixer_names), lambda copy: copy.start())
+        arriving = []
+        gain_sums = []
+        for batch, part in enumerate(parts):
+            grad_h, gain_sum = through_norm(
+                batch, part, rows_in[batch].astype(F32), r.gains[layer, 0:1, :]
+            )
+            gain_sums.append(gain_sum[None])
+            grad_h = (grad_h + r.grad_mid[batch]).astype(BF)
+            grads[layer][batch] = grad_h
+            if layer == 1:
+                gather = Gather(r.grad_next, batch, r.gsend, r.grecv)
+                gather.start(grad_h)
+                arriving.append(gather)
+        r.gain_sums[layer, 0:1] = gain_sums[0] + gain_sums[1]
+    each(feeds[0], lambda part: part.finish())
+
+    for layer in range(2):
+        persist = r.grad_persist[layer].reshape(-1, HD)
+        rate = r.grad_rate[layer]
+        rate = sum(rate[:, begin : begin + HD] for begin in range(0, length, HD))
+        for owner in range(4):
+            r.small[owner, layer * 32 : (layer + 1) * 32, :] = persist
+            r.small[owner, 64 + layer : 65 + layer, :] = rate
+            for kind in range(2):
+                for half in range(2):
+                    row = 72 + 4 * layer + 2 * kind + half
+                    begin = owner * 2 * HD + half * HD
+                    r.small[owner, row : row + 1, :] = r.gain_sums[
+                        layer, kind : kind + 1, begin : begin + HD
+                    ]
+    for owner in range(4):
+        r.small[owner, 66:72, :] = jnp.zeros((6, HD), F32)
+
+    sibling, beside, partner = (peer(place, 0, True), peer(place, 2, False), peer(place, 1, False))
+    across = peer(place, 3, False)
+    bufs = (r.mix_buf, r.gu_buf, r.down_buf)
+    out_buf, rows_buf, grads_buf, plane_buf = r.out_buf, r.rows_buf, r.grads_buf, r.plane_buf
+    by_layer = [
+        [r.mix_sum.at[i], r.gu_sum.at[i], r.down_sum.at[i], r.out_sum.at[i]] for i in range(2)
+    ]
+    by_layer[0] += [r.out_low, r.grad_low]
+    by_layer[1] += [r.out_high, r.grad_high]
+    copy = remote
 
     def to_plane_of(dz):
         target = (z + dz) % 4
         return copy(
-            small_ref.at[target], column_buf.at[dz - 1], (zsend, zrecv), dz - 1, (x, s, target)
+            r.small.at[target], r.column_buf.at[dz - 1], (r.zsend, r.zrecv), dz - 1, (x, s, target)
         )
 
     def to_plane(index):
         slot = plane_buf.at[x * 4 + s]
-        return copy(slot, slot, (ssend, srecv), index, plane[index])
+        return copy(slot, slot, (r.qsend, r.qrecv), index, plane[index])
 
     for dz in (1, 2, 3):
         to_plane_of(dz).start()
 
-    psems = [(psend.at[i], precv.at[i]) for i in range(3)]
+    psems = [(r.psend.at[i], r.precv.at[i]) for i in range(3)]
 
     def piece(index, kind, slot, target, source=None):
         landing = bufs[index].at[slot]
@@ -1550,28 +1576,24 @@
             piece(index, 3, turned, beside).start()
             piece(index, 4, turned, sibling).start()
 
-    for column in columns:
-        column.start()
     send((1, 2))
     for layer in (0, 1):
 
         @pl.when(x == layer)
         def _():
-            copy(by_layer[1 - layer][4], rows_buf, (rsend, rrecv), 0, partner).start()
-            copy(by_layer[1 - layer][5], grads_buf, (rsend, rrecv), 1, partner).start()
-
-    total = small_ref[z]
+            copy(by_layer[1 - layer][4], rows_buf, (r.rsend, r.rrecv), 0, partner).start()
+            copy(by_layer[1 - layer][5], grads_buf, (r.rsend, r.rrecv), 1, partner).start()
+
+    total = r.small[z]
     for dz in (1, 2, 3):
         to_plane_of(dz).wait_recv()
-        total = total + column_buf[dz - 1]
+        total = total + r.column_buf[dz - 1]
     plane_buf[x * 4 + s] = total
     for index in range(7):
         to_plane(index).start()
-    for column in columns:
-        column.hop()
+    each(mixers[0], lambda part: part.hop())
     turn((1, 2))
-    for column in columns:
-        column.finish()
+    each(mixers[0], lambda part: part.finish())
     send((0,))
 
     core = s % 2
@@ -1581,7 +1603,7 @@
 
     def out_copy(index, target, source=None):
         landing = out_buf.at[core]
-        return copy(landing if source is None else source, landing, (osend, orecv), index, target)
+        return copy(landing if source is None else source, landing, (r.osend, r.orecv), index, target)
 
     for layer in (0, 1):
 
@@ -1617,13 +1639,13 @@
         piece(index, 5, (x, far_twin), sibling).wait_recv()
         piece(index, 6, (1 - x, far_twin), sibling).wait_recv()
     other_out = out_buf.at[1 - core]
-    copy(other_out, other_out, (osend, orecv), 0, sibling).wait_recv()
+    copy(other_out, other_out, (r.osend, r.orecv), 0, sibling).wait_recv()
     for index in range(7):
         dx, ds = flips[index]
         slot = plane_buf.at[((x + dx) % 2) * 4 + (s + 4 - ds) % 4]
-        copy(slot, slot, (ssend, srecv), index, plane[index]).wait_recv()
+        copy(slot, slot, (r.qsend, r.qrecv), index, plane[index]).wait_recv()
     for index in (0, 1):
-        copy(rows_buf, rows_buf, (rsend, rrecv), index, partner).wait()
+        copy(rows_buf, rows_buf, (r.rsend, r.rrecv), index, partner).wait()
     for index in range(7):
         to_plane(index).wait_send()
     for dz in (1, 2, 3):
@@ -1639,13 +1661,13 @@
             out_copy(index, sibling).wait_send()
 
 
-def kernel_call(kernel, number, operands, outs, scratch, spaces=None):
-    vmem = pl.BlockSpec(memory_space=pltpu.VMEM)
+def kernel_call(kernel, number, operands, outs, scratch, spaces=None, places=None):
     spaces = spaces or [pltpu.VMEM] * len(outs)
+    places = places or [pltpu.VMEM] * len(operands)
     return pl.pallas_call(
         kernel,
-        out_shape=outs,
-        in_specs=[vmem] * len(operands),
+        out_shape=list(outs),
+        in_specs=[pl.BlockSpec(memory_space=space) for space in places],
         out_specs=[pl.BlockSpec(memory_space=space) for space in spaces],
         scratch_shapes=scratch,
         compiler_params=pltpu.CompilerParams(
@@ -1720,68 +1742,56 @@
     )
 
 
-def backward_call(number, layer, given):
-    count, length, _ = given.normed.shape
-    half = 4 * given.down.shape[1]
-    last = layer == 0
-    depth = D // 4
+def backward_call(number, given, below, above):
+    saved = Kept._fields[:-1]
+    kept = [getattr(part, name) for part in (below, above) for name in saved]
+    count, length, _ = below.normed.shape
+    depth, half, size = D // 4, 4 * below.down.shape[1], length // 8
     shape = jax.ShapeDtypeStruct
-    outs = dict(
-        grad_mix=shape((4, depth, 4 * HD), BF),
-        grad_out=shape((HD, D), BF),
-        gain_sums=shape((2, D), F32),
-        grad_persist=shape(given.persist.shape[1:], F32),
-        grad_rate=shape((1, length), F32),
-        gu_sum=shape((depth, 2 * half), BF),
-        down_sum=shape((half // 4, D), BF),
-        grad_h=shape((count, length // 8, D), BF),
-    )
-    ins = BackwardIn._fields
-    if last:
-        ins += EarlyIn._fields
-        outs |= dict(mix_sum=shape((depth, 4 * HD), BF), out_sum=shape((HD, D), BF))
-    else:
-        outs |= dict(grad_next=shape((count, length, D), BF))
-    scratch = scatter_scratch(length) + [
+    outs = BackwardOut(
+        mix_buf=shape((2, 4, depth, 4 * HD), BF),
+        gu_buf=shape((2, 4, depth, 2 * half), BF),
+        down_buf=shape((2, 4, half // 4, D), BF),
+        out_buf=shape((2, HD, D), BF),
+        rows_buf=shape((count, size, D), BF),
+        grads_buf=shape((count, size, D), BF),
+        plane_buf=shape((8, 80, HD), F32),
+        grad_low=shape((count, size, D), BF),
+        grad_high=shape((count, size, D), BF),
+    )
+    scratch = [pltpu.VMEM(part.shape, part.dtype) for part in kept[: len(saved)]]
+    scratch += scatter_scratch(length) + [
         pltpu.VMEM((count, length, 2 * half), BF),
         pltpu.VMEM((count, length, 4 * HD), BF),
         pltpu.VMEM((length, HD), F32),
         pltpu.VMEM((length, HD), F32),
+        pltpu.VMEM((count, length, D), BF),
+        pltpu.VMEM((count, size, D), F32),
+        pltpu.VMEM((count, length, D), BF),
+        pltpu.VMEM((2, 2, 16, HD), F32),
+        pltpu.VMEM((2, 1, length), F32),
+        pltpu.VMEM((2, 2, D), F32),
+        pltpu.VMEM((4, 80, HD), F32),
+        pltpu.VMEM((3, 80, HD), F32),
         pltpu.VMEM((4, depth, 2 * half), BF),
         pltpu.VMEM((4, half // 4, D), BF),
-        pltpu.VMEM((count, length, D), BF),
-        pltpu.VMEM((count, length // 8, D), F32),
-        pltpu.VMEM((4, depth, 2 * half), BF),
-        pltpu.VMEM((4, half // 4, D), BF),
-        *pairs_of((3, 4)),
+        pltpu.VMEM((4, depth, 4 * HD), BF),
+        pltpu.VMEM((HD, D), BF),
+        pltpu.VMEM((2, 4, depth, 2 * half), BF),
+        pltpu.VMEM((2, 4, half // 4, D), BF),
+        pltpu.VMEM((2, 4, depth, 4 * HD), BF),
+        pltpu.VMEM((2, 2, HD, D), BF),
+        pltpu.VMEM((2, depth, 2 * half), BF),
+        pltpu.VMEM((2, half // 4, D), BF),
+        pltpu.VMEM((2, depth, 4 * HD), BF),
+        pltpu.VMEM((2, HD, D), BF),
+        *pairs_of((6, 4), (2, 2), (3, 7), (4,), (2,), (3,), (7,)),
+        pltpu.SemaphoreType.DMA((len(saved),)),
     ]
-    if last:
-        scratch += [
-            pltpu.VMEM((4, depth, 4 * HD), BF),
-            pltpu.VMEM((2, HD, D), BF),
-            *pairs_of((2,)),
-        ]
-    kernel = functools.partial(backward_layer, layer, ins, tuple(outs))
-    operands = [getattr(given, name) for name in ins]
-    return named(outs, kernel_call(kernel, number, operands, list(outs.values()), scratch))
-
-
-def final_call(number, by_layer, small):
-    operands = (*by_layer[0], *by_layer[1], small)
-    mix, gu, down, out, *rows = by_layer[1]
-    outs = [jax.ShapeDtypeStruct((2, 4) + part.shape, BF) for part in (mix, gu, down)]
-    outs.append(jax.ShapeDtypeStruct((2,) + out.shape, BF))
-    outs += [jax.ShapeDtypeStruct(part.shape, BF) for part in rows]
-    outs.append(jax.ShapeDtypeStruct((8,) + small.shape[1:], F32))
-    scratch = [
-        pltpu.VMEM((3,) + small.shape[1:], F32),
-        pltpu.VMEM(mix.shape, BF),
-        pltpu.VMEM(out.shape, BF),
-        pltpu.VMEM((4,) + mix.shape, BF),
-        pltpu.VMEM((2,) + out.shape, BF),
-        *pairs_of((3, 7), (4,), (2,), (3,), (7,), (4,), (2,)),
-    ]
-    return kernel_call(final_kernel, number, operands, outs, scratch)
+    operands = [*(getattr(given, name) for name in BackwardIn._fields), *kept]
+    spaces = [pltpu.VMEM] * len(BackwardIn._fields) + [pl.ANY] * len(kept)
+    found = kernel_call(backward_kernel, number, operands, outs, scratch, None, spaces)
+    return named(BackwardOut._fields, found)
 
 
 def assemble_kernel(unit, mix_buf, gu_buf, down_buf, mix_ref, gu_ref, down_ref):
@@ -1856,65 +1866,40 @@
     ready, below, above = forward_call(
         1, inputs, small, gain_rows, w_mix, w_out, w_gu, w_down, *segments
     )
-    shared = dict(
+    cot_full = lax.all_gather(cotangent[:, 0], "seq", axis=1, tiled=True)
+    given = BackwardIn(
+        grad_full=cot_full,
+        grad_rows=lax.dynamic_slice_in_dim(cotangent[:, 0], x * size, size, 1),
+        rows=ready.rows,
+        out_low=below.out_rows,
+        out_high=above.out_rows,
         gains=ready.gains,
         persist=ready.persist,
         rates=ready.rates,
         seg_rows=segments[0],
         seg_cols=segments[1],
     )
-    lower = dict(shared, rows=ready.rows)
-    upper = dict(shared, rows=below.out_rows)
-    outputs = [below.out_rows, above.out_rows]
-    cot_full = lax.all_gather(cotangent[:, 0], "seq", axis=1, tiled=True)
-    cot_rows = lax.dynamic_slice_in_dim(cotangent[:, 0], x * size, size, 1)
-    upper |= dict(vars(above), grad_full=cot_full, grad_rows=cot_rows)
-    later = backward_call(3, 1, types.SimpleNamespace(**upper))
-    lower |= dict(
-        vars(below),
-        grad_full=later.grad_next,
-        grad_rows=later.grad_h,
-        early_mix=later.grad_mix,
-        early_out=later.grad_out,
-    )
-    earlier = backward_call(4, 0, types.SimpleNamespace(**lower))
-    by_layer = [
-        (earlier.grad_mix, earlier.gu_sum, earlier.down_sum, earlier.grad_out),
-        (earlier.mix_sum, later.gu_sum, later.down_sum, earlier.out_sum),
-    ]
-    both = (earlier, later)
-    grads = [found.grad_h for found in both]
-    gain_sums = [found.gain_sums for found in both]
-
-    memory_all = jnp.stack([found.grad_persist for found in both], 0).reshape(-1, HD)
-    rate_all = jnp.stack([jnp.sum(found.grad_rate) for found in both])
-    rate_all = jnp.pad(rate_all[None], ((0, 7), (0, HD - 2)))
-    gain_all = jnp.stack(gain_sums, 0).reshape(4, nz, 2, HD).transpose(1, 0, 2, 3)
-    memory_all = jnp.concatenate([memory_all, rate_all], 0)
-    small = jnp.concatenate(
-        [jnp.broadcast_to(memory_all[None], (nz,) + memory_all.shape), gain_all.reshape(nz, 8, HD)],
-        1,
-    )
-    by_layer = [(*by_layer[layer], outputs[layer], grads[layer]) for layer in range(2)]
-    mix_all, gu_all, down_all, out_all, rows_got, grads_got, plane_all = final_call(
-        5, by_layer, small
-    )
+    found = backward_call(2, given, below, above)
+    outputs = (below.out_rows, above.out_rows)
+    grads = (found.grad_low, found.grad_high)
 
     def whole_rows(of_layer, got):
         both = layers(jnp.where(first, of_layer[0], of_layer[1]), got)
         return jnp.concatenate(both, 1)[None, :, None]
 
-    section_out = whole_rows(outputs, rows_got)
-    section_grad = whole_rows(grads, grads_got).astype(F32)
-    grad_mix, grad_gu, grad_down = assemble_call(unit, mix_all, gu_all, down_all)
-    grad_out = out_all.astype(F32).reshape(1, 2 * HD, D)
-
+    section_out = whole_rows(outputs, found.rows_buf)
+    section_grad = whole_rows(grads, found.grads_buf).astype(F32)
+    grad_mix, grad_gu, grad_down = assemble_call(unit, found.mix_buf, found.gu_buf, found.down_buf)
+    grad_out = found.out_buf.astype(F32).reshape(1, 2 * HD, D)
+
+    plane_all = found.plane_buf
     heads_of = lax.dynamic_slice_in_dim(plane_all, 2 * s, 2, 0)
     of_section = lax.dynamic_index_in_dim(
         heads_of[:, :64].reshape(2, 2, 2, -1, HD), x, 1, keepdims=False
     )
     grad_persist = of_section.transpose(1, 2, 0, 3).reshape(1, 2, -1, 2 * HD)
-    grad_rate = lax.dynamic_index_in_dim(heads_of[:, 64], x, 1, keepdims=False)[None]
+    of_section = lax.dynamic_index_in_dim(heads_of[:, 64:66], x, 1, keepdims=False)
+    grad_rate = jnp.sum(of_section, 1)[None]
     gain_all = jnp.sum(plane_all[:, 72:], 0).reshape(2, 2, depth)
     grad_gain = lax.dynamic_index_in_dim(gain_all, x, 0).transpose(0, 2, 1)
     return (

time: 468 us -> 422 us (0.902)
  Pallas kernels: 420 us -> 386 us
  other arithmetic: 16.9 us -> 10.6 us
    pallas_call x4 -> x2, Pallas kernels: 414 us -> 380 us  [kernel_call(): pl.pallas_call(kernel, out_shape=list(outs), in_specs=[pl.BlockSpec(memor...]
  transfers between devices with their start and end apart: 1 -> 1, of which waited for: 0 -> 0; matrix products, arithmetic and copies ran while one was open for 1% -> 1% of each run, Pallas kernels for 40% -> 44%
where the time goes in v6:
time: 422 us; the launch traced here: 418 us
  Pallas kernels  386 us (91%)
  between operations  14.3 us (3%)
  other arithmetic  10.6 us (3%)
  local copies, waits for them, and re-layouts  6.18 us (1%)
    pallas_call x2, Pallas kernels, kernel_call(): pl.pallas_call(kernel, out_shape=list(outs), in_specs=[pl.BlockSpec(memor...  380 us
  transfers between devices with their start and end apart: 1, of which 0 were waited for; matrix products, arithmetic and copies ran while one was open for 1% of the time, Pallas kernels for 44%

profile of v6, /device:TPU:3, one launch (start us, length us, event | category | flops | bytes accessed | tf_op | source)
XLA Modules:
  0.0 417.9 jit_solution(1429286071663722974)
XLA Ops:
  7.2 0.7 all-gather.3.cloned.1.call-update
  7.9 0.7 reduce.1
  8.6 1.0 broadcast_in_dim_squeeze.5.refs_7_.refs_8_
  9.6 0.7 reshape.87
  10.4 0.7 broadcast_in_dim.19
  11.1 0.1 reshape.90
  11.2 0.7 reshape.78
  11.9 0.1 pad.13.clone
  12.0 0.6 pad_convert_fusion.refs_2_
  12.5 0.7 pad_maximum_fusion.refs_1_
  13.2 184.7 %shard_map.169 = (bf16[2,64,1024]{2,1,0:T(8,128)(2,1)}, f32[2,2,1024]{2,1,0:T(2,128)}, bf16[2,2,16,128]{3,2,1,0:T(8,128)(2,1)}, f32[2,8,128]{2,1,0:T(8,128)}, bf...) custom-call(bf16[2,1,128,1024]{3,2,1,0:T(8,128)(2,1)} %refs_0_.1, ...), custom_call_target="tpu_custom_call" | custom-call | tf_op jit(solution)/shard_map/pallas_call | solution.py:1667
  198.0 0.7 dynamic-slice_bitcast_fusion.refs_1_
  198.7 195.7 %shard_map.170 = (bf16[2,4,256,512]{3,2,1,0:T(8,128)(2,1)}, bf16[2,4,256,768]{3,2,1,0:T(8,128)(2,1)}, bf16[2,4,96,1024]{3,2,1,0:T(8,128)(2,1)}, bf16[2,128,1024]...) custom-call(bf16[2,512,1024]{2,1,0:T(8,128)(2,1)} %bitcast.40, ...), custom_call_target="tpu_custom_call" | custom-call | tf_op jit(solution)/shard_map/pallas_call | solution.py:1667
  394.4 2.3 bitcast_convert_fusion
  396.7 0.8 slice_reduce_fusion
  397.5 0.8 constant_dynamic-slice_fusion
  398.4 0.6 reshape.83
  399.0 1.3 fusion.1
  400.3 0.6 dynamic-slice_bitcast_fusion.2
  400.9 1.1 broadcast_select_fusion.2
  402.1 1.2 select_bitcast_fusion.1
  403.3 1.1 fusion
  404.4 0.8 maximum_bitcast_fusion
  405.2 5.6 %shard_map.171 = (f32[1,256,4096]{2,1,0:T(8,128)}, f32[1,256,5632]{2,1,0:T(8,128)}, f32[1,704,1024]{2,1,0:T(8,128)}) custom-call(bf16[2,4,256,512]{3,2,1,0:T(8,128)(2,1)S(1)} %copy-done.1, bf16[2,4,256,768]{3,2,1,0:T(8,128)(2,1)S(1)} %copy-done, bf16[2,4,96,1024]{3,2,1,0:T(8,128)(2,1)S(1)} %copy-done.2), custom_call_target="tpu_custom_call" | custom-call | tf_op jit(solution)/shard_map/pallas_call | solution.py:1820
  (18 shorter events, 0.1 us)
Async XLA Ops:
  7.2 191.6 %all-gather.3.cloned.1.call-start = ((), (), s32[]{:S(2)}) async-start(), calls=%async_computation | async-start | bytes 2621440 | tf_op jit(solution)/shard_map/all_gather | solution.py:1869
  13.2 184.8 %copy-start.3 = (bf16[2,1,128,1024]{3,2,1,0:T(8,128)(2,1)S(1)}, bf16[2,1,128,1024]{3,2,1,0:T(8,128)(2,1)}, u32[]{:S(2)}) copy-start(bf16[2,1,128,1024]{3,2,1,0:T(8,128)(2,1)} %param.12) | copy-start | bytes 1572868
  198.7 202.2 %copy-start.5 = (bf16[2,64,1024]{2,1,0:T(8,128)(2,1)S(1)}, bf16[2,64,1024]{2,1,0:T(8,128)(2,1)}, u32[]{:S(2)}) copy-start(bf16[2,64,1024]{2,1,0:T(8,128)(2,1)} %get-tuple-element.54.refs_4_) | copy-start | bytes 786436
  394.4 6.5 %copy-start.4 = (bf16[2,64,1024]{2,1,0:T(8,128)(2,1)S(1)}, bf16[2,64,1024]{2,1,0:T(8,128)(2,1)}, u32[]{:S(2)}) copy-start(bf16[2,64,1024]{2,1,0:T(8,128)(2,1)} %get-tuple-element.53.refs_3_) | copy-start | bytes 786436
  394.4 10.8 %copy-start.2 = (bf16[2,4,96,1024]{3,2,1,0:T(8,128)(2,1)S(1)}, bf16[2,4,96,1024]{3,2,1,0:T(8,128)(2,1)}, u32[]{:S(2)}) copy-start(bf16[2,4,96,1024]{3,2,1,0:T(8,128)(2,1)} %get-tuple-element.91.down_buf) | copy-start | bytes 4718596
  400.9 4.3 %copy-start.1 = (bf16[2,4,256,512]{3,2,1,0:T(8,128)(2,1)S(1)}, bf16[2,4,256,512]{3,2,1,0:T(8,128)(2,1)}, u32[]{:S(2)}) copy-start(bf16[2,4,256,512]{3,2,1,0:T(8,128)(2,1)} %get-tuple-element.89.mix_buf) | copy-start | bytes 6291460
  402.1 3.2 copy-start
Sparse Core Ops, SparseCore 0:
  9.6 32.3 all-gather.2

commit v7 on v6

--- a/solution.py
+++ b/solution.py
@@ -1110,8 +1110,6 @@
         def _():
             remote(r.gu_away, v.gu.at[z], xsems, 2, partner).start()
             remote(r.down_away, v.down.at[z], xsems, 3, partner).start()
-            gu_part(mine, v.gu.at[z])
-            down_part(mine, v.down.at[z])
 
     mixers, feeds = [], []
     for layer, v in enumerate(views):
@@ -1144,9 +1142,16 @@
             part.start()
 
     start_mixer(0)
+    for layer, v in enumerate(views):
+
+        @pl.when(x == layer)
+        def _():
+            gu_part(mine, v.gu.at[z])
+            down_part(mine, v.down.at[z])
+
+    start_feed(0)
     arriving[0].forward()
     each(mixers[0], lambda part: part.hop())
-    start_feed(0)
     arriving[1].forward()
 
     for index in range(7):
@@ -1234,14 +1239,14 @@
             part.forward()
             parts.append(part)
         each(save(layer, mixer_names), lambda copy: copy.start())
+        if layer == 0:
+            start_mixer(1)
         gathers = []
         for batch, part in enumerate(parts):
             mid = v.rows[batch].astype(F32) + part.finish()
             v.mid[batch] = mid
             gathers.append(send_normed(batch, mid, r.gains[layer, 1:2, :], v.normed_two))
         each(feeds[layer], lambda part: part.hop())
-        if layer == 0:
-            start_mixer(1)
         parts = []
         for batch, gather in enumerate(gathers):
             gather.forward()
@@ -1346,7 +1351,7 @@
 
         in_blocks(length, 256, block)
 
-    def feed_weights(full):
+    def down_weights(full):
         def down(cols, begin):
             grad = tn(r.hidden[0], full[0, :, cols])
             grad = grad + tn(r.hidden[1], full[1, :, cols])
@@ -1354,7 +1359,6 @@
             r.own_down[:, :, cols] = grad.astype(BF)
 
         in_blocks(D, 256, down)
-        product(r.own_gu, r.normed_two, r.grad_gu)
 
     def product(out, left, right):
         for owner in range(4):
@@ -1446,6 +1450,11 @@
             if arriving:
                 arriving[batch].forward()
                 arriving[batch].finish()
+            if batch == 1 - layer:
+                if layer == 0:
+                    feeds[1][1].finish()
+                down_weights(full)
+                feeds[layer][1].start()
             feed_back(full, batch)
             part = scatter(batch)
             part.start()
@@ -1453,9 +1462,11 @@
             parts.append(part)
         if layer == 0:
             each(mixers[1], lambda part: part.hop())
-            each(feeds[1], lambda part: part.finish())
-        feed_weights(full)
-        each(feeds[layer], lambda part: part.start())
+            feeds[1][0].finish()
+        else:
+            feeds[1][1].hop()
+        product(r.own_gu, r.normed_two, r.grad_gu)
+        feeds[layer][0].start()
         gathers = []
         gain_sums = []
         for batch, part in enumerate(parts):
@@ -1476,19 +1487,23 @@
         for batch, gather in enumerate(gathers):
             gather.forward()
             gather.finish()
+            if batch == 1:
+                if layer == 0:
+                    mixers[1][1].finish()
+                grad_out = tn(r.combined[0], r.branch[0]) + tn(r.combined[1], r.branch[1])
+                r.grad_out[...] = grad_out.astype(BF)
+                mixers[layer][1].start()
             mixer_back(layer, batch)
             part = scatter(batch)
             part.start()
             part.forward()
             parts.append(part)
             if batch == 0:
-                each(feeds[layer], lambda part: part.hop())
+                each(feeds[layer][: 2 - layer], lambda part: part.hop())
         if layer == 0:
-            each(mixers[1], lambda part: part.finish())
+            mixers[1][0].finish()
         product(r.grad_mix, r.normed, r.grad_proj)
-        grad_out = tn(r.combined[0], r.branch[0]) + tn(r.combined[1], r.branch[1])
-        r.grad_out[...] = grad_out.astype(BF)
-        each(mixers[layer], lambda part: part.start())
+        mixers[layer][0].start()
         if layer == 1:
             each(load(0, mixer_names), lambda copy: copy.start())
         arriving = []
@@ -1687,7 +1702,7 @@
         pltpu.VMEM((2, 4, size, D), BF),
         pltpu.VMEM((2, 3, size, D), BF),
         pltpu.VMEM((2, 3, size, D), BF),
-        *pairs_of((2, 7), (2, 7)),
+        *pairs_of((2, 8), (2, 8)),
     ]
 
 
@@ -1728,7 +1743,7 @@
         pltpu.VMEM((depth, 4 * HD), BF),
         pltpu.VMEM((depth, 8 * padded), BF),
         pltpu.VMEM((padded, D), BF),
-        *pairs_of((7,), (7,), (4,), (2, 7), (6, 4), (2, 2)),
+        *pairs_of((7,), (7,), (4,), (2, 8), (6, 4), (2, 2)),
         pltpu.SemaphoreType.DMA((2, len(kept))),
     ]
     kernel = functools.partial(forward_kernel, unit)

time: 422 us -> 400 us (0.948)
  Pallas kernels: 386 us -> 364 us
    pallas_call x2, Pallas kernels: 380 us -> 359 us  [kernel_call(): pl.pallas_call(kernel, out_shape=list(outs), in_specs=[pl.BlockSpec(memor...]
  transfers between devices with their start and end apart: 1 -> 1, of which waited for: 0 -> 0; matrix products, arithmetic and copies ran while one was open for 1% -> 2% of each run, Pallas kernels for 44% -> 45%
where the time goes in v7:
time: 400 us; the launch traced here: 396 us
  Pallas kernels  364 us (91%)
  between operations  14.3 us (4%)
  other arithmetic  10.6 us (3%)
  local copies, waits for them, and re-layouts  6.18 us (2%)
    pallas_call x2, Pallas kernels, kernel_call(): pl.pallas_call(kernel, out_shape=list(outs), in_specs=[pl.BlockSpec(memor...  359 us
  transfers between devices with their start and end apart: 1, of which 0 were waited for; matrix products, arithmetic and copies ran while one was open for 2% of the time, Pallas kernels for 45%

profile of v7, /device:TPU:3, one launch (start us, length us, event | category | flops | bytes accessed | tf_op | source)
XLA Modules:
  0.0 396.2 jit_solution(12192049232783575290)
XLA Ops:
  7.2 0.7 all-gather.3.cloned.1.call-update
  7.9 0.7 reduce.1
  8.6 1.0 broadcast_in_dim_squeeze.5.refs_7_.refs_8_
  9.6 0.7 reshape.87
  10.4 0.7 broadcast_in_dim.19
  11.1 0.1 reshape.90
  11.2 0.7 reshape.78
  11.9 0.1 pad.13.clone
  12.0 0.6 pad_convert_fusion.refs_2_
  12.5 0.7 pad_maximum_fusion.refs_1_
  13.2 179.0 %shard_map.169 = (bf16[2,64,1024]{2,1,0:T(8,128)(2,1)}, f32[2,2,1024]{2,1,0:T(2,128)}, bf16[2,2,16,128]{3,2,1,0:T(8,128)(2,1)}, f32[2,8,128]{2,1,0:T(8,128)}, bf...) custom-call(bf16[2,1,128,1024]{3,2,1,0:T(8,128)(2,1)} %refs_0_.1, ...), custom_call_target="tpu_custom_call" | custom-call | tf_op jit(solution)/shard_map/pallas_call | solution.py:1682
  192.3 0.7 dynamic-slice_bitcast_fusion.refs_1_
  193.0 179.7 %shard_map.170 = (bf16[2,4,256,512]{3,2,1,0:T(8,128)(2,1)}, bf16[2,4,256,768]{3,2,1,0:T(8,128)(2,1)}, bf16[2,4,96,1024]{3,2,1,0:T(8,128)(2,1)}, bf16[2,128,1024]...) custom-call(bf16[2,512,1024]{2,1,0:T(8,128)(2,1)} %bitcast.40, ...), custom_call_target="tpu_custom_call" | custom-call | tf_op jit(solution)/shard_map/pallas_call | solution.py:1682
  372.8 2.3 bitcast_convert_fusion
  375.0 0.8 slice_reduce_fusion
  375.8 0.8 constant_dynamic-slice_fusion
  376.7 0.6 reshape.83
  377.3 1.3 fusion.1
  378.6 0.6 dynamic-slice_bitcast_fusion.2
  379.2 1.1 broadcast_select_fusion.2
  380.4 1.2 select_bitcast_fusion.1
  381.6 1.1 fusion
  382.7 0.8 maximum_bitcast_fusion
  383.5 5.6 %shard_map.171 = (f32[1,256,4096]{2,1,0:T(8,128)}, f32[1,256,5632]{2,1,0:T(8,128)}, f32[1,704,1024]{2,1,0:T(8,128)}) custom-call(bf16[2,4,256,512]{3,2,1,0:T(8,128)(2,1)S(1)} %copy-done.1, bf16[2,4,256,768]{3,2,1,0:T(8,128)(2,1)S(1)} %copy-done, bf16[2,4,96,1024]{3,2,1,0:T(8,128)(2,1)S(1)} %copy-done.2), custom_call_target="tpu_custom_call" | custom-call | tf_op jit(solution)/shard_map/pallas_call | solution.py:1835
  (18 shorter events, 0.1 us)
Async XLA Ops:
  7.2 185.8 %all-gather.3.cloned.1.call-start = ((), (), s32[]{:S(2)}) async-start(), calls=%async_computation | async-start | bytes 2621440 | tf_op jit(solution)/shard_map/all_gather | solution.py:1884
  13.2 179.0 %copy-start.3 = (bf16[2,1,128,1024]{3,2,1,0:T(8,128)(2,1)S(1)}, bf16[2,1,128,1024]{3,2,1,0:T(8,128)(2,1)}, u32[]{:S(2)}) copy-start(bf16[2,1,128,1024]{3,2,1,0:T(8,128)(2,1)} %param.12) | copy-start | bytes 1572868
  193.0 186.2 %copy-start.5 = (bf16[2,64,1024]{2,1,0:T(8,128)(2,1)S(1)}, bf16[2,64,1024]{2,1,0:T(8,128)(2,1)}, u32[]{:S(2)}) copy-start(bf16[2,64,1024]{2,1,0:T(8,128)(2,1)} %get-tuple-element.54.refs_4_) | copy-start | bytes 786436
  372.7 6.5 %copy-start.4 = (bf16[2,64,1024]{2,1,0:T(8,128)(2,1)S(1)}, bf16[2,64,1024]{2,1,0:T(8,128)(2,1)}, u32[]{:S(2)}) copy-start(bf16[2,64,1024]{2,1,0:T(8,128)(2,1)} %get-tuple-element.53.refs_3_) | copy-start | bytes 786436
  372.7 10.8 %copy-start.2 = (bf16[2,4,96,1024]{3,2,1,0:T(8,128)(2,1)S(1)}, bf16[2,4,96,1024]{3,2,1,0:T(8,128)(2,1)}, u32[]{:S(2)}) copy-start(bf16[2,4,96,1024]{3,2,1,0:T(8,128)(2,1)} %get-tuple-element.91.down_buf) | copy-start | bytes 4718596
  379.2 4.3 %copy-start.1 = (bf16[2,4,256,512]{3,2,1,0:T(8,128)(2,1)S(1)}, bf16[2,4,256,512]{3,2,1,0:T(8,128)(2,1)}, u32[]{:S(2)}) copy-start(bf16[2,4,256,512]{3,2,1,0:T(8,128)(2,1)} %get-tuple-element.89.mix_buf) | copy-start | bytes 6291460
  380.4 3.2 copy-start
Sparse Core Ops, SparseCore 0:
  9.6 32.3 all-gather.2

commit v8 on v7

--- a/solution.py
+++ b/solution.py
@@ -1254,13 +1254,13 @@
             if batch == 0:
                 each(feeds[layer], lambda part: part.finish())
             feed(layer, batch)
+            if layer == 0 and batch == 0:
+                each(mixers[1], lambda part: part.hop())
+                start_feed(1)
             part = scatter(batch)
             part.start()
             part.forward()
             parts.append(part)
-        if layer == 0:
-            each(mixers[1], lambda part: part.hop())
-            start_feed(1)
         each(save(layer, Kept._fields[3:5] + Kept._fields[9:13]), lambda copy: copy.start())
         arriving = []
         for batch, part in enumerate(parts):
@@ -1809,7 +1809,36 @@
     return named(BackwardOut._fields, found)
 
 
-def assemble_kernel(unit, mix_buf, gu_buf, down_buf, mix_ref, gu_ref, down_ref):
+def assemble_kernel(unit, *refs):
+    mix_buf, gu_buf, down_buf, out_buf, *rows, plane_buf = refs[:11]
+    mix_ref, gu_ref, down_ref, out_ref, rows_ref, grads_ref, persist_ref, rate_ref = refs[11:]
+    x, s, _ = here()
+
+    @pl.when(pl.program_id(0) == 0)
+    def _():
+        size = rows[0].shape[1]
+        own = pl.ds(pl.multiple_of(x * size, size), size)
+        got = pl.ds(pl.multiple_of((1 - x) * size, size), size)
+        for ref, (low, high, other) in ((rows_ref, rows[:3]), (grads_ref, rows[3:])):
+            for layer, part in enumerate((low, high)):
+
+                @pl.when(x == layer)
+                def _():
+                    for batch in range(2):
+                        ref[0, batch, 0, own, :] = part[batch].astype(ref.dtype)
+
+            for batch in range(2):
+                ref[0, batch, 0, got, :] = other[batch].astype(ref.dtype)
+        for head in range(2):
+            out_ref[0, head * HD : (head + 1) * HD, :] = out_buf[head].astype(F32)
+            for kind in range(2):
+                begin = pl.multiple_of(x * 32 + kind * 16, 16)
+                persist_ref[0, kind, :, head * HD : (head + 1) * HD] = plane_buf[
+                    2 * s + head, pl.ds(begin, 16), :
+                ]
+            both = jnp.sum(plane_buf[2 * s + head, 64:72, :], axis=1, keepdims=True)
+            rate_ref[0:1, head : head + 1] = jnp.where(x == 0, both[0:1], both[1:2])
+
     padded = down_buf.shape[2]
     half = gu_buf.shape[3] // 2
     for which in range(8):
@@ -1829,29 +1858,47 @@
         down_ref[0, pair * unit : (pair + 1) * unit, :] = down[:unit]
 
 
-def assemble_call(unit, mix_buf, gu_buf, down_buf):
+def assemble_call(unit, found, outputs, grads):
+    mix_buf, gu_buf, down_buf = found.mix_buf, found.gu_buf, found.down_buf
     depth, padded = mix_buf.shape[2], down_buf.shape[2]
     rows = depth // 4
+    count, size, _ = outputs[0].shape
+    shape = jax.ShapeDtypeStruct
+    outs = [
+        shape((1, depth, 4 * D), F32),
+        shape((1, depth, 2 * FF), F32),
+        shape((1, 8 * unit, D), F32),
+    ]
+    once = [
+        shape((1, 2 * HD, D), F32),
+        shape((1, count, 1, 2 * size, D), BF),
+        shape((1, count, 1, 2 * size, D), F32),
+        shape((1, 2, 16, 2 * HD), F32),
+        shape((1, 2), F32),
+    ]
+    given = (found.out_buf, *outputs, found.rows_buf, *grads, found.grads_buf, found.plane_buf)
+
+    def whole(part):
+        return pl.BlockSpec(part.shape, lambda i, zeros=(0,) * len(part.shape): zeros)
+
     return pl.pallas_call(
         functools.partial(assemble_kernel, unit),
         grid=(4,),
-        out_shape=[
-            jax.ShapeDtypeStruct((1, depth, 4 * D), F32),
-            jax.ShapeDtypeStruct((1, depth, 2 * FF), F32),
-            jax.ShapeDtypeStruct((1, 8 * unit, D), F32),
-        ],
+        out_shape=outs + once,
         in_specs=[
             pl.BlockSpec((2, 4, rows, 4 * HD), lambda i: (0, 0, i, 0)),
             pl.BlockSpec((2, 4, rows, gu_buf.shape[3]), lambda i: (0, 0, i, 0)),
             pl.BlockSpec((1, 2, padded, D), lambda i: (i // 2, i % 2, 0, 0)),
+            *(whole(part) for part in given),
         ],
         out_specs=[
             pl.BlockSpec((1, rows, 4 * D), lambda i: (0, i, 0)),
             pl.BlockSpec((1, rows, 2 * FF), lambda i: (0, i, 0)),
             pl.BlockSpec((1, 2 * unit, D), lambda i: (0, i, 0)),
+            *(whole(part) for part in once),
         ],
-        compiler_params=pltpu.CompilerParams(vmem_limit_bytes=40 * 2**20),
-    )(mix_buf, gu_buf, down_buf)
+        compiler_params=pltpu.CompilerParams(vmem_limit_bytes=60 * 2**20),
+    )(mix_buf, gu_buf, down_buf, *given)
 
 
 def tensor_parallel(
@@ -1860,17 +1907,11 @@
     x, s, z = here()
     nx, ns, nz = (lax.axis_size(a) for a in ("section", "seq", "shard"))
     width = nx * ns
-    mine = x * ns + s
-    other = (1 - x) * ns + s
-    first = x == 0
     count, _, tokens, _ = inputs.shape
     length = tokens * ns
     size = length // width
     depth = w_mix.shape[1]
     unit = w_down.shape[1] // (nx * ns)
-
-    def layers(own, got):
-        return (jnp.where(first, own, got), jnp.where(first, got, own))
 
     small = persist_kv[0].reshape(-1, 2, HD).transpose(1, 0, 2).reshape(-1, HD).astype(F32)
     rates = jnp.broadcast_to(memory_decay[0][:, None, None], (2, 8, HD)).reshape(-1, HD)
@@ -1898,24 +1939,10 @@
     outputs = (below.out_rows, above.out_rows)
     grads = (found.grad_low, found.grad_high)
 
-    def whole_rows(of_layer, got):
-        both = layers(jnp.where(first, of_layer[0], of_layer[1]), got)
-        return jnp.concatenate(both, 1)[None, :, None]
-
-    section_out = whole_rows(outputs, found.rows_buf)
-    section_grad = whole_rows(grads, found.grads_buf).astype(F32)
-    grad_mix, grad_gu, grad_down = assemble_call(unit, found.mix_buf, found.gu_buf, found.down_buf)
-    grad_out = found.out_buf.astype(F32).reshape(1, 2 * HD, D)
-
-    plane_all = found.plane_buf
-    heads_of = lax.dynamic_slice_in_dim(plane_all, 2 * s, 2, 0)
-    of_section = lax.dynamic_index_in_dim(
-        heads_of[:, :64].reshape(2, 2, 2, -1, HD), x, 1, keepdims=False
-    )
-    grad_persist = of_section.transpose(1, 2, 0, 3).reshape(1, 2, -1, 2 * HD)
-    of_section = lax.dynamic_index_in_dim(heads_of[:, 64:66], x, 1, keepdims=False)
-    grad_rate = jnp.sum(of_section, 1)[None]
-    gain_all = jnp.sum(plane_all[:, 72:], 0).reshape(2, 2, depth)
+    grad_mix, grad_gu, grad_down, grad_out, section_out, section_grad, grad_persist, grad_rate = (
+        assemble_call(unit, found, outputs, grads)
+    )
+    gain_all = jnp.sum(found.plane_buf[:, 72:], 0).reshape(2, 2, depth)
     grad_gain = lax.dynamic_index_in_dim(gain_all, x, 0).transpose(0, 2, 1)
     return (
         section_out,

time: 400 us -> 392 us (0.980)
  other arithmetic: 10.6 us -> 2.76 us
    pallas_call x1, Pallas kernels: 5.61 us -> 9.98 us  [assemble_call(): pl.pallas_call(functools.partial(assemble_kernel, unit), grid=(4,), out_s...]
where the time goes in v8:
time: 392 us; the launch traced here: 388 us
  Pallas kernels  366 us (93%)
  between operations  14.3 us (4%)
  local copies, waits for them, and re-layouts  4.64 us (1%)
    pallas_call x2, Pallas kernels, kernel_call(): pl.pallas_call(kernel, out_shape=list(outs), in_specs=[pl.BlockSpec(memor...  356 us
    pallas_call x1, Pallas kernels, assemble_call(): pl.pallas_call(functools.partial(assemble_kernel, unit), grid=(4,), out_s...  9.98 us
  transfers between devices with their start and end apart: 1, of which 0 were waited for; matrix products, arithmetic and copies ran while one was open for 2% of the time, Pallas kernels for 45%

profile of v8, /device:TPU:3, one launch (start us, length us, event | category | flops | bytes accessed | tf_op | source)
XLA Modules:
  0.0 388.3 jit_solution(3431566032953060440)
XLA Ops:
  7.2 0.0 all-gather.3.cloned.1.call-start
  7.2 0.7 all-gather.3.cloned.1.call-update
  7.9 0.7 reshape.36
  8.6 0.7 broadcast_in_dim.12
  9.3 0.1 reshape.42
  9.4 0.7 reduce
  10.1 0.7 reshape.39
  10.9 1.0 broadcast_in_dim_squeeze.5.refs_7_.refs_8_
  11.9 0.1 pad.9.clone
  11.9 0.6 pad_convert_fusion.refs_2_
  12.5 0.7 pad_maximum_fusion.refs_1_
  13.2 0.0 copy-start
  13.2 176.6 %shard_map.169 = (bf16[2,64,1024]{2,1,0:T(8,128)(2,1)}, f32[2,2,1024]{2,1,0:T(2,128)}, bf16[2,2,16,128]{3,2,1,0:T(8,128)(2,1)}, f32[2,8,128]{2,1,0:T(8,128)}, bf...) custom-call(bf16[2,1,128,1024]{3,2,1,0:T(8,128)(2,1)} %refs_0_.1, ...), custom_call_target="tpu_custom_call" | custom-call | tf_op jit(solution)/shard_map/pallas_call | solution.py:1682
  189.8 0.0 copy-done
  189.8 0.7 dynamic-slice_bitcast_fusion.refs_1_
  190.5 0.0 all-gather.3.cloned.1.call-done
  190.5 179.4 %shard_map.170 = (bf16[2,4,256,512]{3,2,1,0:T(8,128)(2,1)}, bf16[2,4,256,768]{3,2,1,0:T(8,128)(2,1)}, bf16[2,4,96,1024]{3,2,1,0:T(8,128)(2,1)}, bf16[2,128,1024]...) custom-call(bf16[2,512,1024]{2,1,0:T(8,128)(2,1)} %bitcast.15, ...), custom_call_target="tpu_custom_call" | custom-call | tf_op jit(solution)/shard_map/pallas_call | solution.py:1682
  370.0 0.8 slice_reduce_fusion
  370.7 0.6 dynamic-slice_bitcast_fusion.1
  371.3 10.0 %shard_map.171 = (f32[1,256,4096]{2,1,0:T(8,128)}, f32[1,256,5632]{2,1,0:T(8,128)}, f32[1,704,1024]{2,1,0:T(8,128)}, f32[1,256,1024]{2,1,0:T(8,128)}, bf16[1,2,1...) custom-call(bf16[2,4,256,512]{3,2,1,0:T(8,128)(2,1)} %get-tuple-eleme, ...), custom_call_target="tpu_custom_call" | custom-call | tf_op jit(solution)/shard_map/pallas_call | solution.py:1884
  (2 shorter events, 0.0 us)
Async XLA Ops:
  7.2 183.4 %all-gather.3.cloned.1.call-start = ((), (), s32[]{:S(2)}) async-start(), calls=%async_computation | async-start | bytes 2621440 | tf_op jit(solution)/shard_map/all_gather | solution.py:1925
  13.2 176.6 %copy-start = (bf16[2,1,128,1024]{3,2,1,0:T(8,128)(2,1)S(1)}, bf16[2,1,128,1024]{3,2,1,0:T(8,128)(2,1)}, u32[]{:S(2)}) copy-start(bf16[2,1,128,1024]{3,2,1,0:T(8,128)(2,1)} %param.12) | copy-start | bytes 1572868
Sparse Core Ops, SparseCore 0:
  9.6 32.3 all-gather.2

commit v9 on v8

--- a/solution.py
+++ b/solution.py
@@ -556,7 +556,8 @@
 
 class ColumnSum(Column):
     RELAYED = ((3, 1), None, None, (0, 2))
-    DIRECT = ((2, 1), (2, 0), (1, 3), (1, 2))
+    DIRECT = ((2,), (2, 0), (1, 3), (1,))
+    LATE = ((1,), (), (), (2,))
     SOURCES = ((1, 2), (0, 2, 3), (0, 1, 3), (1, 2))
 
     def __init__(self, own, slots, out, send, recv):
@@ -593,6 +594,13 @@
                     self.slots[at].astype(F32) + self.own[block].astype(F32)
                 ).astype(BF)
                 self.relayed(at).start()
+
+        for at in (0, 3):
+
+            @pl.when(self.place[2] == at)
+            def _():
+                for plane in self.LATE[at]:
+                    self.direct(at, plane).start()
 
     def finish(self):
         def body(at):
@@ -605,7 +613,7 @@
                 self.first(at).wait_send()
             else:
                 self.relayed(at).wait_send()
-            for plane in self.DIRECT[at]:
+            for plane in self.DIRECT[at] + self.LATE[at]:
                 self.direct(at, plane).wait_send()
 
         self.at_each(body)
@@ -1237,6 +1245,8 @@
             part = scatter(batch)
             part.start()
             part.forward()
+            if layer == 1 and batch == 0:
+                each(feeds[1], lambda part: part.hop())
             parts.append(part)
         each(save(layer, mixer_names), lambda copy: copy.start())
         if layer == 0:
@@ -1246,7 +1256,8 @@
             mid = v.rows[batch].astype(F32) + part.finish()
             v.mid[batch] = mid
             gathers.append(send_normed(batch, mid, r.gains[layer, 1:2, :], v.normed_two))
-        each(feeds[layer], lambda part: part.hop())
+        if layer == 0:
+            each(feeds[0], lambda part: part.hop())
         parts = []
         for batch, gather in enumerate(gathers):
             gather.forward()

time: 392 us -> 387 us (0.987)
  Pallas kernels: 366 us -> 360 us
    pallas_call x2, Pallas kernels: 356 us -> 350 us  [kernel_call(): pl.pallas_call(kernel, out_shape=list(outs), in_specs=[pl.BlockSpec(memor...]
where the time goes in v9:
time: 387 us; the launch traced here: 383 us
  Pallas kernels  360 us (93%)
  between operations  14.3 us (4%)
  local copies, waits for them, and re-layouts  4.64 us (1%)
    pallas_call x2, Pallas kernels, kernel_call(): pl.pallas_call(kernel, out_shape=list(outs), in_specs=[pl.BlockSpec(memor...  350 us
    pallas_call x1, Pallas kernels, assemble_call(): pl.pallas_call(functools.partial(assemble_kernel, unit), grid=(4,), out_s...  9.98 us
  transfers between devices with their start and end apart: 1, of which 0 were waited for; matrix products, arithmetic and copies ran while one was open for 2% of the time, Pallas kernels for 45%

profile of v9, /device:TPU:3, one launch (start us, length us, event | category | flops | bytes accessed | tf_op | source)
XLA Modules:
  0.0 382.8 jit_solution(12122564948822680308)
XLA Ops:
  7.2 0.0 all-gather.3.cloned.1.call-start
  7.2 0.7 all-gather.3.cloned.1.call-update
  7.9 0.7 reshape.36
  8.6 0.7 broadcast_in_dim.12
  9.3 0.1 reshape.42
  9.4 0.7 reduce
  10.1 0.7 reshape.39
  10.9 1.0 broadcast_in_dim_squeeze.5.refs_7_.refs_8_
  11.9 0.1 pad.9.clone
  11.9 0.6 pad_convert_fusion.refs_2_
  12.5 0.7 pad_maximum_fusion.refs_1_
  13.2 0.0 copy-start
  13.2 173.0 %shard_map.169 = (bf16[2,64,1024]{2,1,0:T(8,128)(2,1)}, f32[2,2,1024]{2,1,0:T(2,128)}, bf16[2,2,16,128]{3,2,1,0:T(8,128)(2,1)}, f32[2,8,128]{2,1,0:T(8,128)}, bf...) custom-call(bf16[2,1,128,1024]{3,2,1,0:T(8,128)(2,1)} %refs_0_.1, ...), custom_call_target="tpu_custom_call" | custom-call | tf_op jit(solution)/shard_map/pallas_call | solution.py:1693
  186.3 0.0 copy-done
  186.3 0.7 dynamic-slice_bitcast_fusion.refs_1_
  187.0 0.0 all-gather.3.cloned.1.call-done
  187.0 177.4 %shard_map.170 = (bf16[2,4,256,512]{3,2,1,0:T(8,128)(2,1)}, bf16[2,4,256,768]{3,2,1,0:T(8,128)(2,1)}, bf16[2,4,96,1024]{3,2,1,0:T(8,128)(2,1)}, bf16[2,128,1024]...) custom-call(bf16[2,512,1024]{2,1,0:T(8,128)(2,1)} %bitcast.15, ...), custom_call_target="tpu_custom_call" | custom-call | tf_op jit(solution)/shard_map/pallas_call | solution.py:1693
  364.4 0.8 slice_reduce_fusion
  365.2 0.6 dynamic-slice_bitcast_fusion.1
  365.8 10.0 %shard_map.171 = (f32[1,256,4096]{2,1,0:T(8,128)}, f32[1,256,5632]{2,1,0:T(8,128)}, f32[1,704,1024]{2,1,0:T(8,128)}, f32[1,256,1024]{2,1,0:T(8,128)}, bf16[1,2,1...) custom-call(bf16[2,4,256,512]{3,2,1,0:T(8,128)(2,1)} %get-tuple-eleme, ...), custom_call_target="tpu_custom_call" | custom-call | tf_op jit(solution)/shard_map/pallas_call | solution.py:1895
  (2 shorter events, 0.0 us)
Async XLA Ops:
  7.2 179.8 %all-gather.3.cloned.1.call-start = ((), (), s32[]{:S(2)}) async-start(), calls=%async_computation | async-start | bytes 2621440 | tf_op jit(solution)/shard_map/all_gather | solution.py:1936
  13.2 173.0 %copy-start = (bf16[2,1,128,1024]{3,2,1,0:T(8,128)(2,1)S(1)}, bf16[2,1,128,1024]{3,2,1,0:T(8,128)(2,1)}, u32[]{:S(2)}) copy-start(bf16[2,1,128,1024]{3,2,1,0:T(8,128)(2,1)} %param.12) | copy-start | bytes 1572868
Sparse Core Ops, SparseCore 0:
  9.6 32.3 all-gather.2
